TPU v7x, 32 devices: a whole 2x2x4 slice. The times are simulated.
32 devices in a mesh: tm: 4 (over y, core), gx: 8 (over z, x).
Axes of the slice: x: 2, y: 2, z: 4, core: 2. Of those that a mesh axis runs over, the one named last changes fastest.
Arguments:
- end_modes: float32 [4, 256, 256, 256], P('tm', None, 'gx'), may hold values from -1 to 1
- initial_modes: float32 [256, 256, 256], P(None, 'gx'), may hold values from -1 to 1
Outputs:
- new_end_modes: float32 [4, 256, 256, 256], P('tm', None, 'gx')
- coarse_ends: float32 [4, 128, 128, 128], P('tm', None, 'gx')
All inputs are finite; a program needn't handle non-finite values.
Results may differ from a plain program's by a relative error of at most 0.00014.
Values sent between devices are 32-bit elements; how exact they have to be, the bound alone decides.
No kernel may reach another device: no remote copies, remote signals or barrier semaphores. Data moves between devices by JAX's collectives and lax.ppermute only.
A program may use at most 192 MiB of HBM per device.

v0:
```python
import math

import jax
import jax.numpy as jnp
from jax import lax
from jax.sharding import PartitionSpec as P

DIFFUSION = 0.25
HIGHEST = lax.Precision.HIGHEST


def shifted(value, axis, by):
    length = lax.axis_size(axis)
    pairs = [(i, i + by) for i in range(length) if 0 <= i + by < length]
    return lax.ppermute(value, axis, pairs)


def sine_table(length, rows, modes):
    phase = (rows[:, None] + 1) * (modes[None, :] + 1) % (2 * (length + 1))
    angle = phase.astype(jnp.float32) * (math.pi / (length + 1))
    return jnp.sin(angle) * math.sqrt(2.0 / (length + 1))


def fine_order(positions, block, coarse):
    within = positions % block
    group = positions // block
    half = block // 2
    return jnp.where(within < half, group * half + within, coarse + group * half + within - half)


def omega(modes, length):
    return 2.0 - 2.0 * jnp.cos((modes.astype(jnp.float32) + 1.0) * (math.pi / (length + 1)))


def reaction(field):
    return field - field * field * field


def per_device(end_modes, initial_modes):
    grid = initial_modes.shape[0]
    coarse = grid // 2
    groups = lax.axis_size("gx")
    block = grid // groups
    half = block // 2
    slice_index = lax.axis_index("tm")
    group_index = lax.axis_index("gx")
    every = jnp.arange(grid, dtype=jnp.int32)
    table = sine_table(grid, every, every)
    permuted = sine_table(grid, every, fine_order(every, block, coarse))
    low_table = table[:, :coarse]
    local_rows = group_index * block + jnp.arange(block, dtype=jnp.int32)
    fine_z = omega(every, grid)
    fine_y = omega(fine_order(local_rows, block, coarse), grid)
    fine_eigen = DIFFUSION * (fine_z[:, None, None] + fine_y[None, :, None] + fine_z[None, None, :])
    coarse_every = jnp.arange(coarse, dtype=jnp.int32)
    coarse_rows = group_index * half + jnp.arange(half, dtype=jnp.int32)
    coarse_z = omega(coarse_every, coarse)
    coarse_y = omega(coarse_rows, coarse)
    coarse_eigen = (
        0.25
        * DIFFUSION
        * (coarse_z[:, None, None] + coarse_y[None, :, None] + coarse_z[None, None, :])
    )
    factor = ((coarse + 1) / (grid + 1)) ** 1.5

    def depth(stack):
        return jnp.einsum("fzpk,zq->fqpk", stack, table, precision=HIGHEST)

    def planes_back(stack):
        along_y = jnp.einsum("fzpk,yp->fzyk", stack, permuted, precision=HIGHEST)
        return jnp.einsum("fzyk,xk->fzyx", along_y, table, precision=HIGHEST)

    def restrict(modes):
        return factor * modes[..., :coarse, :half, :coarse]

    previous = shifted(end_modes[0], "tm", 1)
    start_modes = jnp.where(slice_index == 0, initial_modes, previous)
    start_field = planes_back(
        lax.all_to_all(depth(start_modes[None]), "gx", split_axis=1, concat_axis=2, tiled=True)
    )
    along_x = jnp.einsum("fzyx,xk->fzyk", reaction(start_field), table, precision=HIGHEST)
    start_reaction = depth(
        lax.all_to_all(
            jnp.einsum("fzyk,yp->fzpk", along_x, permuted, precision=HIGHEST),
            "gx",
            split_axis=2,
            concat_axis=1,
            tiled=True,
        )
    )[0]
    node_mid = (start_modes + 0.5 * start_reaction) / (1.0 + 0.5 * fine_eigen)
    node_end = (start_modes + start_reaction) / (1.0 + fine_eigen)
    node_stack = jnp.stack([node_mid, node_end])
    node_fields = planes_back(
        lax.all_to_all(depth(node_stack), "gx", split_axis=1, concat_axis=2, tiled=True)
    )
    node_terms = reaction(node_fields)
    along_x = jnp.einsum("fzyx,xk->fzyk", node_terms, low_table, precision=HIGHEST)
    node_low = factor * jnp.einsum(
        "fzpk,zq->fqpk",
        lax.all_to_all(
            jnp.einsum("fzyk,yp->fzpk", along_x, low_table, precision=HIGHEST),
            "gx",
            split_axis=2,
            concat_axis=1,
            tiled=True,
        ),
        low_table,
        precision=HIGHEST,
    )
    low_eigen = fine_eigen[:coarse, :half, :coarse]
    first_term = restrict(start_reaction) - low_eigen * restrict(start_modes)
    mid_term = node_low[0] - low_eigen * restrict(node_mid)
    end_term = node_low[1] - low_eigen * restrict(node_end)
    integral = (first_term + 4.0 * mid_term + end_term) / 6.0
    decay = 1.0 / (1.0 + coarse_eigen)
    offset_part = (integral + coarse_eigen * restrict(node_end)) / (1.0 + coarse_eigen)
    is_first = slice_index == 0
    offset = jnp.where(is_first, decay * restrict(start_modes) + offset_part, offset_part)

    def relay_turn(step, current):
        incoming = shifted(current, "tm", 1)
        return jnp.where(is_first, offset, decay * incoming + offset)

    coarse_end = lax.fori_loop(0, lax.axis_size("tm") - 1, relay_turn, offset)
    corrected = node_end.at[:coarse, :half, :coarse].set(coarse_end / factor)
    return (corrected[None], coarse_end[None])


def solution(mesh):
    return jax.shard_map(
        per_device,
        mesh=mesh,
        in_specs=(P("tm", None, "gx", None), P(None, "gx", None)),
        out_specs=(P("tm", None, "gx", None), P("tm", None, "gx", None)),
        check_vma=False,
    )
```

profile of v0, /device:TPU:1, one launch (start us, length us, event | category | flops | bytes accessed | tf_op | source)
XLA Modules:
  0.0 1124.7 jit_solution(18350096714170236506)
XLA Ops:
  0.6 11.6 %copy.94 = f32[1,256,32,256]{3,1,2,0:T(8,128)} copy(f32[1,256,32,256]{3,2,1,0:T(8,128)} %param.6) | data formatting | bytes 16777216 | tf_op args[0]
  16.8 90.7 %collective-permute-done.1 = f32[256,32,256]{2,0,1:T(8,128)} collective-permute-done((f32[256,32,256]{2,0,1:T(8,128)}, f32[256,32,256]{2,0,1:T(8,128)}, u32[]{:S(2)}, u32[]{:S(2)}) %collective-permute-start.1) | collective-permute-done | bytes 8388640 | tf_op jit(solution)/shard_map/ppermute | solution.py:15
  107.5 14.2 %copy_select_fusion = f32[256,32,256]{2,0,1:T(8,128)} fusion(f32[256,32,256]{2,0,1:T(8,128)} %collective-permute-done.1, f32[256,32,256]{2,1,0:T(8,128)} %param.7, pred[]{:T(512)} %eq.11), kind=kLoop, calls=%fused_computation.19 | loop fusion | flops 2097152 | bytes 25165824 | tf_op jit(solution)/shard_map/jit(_where)/select_n | solution.py:77
  121.7 12.7 %convolution_bitcast_fusion.1 = f32[1,256,32,256]{3,1,2,0:T(8,128)S(1)} fusion(f32[256,32,256]{2,0,1:T(8,128)} %copy_select_fusion, s32[256]{0:T(256)S(1)} %iota_add_fusion), kind=kOutput, calls=%fused_computation.24 | convolution fusion | flops 6443106304 | bytes 16778240 | tf_op jit(solution)/shard_map/fzpk,zq->fqpk/dot_general | solution.py:67
  134.4 8.1 copy.54
  142.5 5.9 all-to-all-start
  148.4 103.1 %all-to-all-done = f32[1,256,32,256]{3,2,0,1:T(8,128)} async-done(((f32[1,256,32,256]{3,2,0,1:T(8,128)}), f32[1,256,32,256]{3,2,0,1:T(8,128)}, u32[]{:S(2)}, u32[]{:S(2)}) %all-to-all-start) | async-done | bytes 8388640 | tf_op jit(solution)/shard_map/all_to_all | solution.py:79
  255.7 9.7 fusion.39
  265.5 8.1 fusion.12
  273.5 8.9 fusion.11
  282.5 9.8 convolution_bitcast_fusion
  292.2 8.2 copy.57
  300.5 5.0 all-to-all-start.1
  305.7 136.2 %all-to-all-done.1 = f32[1,32,256,256]{3,1,0,2:T(8,128)} async-done(((f32[1,32,256,256]{3,1,0,2:T(8,128)}), f32[1,32,256,256]{3,1,0,2:T(8,128)}, u32[]{:S(2)}, u32[]{:S(2)}) %all-to-all-start.1) | async-done | bytes 8388640 | tf_op jit(solution)/shard_map/all_to_all | solution.py:83
  441.9 8.3 copy.58
  450.2 24.7 %fusion.10 = (f32[256,32,256]{2,0,1:T(8,128)}, f32[256,32,256]{2,0,1:T(8,128)}, f32[256,32,256]{2,0,1:T(8,128)}, f32[256,32,256]{2,0,1:T(8,128)}) fusion(f32[256,32,256]{2,0,1:T(8,128)} %copy_select_fusion, f32[256]{0:T(256)S(1)} %multiply_subtract_fusion.4, f32[256,32]{0,1:T(8,128)S(1)} %broadcast_add_fusion.1, f32[256,32,256]{2,0,1:T(8,128)} %bitcast.118, ...), kind=kOutput, calls=%fused_computation.15 | convolution fusion | flops 6464077824 | bytes 50366464 | tf_op jit(solution)/shard_map/fzpk,zq->fqpk/dot_general | solution.py:67
  474.9 24.6 %fusion.14 = f32[2,256,32,256]{3,1,2,0:T(8,128)} fusion(f32[1,256,32,256]{3,1,2,0:T(8,128)} %bitcast.113, f32[1,256,32,256]{3,1,2,0:T(8,128)} %bitcast.117, s32[256]{0:T(256)S(1)} %iota_add_fusion), kind=kOutput, calls=%fused_computation.22 | convolution fusion | flops 12889751552 | bytes 33555456 | tf_op jit(solution)/shard_map/fzpk,zq->fqpk/dot_general | solution.py:67
  499.6 17.7 %copy.62 = f32[2,256,32,256]{3,2,0,1:T(8,128)} copy(f32[2,256,32,256]{3,1,2,0:T(8,128)} %fusion.14) | data formatting | bytes 33554432 | tf_op jit(solution)/shard_map/fzpk,zq->fqpk/transpose | solution.py:67
  517.2 6.1 all-to-all-start.2
  524.5 347.4 %all-to-all-done.2 = f32[2,256,32,256]{3,2,0,1:T(8,128)} async-done(((f32[2,256,32,256]{3,2,0,1:T(8,128)}), f32[2,256,32,256]{3,2,0,1:T(8,128)}, u32[]{:S(2)}, u32[]{:S(2)}) %all-to-all-start.2) | async-done | bytes 16777248 | tf_op jit(solution)/shard_map/all_to_all | solution.py:95
  871.8 11.9 %copy.64 = f32[2,32,8,32,256]{4,3,2,1,0:T(8,128)} copy(f32[2,32,8,32,256]{4,3,0,1,2:T(8,128)} %bitcast.28) | data formatting | bytes 33554432 | tf_op jit(solution)/shard_map/all_to_all | solution.py:95
  883.7 24.1 %fusion.35 = f32[256,2,32,256]{3,0,2,1:T(8,128)} fusion(f32[2,32,256,256]{3,2,1,0:T(8,128)} %bitcast.112, s32[256]{0:T(256)S(1)} %fusion.64, s32[256]{0:T(256)S(1)} %iota_add_fusion), kind=kOutput, calls=%fused_computation.56 | convolution fusion | flops 12885557248 | bytes 33556480 | tf_op jit(solution)/shard_map/fzpk,yp->fzyk/dot_general | solution.py:70
  907.8 22.4 %fusion.7 = f32[2,32,256,256]{3,2,1,0:T(8,128)} fusion(f32[256,2,32,256]{3,0,2,1:T(8,128)} %fusion.35, s32[256]{0:T(256)S(1)} %iota_add_fusion), kind=kOutput, calls=%fused_computation.9 | convolution fusion | flops 12885557248 | bytes 33555456 | tf_op jit(solution)/shard_map/fzyk,xk->fzyx/dot_general | solution.py:71
  930.2 16.7 %fusion.2 = f32[2,32,256,128]{3,2,1,0:T(8,128)S(1)} fusion(f32[2,32,256,256]{3,2,1,0:T(8,128)} %fusion.7, f32[256,256]{1,0:T(8,128)S(1)} %fusion.30), kind=kOutput, calls=%fused_computation.4 | convolution fusion | flops 6455033856 | bytes 25296896 | tf_op jit(solution)/shard_map/fzyx,xk->fzyk/dot_general | solution.py:98
  946.8 5.3 convolution_bitcast_fusion.2
  956.6 4.8 all-to-all-start.3
  961.6 93.5 %all-to-all-done.3 = f32[2,32,128,128]{3,1,0,2:T(8,128)} async-done(((f32[2,32,128,128]{3,1,0,2:T(8,128)}), f32[2,32,128,128]{3,1,0,2:T(8,128)}, u32[]{:S(2)}, u32[]{:S(2)}) %all-to-all-start.3) | async-done | bytes 4194336 | tf_op jit(solution)/shard_map/all_to_all | solution.py:101
  1064.2 47.0 %while.12 = (s32[]{:T(128)}, f32[128,16,128]{2,1,0:T(8,128)S(1)}, pred[]{:T(512)}, f32[128,16,128]{2,1,0:T(8,128)S(1)}, f32[128]{0:T(128)S(1)}, /*index=5*/f32[128,16]{1,0:T(8,128)S(1)}, s32[]{:T(128)}) while((s32[]{:T(128)}, f32[128,16,128]{2,1,0:T(8,128)S(1)}, pred[]{:T(512)}, f32[128,16,128]{2,1,0:T(8,128)S(1)}, ...), condition=%wide.region_1.2_spmd.clone, body=%wide.region_0.1_spmd.clone.sunk | while | flops 1835010 | bytes 7348854 | solution.py:125
  1066.1 11.7 %collective-permute-done = f32[128,16,128]{2,1,0:T(8,128)S(1)} collective-permute-done((f32[128,16,128]{2,1,0:T(8,128)S(1)}, f32[128,16,128]{2,1,0:T(8,128)S(1)}, u32[]{:S(2)}, u32[]{:S(2)}) %collective-permute-start) | collective-permute-done | bytes 1048608 | tf_op jit(solution)/shard_map/while/body/eval_jaxpr/ppermute | solution.py:15
  1082.6 11.7 %collective-permute-done = f32[128,16,128]{2,1,0:T(8,128)S(1)} collective-permute-done((f32[128,16,128]{2,1,0:T(8,128)S(1)}, f32[128,16,128]{2,1,0:T(8,128)S(1)}, u32[]{:S(2)}, u32[]{:S(2)}) %collective-permute-start) | collective-permute-done | bytes 1048608 | tf_op jit(solution)/shard_map/while/body/eval_jaxpr/ppermute | solution.py:15
  1099.1 11.7 %collective-permute-done = f32[128,16,128]{2,1,0:T(8,128)S(1)} collective-permute-done((f32[128,16,128]{2,1,0:T(8,128)S(1)}, f32[128,16,128]{2,1,0:T(8,128)S(1)}, u32[]{:S(2)}, u32[]{:S(2)}) %collective-permute-start) | collective-permute-done | bytes 1048608 | tf_op jit(solution)/shard_map/while/body/eval_jaxpr/ppermute | solution.py:15
  1112.6 11.6 %copy.72 = f32[1,256,32,256]{3,2,1,0:T(8,128)} copy(f32[1,256,32,256]{3,1,2,0:T(8,128)} %bitcast_dynamic-update-slice_fusion) | data formatting | bytes 16777216
  (27 shorter events, 36.8 us)
Async XLA Ops:
  12.3 95.2 %collective-permute-start.1 = (f32[256,32,256]{2,0,1:T(8,128)}, f32[256,32,256]{2,0,1:T(8,128)}, u32[]{:S(2)}, u32[]{:S(2)}) collective-permute-start(f32[256,32,256]{2,0,1:T(8,128)} %bitcast.111), channel_id=1, source_target_pairs={{0,8},{8,16},{16,24},{1,9},{9,17},{17,25},{2,10},{10,18},{18,26},{... | collective-permute-start | bytes 25165832 | tf_op jit(solution)/shard_map/ppermute | solution.py:15
  142.5 109.0 %all-to-all-start = ((f32[1,256,32,256]{3,2,0,1:T(8,128)}), f32[1,256,32,256]{3,2,0,1:T(8,128)}, u32[]{:S(2)}, u32[]{:S(2)}) async-start(f32[1,256,32,256]{3,2,0,1:T(8,128)} %copy.54), calls=%async_computation | async-start | bytes 16777216 | tf_op jit(solution)/shard_map/all_to_all | solution.py:79
  300.5 141.4 %all-to-all-start.1 = ((f32[1,32,256,256]{3,1,0,2:T(8,128)}), f32[1,32,256,256]{3,1,0,2:T(8,128)}, u32[]{:S(2)}, u32[]{:S(2)}) async-start(f32[1,32,256,256]{3,1,0,2:T(8,128)} %copy.57), calls=%async_computation.1 | async-start | bytes 16777216 | tf_op jit(solution)/shard_map/all_to_all | solution.py:83
  517.2 354.6 %all-to-all-start.2 = ((f32[2,256,32,256]{3,2,0,1:T(8,128)}), f32[2,256,32,256]{3,2,0,1:T(8,128)}, u32[]{:S(2)}, u32[]{:S(2)}) async-start(f32[2,256,32,256]{3,2,0,1:T(8,128)} %copy.62), calls=%async_computation.2 | async-start | bytes 33554432 | tf_op jit(solution)/shard_map/all_to_all | solution.py:95
  956.6 98.6 %all-to-all-start.3 = ((f32[2,32,128,128]{3,1,0,2:T(8,128)}), f32[2,32,128,128]{3,1,0,2:T(8,128)}, u32[]{:S(2)}, u32[]{:S(2)}) async-start(f32[2,32,128,128]{3,1,0,2:T(8,128)} %copy.66), calls=%async_computation.3 | async-start | bytes 8388608 | tf_op jit(solution)/shard_map/all_to_all | solution.py:101
  1064.2 13.7 %collective-permute-start = (f32[128,16,128]{2,1,0:T(8,128)S(1)}, f32[128,16,128]{2,1,0:T(8,128)S(1)}, u32[]{:S(2)}, u32[]{:S(2)}) collective-permute-start(f32[128,16,128]{2,1,0:T(8,128)S(1)} %get-tuple-element.151), channel_id=1, source_target_pairs={{0,8},{8,16},{16,24},{1,9},{9,17},{17,25},{2,10},{10,18},{18,26},{... | collective-permute-start | bytes 3145736 | tf_op jit(solution)/shard_map/while/body/eval_jaxpr/ppermute | solution.py:15
  1078.2 16.1 %collective-permute-start = (f32[128,16,128]{2,1,0:T(8,128)S(1)}, f32[128,16,128]{2,1,0:T(8,128)S(1)}, u32[]{:S(2)}, u32[]{:S(2)}) collective-permute-start(f32[128,16,128]{2,1,0:T(8,128)S(1)} %get-tuple-element.151), channel_id=1, source_target_pairs={{0,8},{8,16},{16,24},{1,9},{9,17},{17,25},{2,10},{10,18},{18,26},{... | collective-permute-start | bytes 3145736 | tf_op jit(solution)/shard_map/while/body/eval_jaxpr/ppermute | solution.py:15
  1094.7 16.1 %collective-permute-start = (f32[128,16,128]{2,1,0:T(8,128)S(1)}, f32[128,16,128]{2,1,0:T(8,128)S(1)}, u32[]{:S(2)}, u32[]{:S(2)}) collective-permute-start(f32[128,16,128]{2,1,0:T(8,128)S(1)} %get-tuple-element.151), channel_id=1, source_target_pairs={{0,8},{8,16},{16,24},{1,9},{9,17},{17,25},{2,10},{10,18},{18,26},{... | collective-permute-start | bytes 3145736 | tf_op jit(solution)/shard_map/while/body/eval_jaxpr/ppermute | solution.py:15
  1111.2 13.0 %copy-start = (f32[128,16,128]{2,1,0:T(8,128)}, f32[128,16,128]{2,1,0:T(8,128)S(1)}, u32[]{:S(2)}) copy-start(f32[128,16,128]{2,1,0:T(8,128)S(1)} %get-tuple-element.41) | copy-start | bytes 3145732
where the time goes:
time: 1130 us; the launch traced here: 1120 us
  waiting for transfers between devices  806 us (71%)
  matrix products  169 us (15%)
  local copies, waits for them, and re-layouts  89.6 us (8%)
  starting transfers between devices  37.1 us (3%)
  other arithmetic  21.1 us (2%)
    all_to_all x1, waiting for transfers between devices, per_device(): lax.all_to_all(depth(node_stack), 'gx', split_axis=1, concat_axis=2, tile...  347 us
    all_to_all x1, waiting for transfers between devices, per_device(): lax.all_to_all(jnp.einsum('fzyk,yp->fzpk', along_x, permuted, precision=H...  136 us
    ppermute x4, waiting for transfers between devices, shifted(): return lax.ppermute(value, axis, pairs)  126 us
    all_to_all x1, waiting for transfers between devices, per_device(): lax.all_to_all(depth(start_modes[None]), 'gx', split_axis=1, concat_axis=...  103 us
    all_to_all x1, waiting for transfers between devices, per_device(): lax.all_to_all(jnp.einsum('fzyk,yp->fzpk', along_x, low_table, precision=...  93.5 us
    dot_general x3, matrix products, depth(): return jnp.einsum('fzpk,zq->fqpk', stack, table, precision=HIGHEST)  62.1 us
    dot_general x2, matrix products, planes_back(): along_y = jnp.einsum('fzpk,yp->fzyk', stack, permuted, precision=HIGHEST)  33.8 us
    dot_general x2, matrix products, planes_back(): return jnp.einsum('fzyk,xk->fzyx', along_y, table, precision=HIGHEST)  30.4 us
  transfers between devices with their start and end apart: 8, of which 8 were waited for; matrix products, arithmetic and copies ran while one was open for 0% of the time, Pallas kernels for 0%

commit v1 on v0

v1 whole, which is shorter than its diff:
```python
import functools
import math

import jax
import jax.numpy as jnp
import ml_dtypes
import numpy as np
from jax import lax
from jax.experimental import pallas as pl
from jax.experimental.pallas import tpu as pltpu
from jax.sharding import PartitionSpec as P

DIFFUSION = 0.25
BF16 = jnp.bfloat16
F32 = jnp.float32
ROWS = 8
VMEM_BYTES = 56 * 1024 * 1024


def sine_matrix(length):
    index = np.arange(1, length + 1)
    phase = np.outer(index, index) % (2 * (length + 1))
    return np.sin(phase * (math.pi / (length + 1))) * math.sqrt(2.0 / (length + 1))


def omega(count):
    return 2.0 - 2.0 * np.cos((np.arange(count) + 1.0) * (math.pi / (count + 1)))


def fine_order(grid, groups):
    block, coarse = grid // groups, grid // 2
    half = block // 2
    position = np.arange(grid)
    within, group = position % block, position // block
    return np.where(within < half, group * half + within, coarse + group * half + within - half)


def halves(table):
    high = table.astype(ml_dtypes.bfloat16)
    low = (table - high.astype(np.float64)).astype(ml_dtypes.bfloat16)
    return high, low


def left_table(table):
    high, low = halves(table)
    return np.concatenate([high, high, low], axis=1)


def right_table(table):
    high, low = halves(table)
    return np.concatenate([high, high, low], axis=0)


def split3(value, axis):
    high = value.astype(BF16)
    low = (value - high.astype(F32)).astype(BF16)
    return jnp.concatenate([high, low, high], axis=axis)


def left(table, value):
    return jnp.dot(table, split3(value, 0), preferred_element_type=F32)


def right(value, table):
    return jnp.dot(split3(value, 1), table, preferred_element_type=F32)


def cube(value):
    return value * value * value


def whole_block(shape):
    return pl.BlockSpec(shape, lambda *_: (0,) * len(shape))


SMEM = pl.BlockSpec(memory_space=pltpu.SMEM)


def call(kernel, name, grid, in_specs, out_specs, out_shape, scratch=(), flops=0, moved=0, aliases=None):
    return pl.pallas_call(
        kernel,
        grid=grid,
        in_specs=in_specs,
        out_specs=out_specs,
        out_shape=out_shape,
        scratch_shapes=list(scratch),
        input_output_aliases=aliases or {},
        compiler_params=pltpu.CompilerParams(vmem_limit_bytes=VMEM_BYTES),
        cost_estimate=pl.CostEstimate(flops=flops, bytes_accessed=moved, transcendentals=0),
        name=name,
    )


def depth_kernel(first_ref, table_ref, initial_ref, previous_ref, out_ref):
    first = first_ref[0] == 1
    for row in range(ROWS):
        value = jnp.where(first, initial_ref[:, row, :], previous_ref[:, row, :])
        out_ref[:, row, :] = left(table_ref[...], value)


def start_kernel(planes, modes_ref, sx_ref, sy_ref, syt_ref, rho_ref,
                 low_ref, high_ref, v_ref, to_right_ref, to_left_ref, power):
    step = pl.program_id(0)

    @pl.when(step == 0)
    def _():
        power[...] = jnp.ones_like(power)
        to_right_ref[...] = jnp.zeros_like(to_right_ref)
        to_left_ref[...] = jnp.zeros_like(to_left_ref)

    groups, _, block, wide = modes_ref.shape
    grid = groups * block
    half = block // 2
    modes = [modes_ref[:, j].reshape(grid, wide) for j in range(planes)]
    along_x = right(jnp.concatenate(modes, axis=0), sx_ref[...])
    terms = [cube(left(sy_ref[...], along_x[j * grid:(j + 1) * grid])) for j in range(planes)]
    along_x = right(jnp.concatenate(terms, axis=0), sx_ref[...])
    for j in reversed(range(planes)):
        cubic = left(syt_ref[...], along_x[j * grid:(j + 1) * grid])
        source_end = 2.0 * modes[j] - cubic
        parts = source_end.reshape(groups, block, wide)
        low_ref[:, j] = parts[:, :half]
        high_ref[:, j] = parts[:, half:]
        for node, source in enumerate((source_end, 0.5 * (modes[j] + source_end))):
            rho = rho_ref[node]
            carried = source + rho * to_left_ref[node]
            to_left_ref[node] = carried
            v_ref[node, j] = carried
            to_right_ref[node] += power[node] * source
            power[node] = power[node] * rho


def node_kernel(planes, slab, modes_ref, low_ref, high_ref, v_ref, from_left_ref, from_right_ref,
                rho_ref, inverse_ref, kappa_ref, sx_ref, sy_ref, sxl_ref, syl_ref,
                out_ref, left_sum, right_sum):
    step = pl.program_id(0)

    @pl.when(step == 0)
    def _():
        left_sum[...] = from_left_ref[...]

    @pl.when(step * planes % ROWS == 0)
    def _():
        rho = rho_ref[...]
        twice = rho * rho
        four = twice * twice
        eight = four * four
        right_sum[...] = lax.fori_loop(
            0, slab // ROWS - step * planes // ROWS, lambda _, total: total * eight, from_right_ref[...]
        )

    groups, _, block, wide = modes_ref.shape
    grid = groups * block
    nodes = []
    for j in range(planes):
        source_end = jnp.concatenate([low_ref[:, j], high_ref[:, j]], axis=1).reshape(grid, wide)
        source_mid = 0.5 * (modes_ref[:, j].reshape(grid, wide) + source_end)
        for node, source in enumerate((source_end, source_mid)):
            behind = rho_ref[node] * left_sum[node]
            left_sum[node] = source + behind
            nodes.append(kappa_ref[node] * (behind + v_ref[node, j] + right_sum[node]))
            right_sum[node] = right_sum[node] * inverse_ref[node]
    along_x = right(jnp.concatenate(nodes, axis=0), sx_ref[...])
    fields = [left(sy_ref[...], along_x[j * grid:(j + 1) * grid]) for j in range(2 * planes)]
    terms = [cube(fields[2 * j]) + 4.0 * cube(fields[2 * j + 1]) for j in range(planes)]
    along_x = right(jnp.concatenate(terms, axis=0), sxl_ref[...])
    for j in range(planes):
        term = left(syl_ref[...], along_x[j * grid:(j + 1) * grid])
        out_ref[:, j] = term.reshape(groups, block // 2, wide // 2)


def low_kernel(factor, fine_ref, coarse_ref, table_ref, eigen_ref, coarse_eigen_ref, source_ref, start_ref,
               out_ref, gathered_ref):
    base = pl.program_id(0) * ROWS
    coarse = start_ref.shape[0]
    for row in range(ROWS):
        source = left(table_ref[...], source_ref[:, row, :])
        eigen = eigen_ref[...] + fine_ref[base + row]
        node_end = source / (1.0 + eigen)
        out_ref[:, row, :] = node_end
        source, node_end, eigen = source[:coarse, :coarse], node_end[:coarse, :coarse], eigen[:coarse, :coarse]
        start = start_ref[:, row, :]
        node_mid = 0.5 * (start + source) / (1.0 + 0.5 * eigen)
        rate = source - (1.0 + eigen) * start + (1.0 - eigen) * (4.0 * node_mid + node_end)
        coarse_eigen = coarse_eigen_ref[...] + coarse_ref[base + row]
        gathered_ref[:, row, :] = factor * (rate / 6.0 + coarse_eigen * node_end)


def offset_kernel(factor, first_ref, coarse_ref, table_ref, coarse_eigen_ref, cubic_ref, gathered_ref, start_ref,
                  out_ref):
    base = pl.program_id(0) * ROWS
    first = first_ref[0] == 1
    for row in range(ROWS):
        cubic = left(table_ref[...], cubic_ref[:, row, :])
        total = gathered_ref[:, row, :] - (factor / 6.0) * cubic
        total += jnp.where(first, factor * start_ref[:, row, :], 0.0)
        out_ref[:, row, :] = total / (1.0 + coarse_eigen_ref[...] + coarse_ref[base + row])


def high_kernel(fine_ref, table_ref, eigen_ref, source_ref, _, out_ref):
    base = pl.program_id(0) * ROWS
    for row in range(ROWS):
        source = left(table_ref[...], source_ref[:, row, :])
        out_ref[:, row, :] = source / (1.0 + eigen_ref[...] + fine_ref[base + row])


def shifted(value, axis, by):
    length = lax.axis_size(axis)
    pairs = [(i, i + by) for i in range(length) if 0 <= i + by < length]
    return lax.ppermute(value, axis, pairs)


def exchange(value):
    return lax.all_to_all(value, "gx", split_axis=0, concat_axis=0, tiled=True)


def per_device(end_modes, initial_modes):
    grid = initial_modes.shape[0]
    coarse = grid // 2
    groups = lax.axis_size("gx")
    block = grid // groups
    half = block // 2
    planes = 2
    slice_index = lax.axis_index("tm")
    group_index = lax.axis_index("gx")
    is_first = slice_index == 0
    first = is_first.astype(jnp.int32)[None]
    order = fine_order(grid, groups)
    sine = sine_matrix(grid)
    fine_w, coarse_w = omega(grid), omega(coarse)
    factor = ((coarse + 1) / (grid + 1)) ** 1.5
    unit = grid * block * grid

    flat = fine_w[order][:, None] + fine_w[None, :]
    scale = np.array([1.0, 0.5])[:, None, None] * DIFFUSION
    diagonal = 1.0 / scale + 2.0 + flat[None]
    rho = 2.0 / (diagonal + np.sqrt(diagonal * diagonal - 4.0))
    inverse = 1.0 / rho
    kappa = 1.0 / (scale * (inverse - rho))
    rho, inverse, kappa = (t.astype(np.float32) for t in (rho, inverse, kappa))
    rho_slab = (rho.astype(np.float64) ** block).astype(np.float32)
    rounds = 1
    while np.float32(float(rho.max()) ** (block * rounds)) > 0:
        rounds += 1

    depth_table = left_table(sine)
    x_table = right_table(sine)
    y_table = left_table(sine[:, order])
    back_table = left_table(sine[order, :])
    x_low_table = right_table(sine[:, :coarse])
    low_table = left_table(sine[:coarse, :])
    eigen = (DIFFUSION * (fine_w[:, None] + fine_w[None, :])).astype(np.float32)
    coarse_eigen = (0.25 * DIFFUSION * (coarse_w[:, None] + coarse_w[None, :])).astype(np.float32)
    fine_own = lax.dynamic_slice(jnp.asarray((DIFFUSION * fine_w[order]).astype(np.float32)), (group_index * block,), (block,))
    coarse_own = lax.dynamic_slice(
        jnp.asarray((0.25 * DIFFUSION * coarse_w).astype(np.float32)), (group_index * half,), (half,)
    )

    previous = shifted(end_modes[0], "tm", 1)
    rows_spec = pl.BlockSpec((grid, ROWS, grid), lambda i: (0, i, 0))
    table_spec = whole_block(depth_table.shape)
    outgoing = call(
        depth_kernel,
        "depth",
        (block // ROWS,),
        [SMEM, table_spec, rows_spec, rows_spec],
        rows_spec,
        jax.ShapeDtypeStruct((grid, block, grid), F32),
        flops=6 * unit * grid,
        moved=12 * unit,
    )(first, depth_table, initial_modes, previous)
    modes = exchange(outgoing).reshape(groups, block, block, grid)
    start_low = jnp.where(is_first, initial_modes[:coarse, :half, :coarse], previous[:coarse, :half, :coarse])

    steps = block // planes
    pair = (2, grid, grid)
    pair_spec = whole_block(pair)
    back = lambda i: (0, steps - 1 - i, 0, 0)
    low, high, v, to_right, to_left = call(
        functools.partial(start_kernel, planes),
        "start",
        (steps,),
        [
            pl.BlockSpec((groups, planes, block, grid), back),
            whole_block(x_table.shape),
            table_spec,
            table_spec,
            pair_spec,
        ],
        [
            pl.BlockSpec((groups, planes, half, grid), back),
            pl.BlockSpec((groups, planes, half, grid), back),
            pl.BlockSpec((2, planes, grid, grid), back),
            pair_spec,
            pair_spec,
        ],
        [
            jax.ShapeDtypeStruct((groups, block, half, grid), F32),
            jax.ShapeDtypeStruct((groups, block, half, grid), F32),
            jax.ShapeDtypeStruct((2, block, grid, grid), F32),
            jax.ShapeDtypeStruct(pair, F32),
            jax.ShapeDtypeStruct(pair, F32),
        ],
        scratch=[pltpu.VMEM(pair, F32)],
        flops=24 * unit * grid,
        moved=16 * unit,
    )(modes, x_table, y_table, back_table, rho)
    low_back = exchange(low.reshape(grid, half, grid))

    from_left = jnp.zeros(pair, F32)
    from_right = jnp.zeros(pair, F32)
    for _ in range(rounds):
        rightward = to_right + rho_slab * from_left
        leftward = to_left + rho_slab * from_right
        from_left = jnp.where(group_index == 0, -rho * leftward, shifted(rightward, "gx", 1))
        from_right = jnp.where(group_index == groups - 1, -rho * rightward, shifted(leftward, "gx", -1))

    ahead = lambda i: (0, i, 0, 0)
    cubic = call(
        functools.partial(node_kernel, planes, block),
        "nodes",
        (steps,),
        [
            pl.BlockSpec((groups, planes, block, grid), ahead),
            pl.BlockSpec((groups, planes, half, grid), ahead),
            pl.BlockSpec((groups, planes, half, grid), ahead),
            pl.BlockSpec((2, planes, grid, grid), ahead),
            pair_spec,
            pair_spec,
            pair_spec,
            pair_spec,
            pair_spec,
            whole_block(x_table.shape),
            table_spec,
            whole_block(x_low_table.shape),
            whole_block(low_table.shape),
        ],
        pl.BlockSpec((groups, planes, half, coarse), ahead),
        jax.ShapeDtypeStruct((groups, block, half, coarse), F32),
        scratch=[pltpu.VMEM(pair, F32), pltpu.VMEM(pair, F32)],
        flops=28 * unit * grid,
        moved=17 * unit,
    )(modes, low, high, v, from_left, from_right, rho, inverse, kappa, x_table, y_table, x_low_table, low_table)
    cubic, high = lax.optimization_barrier((cubic, high))
    cubic_back = exchange(cubic.reshape(grid, half, coarse))
    high_back = exchange(high.reshape(grid, half, grid))

    low_spec = pl.BlockSpec((coarse, ROWS, coarse), lambda i: (0, i, 0))
    eigen_spec = whole_block(eigen.shape)
    coarse_eigen_spec = whole_block(coarse_eigen.shape)
    corner = jax.ShapeDtypeStruct((coarse, half, coarse), F32)
    result, gathered = call(
        functools.partial(low_kernel, factor),
        "low",
        (half // ROWS,),
        [SMEM, SMEM, table_spec, eigen_spec, coarse_eigen_spec, rows_spec, low_spec],
        [rows_spec, low_spec],
        [jax.ShapeDtypeStruct((grid, block, grid), F32), corner],
        flops=3 * unit * grid,
        moved=5 * unit,
    )(fine_own, coarse_own, depth_table, eigen, coarse_eigen, low_back, start_low)
    offset = call(
        functools.partial(offset_kernel, factor),
        "offset",
        (half // ROWS,),
        [
            SMEM,
            SMEM,
            whole_block(low_table.shape),
            coarse_eigen_spec,
            pl.BlockSpec((grid, ROWS, coarse), lambda i: (0, i, 0)),
            low_spec,
            low_spec,
        ],
        low_spec,
        corner,
        flops=unit * grid,
        moved=2 * unit,
    )(first, coarse_own, low_table, coarse_eigen, cubic_back, gathered, start_low)

    decay = 1.0 / (1.0 + coarse_eigen[:, None, :] + coarse_own[None, :, None])
    coarse_end = offset
    for _ in range(lax.axis_size("tm") - 1):
        coarse_end = jnp.where(is_first, offset, decay * shifted(coarse_end, "tm", 1) + offset)
    result = result.at[:coarse, :half, :coarse].set(coarse_end / factor)
    result = call(
        high_kernel,
        "high",
        (half // ROWS,),
        [SMEM, table_spec, eigen_spec, rows_spec, pl.BlockSpec(memory_space=pl.ANY)],
        pl.BlockSpec((grid, ROWS, grid), lambda i: (0, half // ROWS + i, 0)),
        jax.ShapeDtypeStruct((grid, block, grid), F32),
        flops=3 * unit * grid,
        moved=5 * unit,
        aliases={4: 0},
    )(fine_own[half:], depth_table, eigen, high_back, result)
    return (result[None], coarse_end[None])


def solution(mesh):
    return jax.shard_map(
        per_device,
        mesh=mesh,
        in_specs=(P("tm", None, "gx", None), P(None, "gx", None)),
        out_specs=(P("tm", None, "gx", None), P("tm", None, "gx", None)),
        check_vma=False,
    )
```

time: 1130 us -> 645 us (0.57)
  waiting for transfers between devices: 806 us -> 146 us
  blocking collectives: 0 us -> 268 us
  Pallas kernels: 0 us -> 177 us
  matrix products: 169 us -> 0 us
  local copies, waits for them, and re-layouts: 89.6 us -> 1.98 us
    all_to_all x4 -> x1, waiting for transfers between devices: 680 us -> 0.01 us  [exchange(): return lax.all_to_all(value, 'gx', split_axis=0, concat_axis=0, tiled=True)]
    all_to_all x0 -> x3, blocking collectives: none -> 268 us  [exchange(): return lax.all_to_all(value, 'gx', split_axis=0, concat_axis=0, tiled=True)]
    pallas_call x0 -> x6, Pallas kernels: none -> 177 us  [the longest x1 44 us: per_device(): call(functools.partial(node_kernel, planes, block), 'nodes', (steps,), [p...]
    dot_general x12 -> x0, matrix products: 169 us -> none  [the longest x3 62.1 us: depth(): return jnp.einsum('fzpk,zq->fqpk', stack, table, precision=HIGHEST)]
    transpose x4 -> x0, local copies, waits for them, and re-layouts: 38.4 us -> none  [the longest x2 25.8 us: depth(): return jnp.einsum('fzpk,zq->fqpk', stack, table, precision=HIGHEST)]
    all_to_all x4 -> x0, local copies, waits for them, and re-layouts: 27.2 us -> none  [the longest x1 11.9 us: per_device(): lax.all_to_all(depth(node_stack), 'gx', split_axis=1, concat_axis=2, tile...]
    unnamed x6 -> x16, local copies, waits for them, and re-layouts: 24 us -> 0.03 us
    ppermute x4 -> x8, waiting for transfers between devices: 126 us -> 146 us  [shifted(): return lax.ppermute(value, axis, pairs)]
  transfers between devices with their start and end apart: 8 -> 9, of which waited for: 8 -> 8; matrix products, arithmetic and copies ran while one was open for 0% -> 2% of each run, Pallas kernels for 0% -> 6%
where the time goes in v1:
time: 645 us; the launch traced here: 641 us
  blocking collectives  268 us (42%)
  Pallas kernels  177 us (27%)
  waiting for transfers between devices  146 us (23%)
  starting transfers between devices  35 us (5%)
  other arithmetic  13 us (2%)
    all_to_all x3, blocking collectives, exchange(): return lax.all_to_all(value, 'gx', split_axis=0, concat_axis=0, tiled=True)  268 us
    ppermute x8, waiting for transfers between devices, shifted(): return lax.ppermute(value, axis, pairs)  146 us
    pallas_call x1, Pallas kernels, per_device(): call(functools.partial(node_kernel, planes, block), 'nodes', (steps,), [p...  44 us
    pallas_call x1, Pallas kernels, per_device(): call(functools.partial(start_kernel, planes), 'start', (steps,), [pl.Bloc...  38 us
    pallas_call x1, Pallas kernels, per_device(): call(depth_kernel, 'depth', (block // ROWS,), [SMEM, table_spec, rows_spe...  37.3 us
    ppermute x8, starting transfers between devices, shifted(): return lax.ppermute(value, axis, pairs)  30.4 us
    pallas_call x1, Pallas kernels, per_device(): call(functools.partial(offset_kernel, factor), 'offset', (half // ROWS,),...  19.8 us
    pallas_call x1, Pallas kernels, per_device(): call(functools.partial(low_kernel, factor), 'low', (half // ROWS,), [SMEM...  19.8 us
  transfers between devices with their start and end apart: 9, of which 8 were waited for; matrix products, arithmetic and copies ran while one was open for 2% of the time, Pallas kernels for 6%

profile of v1, /device:TPU:1, one launch (start us, length us, event | category | flops | bytes accessed | tf_op | source)
XLA Modules:
  0.0 640.8 jit_solution(17826100151632794290)
XLA Ops:
  0.6 4.5 collective-permute-start
  5.2 90.7 %collective-permute-done.previous_ref = f32[256,32,256]{2,1,0:T(8,128)} collective-permute-done((f32[256,32,256]{2,1,0:T(8,128)}, f32[256,32,256]{2,1,0:T(8,128)}, u32[]{:S(2)}, u32[]{:S(2)}) %collective-permute-start) | collective-permute-done | bytes 8388640 | tf_op jit(solution)/shard_map/ppermute | solution.py:210
  95.9 37.3 %depth.1 = f32[256,32,256]{2,1,0:T(8,128)} custom-call(s32[1]{0:T(128)} %bitcast.first_ref, bf16[256,768]{1,0:T(8,128)(2,1)} %constant.88.clone.table_ref, f32[256,32,256]{2,1,0:T(8,128)} %initial_ref.1, f32[256,32,256]{2,1,0:T(8,128)} %collective-permute-done.previous_ref), custom_call_target="tpu_custom_call" | custom-call | flops 3221225472 | bytes 25165824 | tf_op jit(solution)/shard_map/depth/pallas_call | solution.py:262
  133.1 110.9 %all_to_all.20 = f32[256,32,256]{2,1,0:T(8,128)} all-to-all(f32[256,32,256]{2,1,0:T(8,128)} %depth.1), channel_id=1, replica_groups=mesh['tm'=4,'gx'=8] {'gx'}, dimensions={0} | all-to-all | bytes 16777216 | tf_op jit(solution)/shard_map/all_to_all | solution.py:214
  244.0 38.0 %start.1 = (f32[8,32,16,256]{3,2,1,0:T(8,128)}, f32[8,32,16,256]{3,2,1,0:T(8,128)}, f32[2,32,256,256]{3,2,1,0:T(8,128)}, f32[2,256,256]{2,1,0:T(8,128)}, f32[2,256,256]{2,1,0:T(8,128)}) custom-call(f32[8,32,32,256]{3,2,1,0:T(8,128)} %bitcast.9, bf16[768,256]{1,0:T(8,128)(2,1)} %constant.89.clone.sx_ref, bf16[256,768]{1,0:T(8,128)(2,1)} %constant.90.clone.sy_ref, ...), custom_call_target="tpu_custom_call" | custom-call | flops 12884901888 | bytes 33554432 | tf_op jit(solution)/shard_map/start/pallas_call | solution.py:279
  282.0 1.3 collective-permute-start.1
  283.3 4.0 collective-permute-start.2
  287.3 4.8 collective-permute-done.1
  292.2 1.4 multiply_add_fusion.1
  293.5 1.3 collective-permute-start.4
  294.8 3.7 collective-permute-done.2
  298.6 5.8 collective-permute-done.4
  304.3 2.2 multiply_select_fusion
  306.5 8.7 %collective-permute-start.3 = (f32[2,256,256]{2,1,0:T(8,128)S(1)}, f32[2,256,256]{2,1,0:T(8,128)S(1)}, u32[]{:S(2)}, u32[]{:S(2)}) collective-permute-start(f32[2,256,256]{2,1,0:T(8,128)S(1)} %get-tuple-element.33), channel_id=1, source_target_pairs={{0,1},{1,2},{2,3},{3,4},{4,5},{5,6},{6,7},{8,9},{9,10},{10,11},{11... | collective-permute-start | bytes 1572872 | tf_op jit(solution)/shard_map/ppermute | solution.py:210
  315.2 5.8 collective-permute-done.3
  322.0 44.0 %nodes.1 = f32[8,32,16,128]{3,2,1,0:T(8,128)} custom-call(f32[8,32,32,256]{3,2,1,0:T(8,128)} %bitcast.10, f32[8,32,16,256]{3,2,1,0:T(8,128)} %get-tuple-element.23.low_ref, f32[8,32,16,256]{3,2,1,0:T(8,128)} %get-tuple-element.28.high_ref, f32[2,32,256,256]{3,2,1,0:T(8,128)} %get-tuple-element.25.v_ref, f32[2,256,256]{2,1,0:T(8,128)} %multiply_select_fusion.1.from_left_ref, ...), custom_call_target="tpu_custom_call" | custom-call | flops 15032385536 | bytes 35651584 | tf_op jit(solution)/shard_map/nodes/pallas_call | solution.py:319
  365.9 67.0 %all_to_all.21.cubic_ref = f32[256,16,128]{2,1,0:T(8,128)} all-to-all(f32[256,16,128]{2,1,0:T(8,128)} %bitcast.14), channel_id=1, replica_groups=mesh['tm'=4,'gx'=8] {'gx'}, dimensions={0} | all-to-all | bytes 4194304 | tf_op jit(solution)/shard_map/all_to_all | solution.py:214
  432.9 89.6 %all_to_all.22.source_ref = f32[256,16,256]{2,1,0:T(8,128)} all-to-all(f32[256,16,256]{2,1,0:T(8,128)S(1)} %bitcast.13), channel_id=1, replica_groups=mesh['tm'=4,'gx'=8] {'gx'}, dimensions={0} | all-to-all | bytes 8388608 | tf_op jit(solution)/shard_map/all_to_all | solution.py:214
  522.6 4.6 all-to-all-start.1
  528.5 2.7 slice_select_fusion.start_ref
  531.2 19.8 %low.1 = (f32[256,32,256]{2,1,0:T(8,128)}, f32[128,16,128]{2,1,0:T(8,128)}) custom-call(f32[32]{0:T(128)} %dynamic_slice.6.fine_ref, f32[16]{0:T(128)} %dynamic_slice.7.coarse_ref, bf16[256,768]{1,0:T(8,128)(2,1)} %constant.88.clone.table_ref, f32[256,256]{1,0:T(8,128)} %constant.99.clone.eigen_ref, f32[128,128]{1,0:T(8,128)} %constant.100.clone.coarse_eigen_ref, ...), custom_call_target="tpu_custom_call" | custom-call | flops 1610612736 | bytes 10485760 | tf_op jit(solution)/shard_map/low/pallas_call | solution.py:352
  551.0 19.8 %offset.1 = f32[128,16,128]{2,1,0:T(8,128)} custom-call(s32[1]{0:T(128)} %bitcast.first_ref, f32[16]{0:T(128)} %dynamic_slice.7.coarse_ref, bf16[128,768]{1,0:T(8,128)(2,1)} %constant.98.clone.syl_ref.table_ref, f32[128,128]{1,0:T(8,128)} %constant.100.clone.coarse_eigen_ref, f32[256,16,128]{2,1,0:T(8,128)} %all_to_all.21.cubic_ref, ...), custom_call_target="tpu_custom_call" | custom-call | flops 536870912 | bytes 4194304 | tf_op jit(solution)/shard_map/offset/pallas_call | solution.py:362
  570.8 1.9 collective-permute-start.5
  572.7 12.0 %collective-permute-done.5 = f32[128,16,128]{2,1,0:T(8,128)S(1)} collective-permute-done((f32[128,16,128]{2,1,0:T(8,128)}, f32[128,16,128]{2,1,0:T(8,128)S(1)}, u32[]{:S(2)}, u32[]{:S(2)}) %collective-permute-start.5) | collective-permute-done | bytes 1048608 | tf_op jit(solution)/shard_map/ppermute | solution.py:210
  584.8 1.5 add_select_fusion.2
  586.3 4.3 collective-permute-start.6
  590.6 11.7 %collective-permute-done.6 = f32[128,16,128]{2,1,0:T(8,128)S(1)} collective-permute-done((f32[128,16,128]{2,1,0:T(8,128)S(1)}, f32[128,16,128]{2,1,0:T(8,128)S(1)}, u32[]{:S(2)}, u32[]{:S(2)}) %collective-permute-start.6) | collective-permute-done | bytes 1048608 | tf_op jit(solution)/shard_map/ppermute | solution.py:210
  602.3 1.5 add_select_fusion.1
  603.8 4.4 collective-permute-start.7
  608.8 11.1 %collective-permute-done.7 = f32[128,16,128]{2,1,0:T(8,128)S(1)} collective-permute-done((f32[128,16,128]{2,1,0:T(8,128)S(1)}, f32[128,16,128]{2,1,0:T(8,128)S(1)}, u32[]{:S(2)}, u32[]{:S(2)}) %collective-permute-start.7) | collective-permute-done | bytes 1048608 | tf_op jit(solution)/shard_map/ppermute | solution.py:210
  619.9 2.8 fusion
  622.7 17.9 %high.1 = f32[256,32,256]{2,1,0:T(8,128)} custom-call(f32[16]{0:T(128)} %slice.37.fine_ref, bf16[256,768]{1,0:T(8,128)(2,1)} %constant.88.clone.table_ref, f32[256,256]{1,0:T(8,128)} %constant.99.clone.eigen_ref, f32[256,16,256]{2,1,0:T(8,128)} %all-to-all-done.1.source_ref, f32[256,32,256]{2,1,0:T(8,128)} %get-tuple-element.35._), custom_call_target="tpu_custom_call", output_to_operand_aliasing={{}: (4, {})} | custom-call | flops 1610612736 | bytes 10485760 | tf_op jit(solution)/shard_map/high/pallas_call | solution.py:386
  (21 shorter events, 2.9 us)
Async XLA Ops:
  0.6 95.2 %collective-permute-start = (f32[256,32,256]{2,1,0:T(8,128)}, f32[256,32,256]{2,1,0:T(8,128)}, u32[]{:S(2)}, u32[]{:S(2)}) collective-permute-start(f32[256,32,256]{2,1,0:T(8,128)} %bitcast.15), channel_id=1, source_target_pairs={{0,8},{8,16},{16,24},{1,9},{9,17},{17,25},{2,10},{10,18},{18,26},{... | collective-permute-start | bytes 25165832 | tf_op jit(solution)/shard_map/ppermute | solution.py:210
  244.0 48.1 %copy-start = (f32[2,256,256]{2,1,0:T(8,128)S(1)}, f32[2,256,256]{2,1,0:T(8,128)}, u32[]{:S(2)}) copy-start(f32[2,256,256]{2,1,0:T(8,128)} %constant.94.clone) | copy-start | bytes 1572868
  244.0 48.1 %copy-start.2 = (f32[2,256,256]{2,1,0:T(8,128)S(1)}, f32[2,256,256]{2,1,0:T(8,128)}, u32[]{:S(2)}) copy-start(f32[2,256,256]{2,1,0:T(8,128)} %constant.93.clone) | copy-start | bytes 1572868
  282.0 10.1 %collective-permute-start.1 = (f32[2,256,256]{2,1,0:T(8,128)}, f32[2,256,256]{2,1,0:T(8,128)S(1)}, u32[]{:S(2)}, u32[]{:S(2)}) collective-permute-start(f32[2,256,256]{2,1,0:T(8,128)} %get-tuple-element.26), channel_id=1, source_target_pairs={{1,0},{2,1},{3,2},{4,3},{5,4},{6,5},{7,6},{9,8},{10,9},{11,10},{12... | collective-permute-start | bytes 1572872 | tf_op jit(solution)/shard_map/ppermute | solution.py:210
  283.3 15.2 %collective-permute-start.2 = (f32[2,256,256]{2,1,0:T(8,128)}, f32[2,256,256]{2,1,0:T(8,128)S(1)}, u32[]{:S(2)}, u32[]{:S(2)}) collective-permute-start(f32[2,256,256]{2,1,0:T(8,128)} %get-tuple-element.27), channel_id=1, source_target_pairs={{0,1},{1,2},{2,3},{3,4},{4,5},{5,6},{6,7},{8,9},{9,10},{10,11},{11... | collective-permute-start | bytes 1572872 | tf_op jit(solution)/shard_map/ppermute | solution.py:210
  293.5 10.8 %collective-permute-start.4 = (f32[2,256,256]{2,1,0:T(8,128)S(1)}, f32[2,256,256]{2,1,0:T(8,128)S(1)}, u32[]{:S(2)}, u32[]{:S(2)}) collective-permute-start(f32[2,256,256]{2,1,0:T(8,128)S(1)} %multiply_add_fusion.1), channel_id=1, source_target_pairs={{1,0},{2,1},{3,2},{4,3},{5,4},{6,5},{7,6},{9,8},{10,9},{11,10},{12... | collective-permute-start | bytes 1572872 | tf_op jit(solution)/shard_map/ppermute | solution.py:210
  306.5 14.5 %collective-permute-start.3 = (f32[2,256,256]{2,1,0:T(8,128)S(1)}, f32[2,256,256]{2,1,0:T(8,128)S(1)}, u32[]{:S(2)}, u32[]{:S(2)}) collective-permute-start(f32[2,256,256]{2,1,0:T(8,128)S(1)} %get-tuple-element.33), channel_id=1, source_target_pairs={{0,1},{1,2},{2,3},{3,4},{4,5},{5,6},{6,7},{8,9},{9,10},{10,11},{11... | collective-permute-start | bytes 1572872 | tf_op jit(solution)/shard_map/ppermute | solution.py:210
  322.0 111.0 %copy-start.1 = (f32[8,32,16,256]{3,2,1,0:T(8,128)S(1)}, f32[8,32,16,256]{3,2,1,0:T(8,128)}, u32[]{:S(2)}) copy-start(f32[8,32,16,256]{3,2,1,0:T(8,128)} %get-tuple-element.23.low_ref) | copy-start | bytes 12582916
  432.9 94.3 %copy-start.7 = (f32[128]{0:T(128)S(1)}, f32[128]{0:T(128)}, u32[]{:S(2)}) copy-start(f32[128]{0:T(128)} %constant.87.clone) | copy-start | bytes 1540
  432.9 94.9 %copy-start.6 = (f32[256]{0:T(256)S(1)}, f32[256]{0:T(256)}, u32[]{:S(2)}) copy-start(f32[256]{0:T(256)} %constant.86.clone) | copy-start | bytes 3076
  522.6 100.2 %all-to-all-start.1 = ((f32[256,16,256]{2,1,0:T(8,128)}), f32[256,16,256]{2,1,0:T(8,128)}, u32[]{:S(2)}, u32[]{:S(2)}) async-start(f32[256,16,256]{2,1,0:T(8,128)} %bitcast.12), calls=%async_computation.1 | async-start | bytes 8388608 | tf_op jit(solution)/shard_map/all_to_all | solution.py:214
  527.2 57.6 %copy-start.3 = (f32[128,128]{1,0:T(8,128)S(1)}, f32[128,128]{1,0:T(8,128)}, u32[]{:S(2)}) copy-start(f32[128,128]{1,0:T(8,128)} %constant.104) | copy-start | bytes 196612
  527.9 56.9 %copy-start.4 = (f32[16]{0:T(128)S(1)}, f32[16]{0:T(128)}, u32[]{:S(2)}) copy-start(f32[16]{0:T(128)} %dynamic_slice.7.coarse_ref) | copy-start | bytes 196
  531.2 77.0 %copy-start.5 = (f32[32]{0:T(128)S(1)}, f32[32]{0:T(128)}, u32[]{:S(2)}) copy-start(f32[32]{0:T(128)} %dynamic_slice.6.fine_ref) | copy-start | bytes 388
  570.8 14.0 %collective-permute-start.5 = (f32[128,16,128]{2,1,0:T(8,128)}, f32[128,16,128]{2,1,0:T(8,128)S(1)}, u32[]{:S(2)}, u32[]{:S(2)}) collective-permute-start(f32[128,16,128]{2,1,0:T(8,128)} %offset.1), channel_id=1, source_target_pairs={{0,8},{8,16},{16,24},{1,9},{9,17},{17,25},{2,10},{10,18},{18,26},{... | collective-permute-start | bytes 3145736 | tf_op jit(solution)/shard_map/ppermute | solution.py:210
  586.3 16.0 %collective-permute-start.6 = (f32[128,16,128]{2,1,0:T(8,128)S(1)}, f32[128,16,128]{2,1,0:T(8,128)S(1)}, u32[]{:S(2)}, u32[]{:S(2)}) collective-permute-start(f32[128,16,128]{2,1,0:T(8,128)S(1)} %add_select_fusion.2), channel_id=1, source_target_pairs={{0,8},{8,16},{16,24},{1,9},{9,17},{17,25},{2,10},{10,18},{18,26},{... | collective-permute-start | bytes 3145736 | tf_op jit(solution)/shard_map/ppermute | solution.py:210
  603.8 16.1 %collective-permute-start.7 = (f32[128,16,128]{2,1,0:T(8,128)S(1)}, f32[128,16,128]{2,1,0:T(8,128)S(1)}, u32[]{:S(2)}, u32[]{:S(2)}) collective-permute-start(f32[128,16,128]{2,1,0:T(8,128)S(1)} %add_select_fusion.1), channel_id=1, source_target_pairs={{0,8},{8,16},{16,24},{1,9},{9,17},{17,25},{2,10},{10,18},{18,26},{... | collective-permute-start | bytes 3145736 | tf_op jit(solution)/shard_map/ppermute | solution.py:210

commit v2 on v1

--- a/solution.py
+++ b/solution.py
@@ -92,14 +92,14 @@
 
 
 def depth_kernel(first_ref, table_ref, initial_ref, previous_ref, out_ref):
-    first = first_ref[0] == 1
-    for row in range(ROWS):
-        value = jnp.where(first, initial_ref[:, row, :], previous_ref[:, row, :])
-        out_ref[:, row, :] = left(table_ref[...], value)
+    value = jnp.where(first_ref[0] == 1, initial_ref[...], previous_ref[...])
+    value = jnp.swapaxes(value, 0, 1)
+    rows = [left(table_ref[...], value[row]) for row in range(ROWS)]
+    out_ref[...] = jnp.swapaxes(jnp.stack(rows), 0, 1)
 
 
 def start_kernel(planes, modes_ref, sx_ref, sy_ref, syt_ref, rho_ref,
-                 low_ref, high_ref, v_ref, to_right_ref, to_left_ref, power):
+                 low_ref, high_ref, v_ref, to_right_ref, to_left_ref, power, cubic):
     step = pl.program_id(0)
 
     @pl.when(step == 0)
@@ -115,24 +115,35 @@
     along_x = right(jnp.concatenate(modes, axis=0), sx_ref[...])
     terms = [cube(left(sy_ref[...], along_x[j * grid:(j + 1) * grid])) for j in range(planes)]
     along_x = right(jnp.concatenate(terms, axis=0), sx_ref[...])
-    for j in reversed(range(planes)):
-        cubic = left(syt_ref[...], along_x[j * grid:(j + 1) * grid])
-        source_end = 2.0 * modes[j] - cubic
-        parts = source_end.reshape(groups, block, wide)
-        low_ref[:, j] = parts[:, :half]
-        high_ref[:, j] = parts[:, half:]
-        for node, source in enumerate((source_end, 0.5 * (modes[j] + source_end))):
-            rho = rho_ref[node]
-            carried = source + rho * to_left_ref[node]
-            to_left_ref[node] = carried
-            v_ref[node, j] = carried
-            to_right_ref[node] += power[node] * source
-            power[node] = power[node] * rho
+    for j in range(planes):
+        cubic[j] = left(syt_ref[...], along_x[j * grid:(j + 1) * grid])
+    for strip in range(2 * groups):
+        group, upper = strip // 2, strip % 2
+        rows = slice(strip * half, (strip + 1) * half)
+        within = slice(upper * half, (upper + 1) * half)
+        out_ref = high_ref if upper else low_ref
+        rho = [rho_ref[node, rows] for node in range(2)]
+        carried = [to_left_ref[node, rows] for node in range(2)]
+        weight = [power[node, rows] for node in range(2)]
+        total = [to_right_ref[node, rows] for node in range(2)]
+        for j in reversed(range(planes)):
+            mode = modes_ref[group, j, within]
+            source = 2.0 * mode - cubic[j, rows]
+            out_ref[group, j] = source
+            for node, value in enumerate((source, 0.5 * (mode + source))):
+                carried[node] = value + rho[node] * carried[node]
+                v_ref[node, j, rows] = carried[node]
+                total[node] += weight[node] * value
+                weight[node] = weight[node] * rho[node]
+        for node in range(2):
+            to_left_ref[node, rows] = carried[node]
+            power[node, rows] = weight[node]
+            to_right_ref[node, rows] = total[node]
 
 
 def node_kernel(planes, slab, modes_ref, low_ref, high_ref, v_ref, from_left_ref, from_right_ref,
                 rho_ref, inverse_ref, kappa_ref, sx_ref, sy_ref, sxl_ref, syl_ref,
-                out_ref, left_sum, right_sum):
+                out_ref, left_sum, right_sum, nodes):
     step = pl.program_id(0)
 
     @pl.when(step == 0)
@@ -151,57 +162,79 @@
 
     groups, _, block, wide = modes_ref.shape
     grid = groups * block
-    nodes = []
-    for j in range(planes):
-        source_end = jnp.concatenate([low_ref[:, j], high_ref[:, j]], axis=1).reshape(grid, wide)
-        source_mid = 0.5 * (modes_ref[:, j].reshape(grid, wide) + source_end)
-        for node, source in enumerate((source_end, source_mid)):
-            behind = rho_ref[node] * left_sum[node]
-            left_sum[node] = source + behind
-            nodes.append(kappa_ref[node] * (behind + v_ref[node, j] + right_sum[node]))
-            right_sum[node] = right_sum[node] * inverse_ref[node]
-    along_x = right(jnp.concatenate(nodes, axis=0), sx_ref[...])
+    half = block // 2
+    for strip in range(2 * groups):
+        group, upper = strip // 2, strip % 2
+        rows = slice(strip * half, (strip + 1) * half)
+        within = slice(upper * half, (upper + 1) * half)
+        source_ref = high_ref if upper else low_ref
+        rho = [rho_ref[node, rows] for node in range(2)]
+        inverse = [inverse_ref[node, rows] for node in range(2)]
+        kappa = [kappa_ref[node, rows] for node in range(2)]
+        before = [left_sum[node, rows] for node in range(2)]
+        after = [right_sum[node, rows] for node in range(2)]
+        for j in range(planes):
+            source = source_ref[group, j]
+            for node, value in enumerate((source, 0.5 * (modes_ref[group, j, within] + source))):
+                behind = rho[node] * before[node]
+                before[node] = value + behind
+                nodes[node, j, rows] = kappa[node] * (behind + v_ref[node, j, rows] + after[node])
+                after[node] = after[node] * inverse[node]
+        for node in range(2):
+            left_sum[node, rows] = before[node]
+            right_sum[node, rows] = after[node]
+    along_x = right(nodes[...].reshape(2 * planes * grid, wide), sx_ref[...])
     fields = [left(sy_ref[...], along_x[j * grid:(j + 1) * grid]) for j in range(2 * planes)]
-    terms = [cube(fields[2 * j]) + 4.0 * cube(fields[2 * j + 1]) for j in range(planes)]
+    terms = [cube(fields[j]) + 4.0 * cube(fields[planes + j]) for j in range(planes)]
     along_x = right(jnp.concatenate(terms, axis=0), sxl_ref[...])
     for j in range(planes):
         term = left(syl_ref[...], along_x[j * grid:(j + 1) * grid])
-        out_ref[:, j] = term.reshape(groups, block // 2, wide // 2)
+        out_ref[:, j] = term.reshape(groups, half, wide // 2)
 
 
 def low_kernel(factor, fine_ref, coarse_ref, table_ref, eigen_ref, coarse_eigen_ref, source_ref, start_ref,
                out_ref, gathered_ref):
     base = pl.program_id(0) * ROWS
     coarse = start_ref.shape[0]
+    sources = jnp.swapaxes(source_ref[...], 0, 1)
+    starts = jnp.swapaxes(start_ref[...], 0, 1)
+    ends, gathered = [], []
     for row in range(ROWS):
-        source = left(table_ref[...], source_ref[:, row, :])
+        source = left(table_ref[...], sources[row])
         eigen = eigen_ref[...] + fine_ref[base + row]
         node_end = source / (1.0 + eigen)
-        out_ref[:, row, :] = node_end
+        ends.append(node_end)
         source, node_end, eigen = source[:coarse, :coarse], node_end[:coarse, :coarse], eigen[:coarse, :coarse]
-        start = start_ref[:, row, :]
+        start = starts[row]
         node_mid = 0.5 * (start + source) / (1.0 + 0.5 * eigen)
         rate = source - (1.0 + eigen) * start + (1.0 - eigen) * (4.0 * node_mid + node_end)
         coarse_eigen = coarse_eigen_ref[...] + coarse_ref[base + row]
-        gathered_ref[:, row, :] = factor * (rate / 6.0 + coarse_eigen * node_end)
+        gathered.append(factor * (rate / 6.0 + coarse_eigen * node_end))
+    out_ref[...] = jnp.swapaxes(jnp.stack(ends), 0, 1)
+    gathered_ref[...] = jnp.swapaxes(jnp.stack(gathered), 0, 1)
 
 
 def offset_kernel(factor, first_ref, coarse_ref, table_ref, coarse_eigen_ref, cubic_ref, gathered_ref, start_ref,
                   out_ref):
     base = pl.program_id(0) * ROWS
     first = first_ref[0] == 1
+    cubics = jnp.swapaxes(cubic_ref[...], 0, 1)
+    given = jnp.swapaxes(gathered_ref[...] + jnp.where(first, factor * start_ref[...], 0.0), 0, 1)
+    rows = []
     for row in range(ROWS):
-        cubic = left(table_ref[...], cubic_ref[:, row, :])
-        total = gathered_ref[:, row, :] - (factor / 6.0) * cubic
-        total += jnp.where(first, factor * start_ref[:, row, :], 0.0)
-        out_ref[:, row, :] = total / (1.0 + coarse_eigen_ref[...] + coarse_ref[base + row])
+        total = given[row] - (factor / 6.0) * left(table_ref[...], cubics[row])
+        rows.append(total / (1.0 + coarse_eigen_ref[...] + coarse_ref[base + row]))
+    out_ref[...] = jnp.swapaxes(jnp.stack(rows), 0, 1)
 
 
 def high_kernel(fine_ref, table_ref, eigen_ref, source_ref, _, out_ref):
     base = pl.program_id(0) * ROWS
+    sources = jnp.swapaxes(source_ref[...], 0, 1)
+    rows = []
     for row in range(ROWS):
-        source = left(table_ref[...], source_ref[:, row, :])
-        out_ref[:, row, :] = source / (1.0 + eigen_ref[...] + fine_ref[base + row])
+        source = left(table_ref[...], sources[row])
+        rows.append(source / (1.0 + eigen_ref[...] + fine_ref[base + row]))
+    out_ref[...] = jnp.swapaxes(jnp.stack(rows), 0, 1)
 
 
 def shifted(value, axis, by):
@@ -220,7 +253,7 @@
     groups = lax.axis_size("gx")
     block = grid // groups
     half = block // 2
-    planes = 2
+    planes = 4
     slice_index = lax.axis_index("tm")
     group_index = lax.axis_index("gx")
     is_first = slice_index == 0
@@ -301,7 +334,7 @@
             jax.ShapeDtypeStruct(pair, F32),
             jax.ShapeDtypeStruct(pair, F32),
         ],
-        scratch=[pltpu.VMEM(pair, F32)],
+        scratch=[pltpu.VMEM(pair, F32), pltpu.VMEM((planes, grid, grid), F32)],
         flops=24 * unit * grid,
         moved=16 * unit,
     )(modes, x_table, y_table, back_table, rho)
@@ -337,11 +370,11 @@
         ],
         pl.BlockSpec((groups, planes, half, coarse), ahead),
         jax.ShapeDtypeStruct((groups, block, half, coarse), F32),
-        scratch=[pltpu.VMEM(pair, F32), pltpu.VMEM(pair, F32)],
+        scratch=[pltpu.VMEM(pair, F32), pltpu.VMEM(pair, F32), pltpu.VMEM((2, planes, grid, grid), F32)],
         flops=28 * unit * grid,
         moved=17 * unit,
     )(modes, low, high, v, from_left, from_right, rho, inverse, kappa, x_table, y_table, x_low_table, low_table)
-    cubic, high = lax.optimization_barrier((cubic, high))
+    cubic, high, low_back = lax.optimization_barrier((cubic, high, low_back))
     cubic_back = exchange(cubic.reshape(grid, half, coarse))
     high_back = exchange(high.reshape(grid, half, grid))
 

time: 645 us -> 546 us (0.85)
  blocking collectives: 268 us -> 177 us
  Pallas kernels: 177 us -> 101 us
  waiting for transfers between devices: 146 us -> 192 us
  starting transfers between devices: 35 us -> 59.5 us
    all_to_all x3 -> x2, blocking collectives: 268 us -> 177 us  [exchange(): return lax.all_to_all(value, 'gx', split_axis=0, concat_axis=0, tiled=True)]
    ppermute x8, waiting for transfers between devices: 146 us -> 183 us  [shifted(): return lax.ppermute(value, axis, pairs)]
    pallas_call x1, Pallas kernels: 37.3 us -> 12.2 us  [per_device(): call(depth_kernel, 'depth', (block // ROWS,), [SMEM, table_spec, rows_spe...]
    ppermute x8, starting transfers between devices: 30.4 us -> 50 us  [shifted(): return lax.ppermute(value, axis, pairs)]
    pallas_call x1, Pallas kernels: 19.8 us -> 4.18 us  [per_device(): call(functools.partial(offset_kernel, factor), 'offset', (half // ROWS,),...]
    pallas_call x1, Pallas kernels: 19.8 us -> 7.24 us  [per_device(): call(functools.partial(low_kernel, factor), 'low', (half // ROWS,), [SMEM...]
    pallas_call x1, Pallas kernels: 17.9 us -> 6.45 us  [per_device(): call(high_kernel, 'high', (half // ROWS,), [SMEM, table_spec, eigen_spec,...]
    all_to_all x1 -> x2, waiting for transfers between devices: 0.01 us -> 8.8 us  [exchange(): return lax.all_to_all(value, 'gx', split_axis=0, concat_axis=0, tiled=True)]
  transfers between devices with their start and end apart: 9 -> 10, of which waited for: 8 -> 8; matrix products, arithmetic and copies ran while one was open for 2% -> 3% of each run, Pallas kernels for 6% -> 9%
where the time goes in v2:
time: 546 us; the launch traced here: 545 us
  waiting for transfers between devices  192 us (35%)
  blocking collectives  177 us (32%)
  Pallas kernels  101 us (18%)
  starting transfers between devices  59.5 us (11%)
  other arithmetic  12.6 us (2%)
    ppermute x8, waiting for transfers between devices, shifted(): return lax.ppermute(value, axis, pairs)  183 us
    all_to_all x2, blocking collectives, exchange(): return lax.all_to_all(value, 'gx', split_axis=0, concat_axis=0, tiled=True)  177 us
    ppermute x8, starting transfers between devices, shifted(): return lax.ppermute(value, axis, pairs)  50 us
    pallas_call x1, Pallas kernels, per_device(): call(functools.partial(node_kernel, planes, block), 'nodes', (steps,), [p...  39 us
    pallas_call x1, Pallas kernels, per_device(): call(functools.partial(start_kernel, planes), 'start', (steps,), [pl.Bloc...  32.2 us
    pallas_call x1, Pallas kernels, per_device(): call(depth_kernel, 'depth', (block // ROWS,), [SMEM, table_spec, rows_spe...  12.2 us
  transfers between devices with their start and end apart: 10, of which 8 were waited for; matrix products, arithmetic and copies ran while one was open for 3% of the time, Pallas kernels for 9%

profile of v2, /device:TPU:1, one launch (start us, length us, event | category | flops | bytes accessed | tf_op | source)
XLA Modules:
  0.0 545.4 jit_solution(1729060741541203483)
XLA Ops:
  0.6 4.5 collective-permute-start
  5.2 90.7 %collective-permute-done.previous_ref = f32[256,32,256]{2,1,0:T(8,128)} collective-permute-done((f32[256,32,256]{2,1,0:T(8,128)}, f32[256,32,256]{2,1,0:T(8,128)}, u32[]{:S(2)}, u32[]{:S(2)}) %collective-permute-start) | collective-permute-done | bytes 8388640 | tf_op jit(solution)/shard_map/ppermute | solution.py:243
  95.9 12.2 %depth.1 = f32[256,32,256]{2,1,0:T(8,128)} custom-call(s32[1]{0:T(128)} %bitcast.first_ref, bf16[256,768]{1,0:T(8,128)(2,1)} %constant.88.clone.table_ref, f32[256,32,256]{2,1,0:T(8,128)} %initial_ref.1, f32[256,32,256]{2,1,0:T(8,128)} %collective-permute-done.previous_ref), custom_call_target="tpu_custom_call" | custom-call | flops 3221225472 | bytes 25165824 | tf_op jit(solution)/shard_map/depth/pallas_call | solution.py:295
  108.1 110.9 %all_to_all.20 = f32[256,32,256]{2,1,0:T(8,128)} all-to-all(f32[256,32,256]{2,1,0:T(8,128)} %depth.1), channel_id=1, replica_groups=mesh['tm'=4,'gx'=8] {'gx'}, dimensions={0} | all-to-all | bytes 16777216 | tf_op jit(solution)/shard_map/all_to_all | solution.py:247
  219.0 32.2 %start.1 = (f32[8,32,16,256]{3,2,1,0:T(8,128)}, f32[8,32,16,256]{3,2,1,0:T(8,128)}, f32[2,32,256,256]{3,2,1,0:T(8,128)}, f32[2,256,256]{2,1,0:T(8,128)}, f32[2,256,256]{2,1,0:T(8,128)}) custom-call(f32[8,32,32,256]{3,2,1,0:T(8,128)} %bitcast.9, bf16[768,256]{1,0:T(8,128)(2,1)} %constant.89.clone.sx_ref, bf16[256,768]{1,0:T(8,128)(2,1)} %constant.90.clone.sy_ref, ...), custom_call_target="tpu_custom_call" | custom-call | flops 12884901888 | bytes 33554432 | tf_op jit(solution)/shard_map/start/pallas_call | solution.py:312
  251.2 4.7 all-to-all-start.1
  255.9 1.3 collective-permute-start.1
  257.2 4.0 collective-permute-start.2
  261.2 30.9 %collective-permute-done.1 = f32[2,256,256]{2,1,0:T(8,128)} collective-permute-done((f32[2,256,256]{2,1,0:T(8,128)S(1)}, f32[2,256,256]{2,1,0:T(8,128)}, u32[]{:S(2)}, u32[]{:S(2)}) %collective-permute-start.1) | collective-permute-done | bytes 524320 | tf_op jit(solution)/shard_map/ppermute | solution.py:243
  292.2 1.2 multiply_add_fusion.1
  293.4 1.3 collective-permute-start.4
  294.7 20.9 %collective-permute-done.4 = f32[2,256,256]{2,1,0:T(8,128)} collective-permute-done((f32[2,256,256]{2,1,0:T(8,128)S(1)}, f32[2,256,256]{2,1,0:T(8,128)}, u32[]{:S(2)}, u32[]{:S(2)}) %collective-permute-start.4) | collective-permute-done | bytes 524320 | tf_op jit(solution)/shard_map/ppermute | solution.py:243
  315.6 2.0 multiply_select_fusion
  317.6 13.3 %collective-permute-start.3 = (f32[2,256,256]{2,1,0:T(8,128)S(1)}, f32[2,256,256]{2,1,0:T(8,128)S(1)}, u32[]{:S(2)}, u32[]{:S(2)}) collective-permute-start(f32[2,256,256]{2,1,0:T(8,128)S(1)} %get-tuple-element.35), channel_id=1, source_target_pairs={{0,1},{1,2},{2,3},{3,4},{4,5},{5,6},{6,7},{8,9},{9,10},{10,11},{11... | collective-permute-start | bytes 1572872 | tf_op jit(solution)/shard_map/ppermute | solution.py:243
  330.9 6.1 %collective-permute-done.3 = f32[2,256,256]{2,1,0:T(8,128)S(1)} collective-permute-done((f32[2,256,256]{2,1,0:T(8,128)S(1)}, f32[2,256,256]{2,1,0:T(8,128)S(1)}, u32[]{:S(2)}, u32[]{:S(2)}) %collective-permute-start.3) | collective-permute-done | bytes 524320 | tf_op jit(solution)/shard_map/ppermute | solution.py:243
  337.9 39.0 %nodes.1 = f32[8,32,16,128]{3,2,1,0:T(8,128)} custom-call(f32[8,32,32,256]{3,2,1,0:T(8,128)} %bitcast.10, f32[8,32,16,256]{3,2,1,0:T(8,128)} %get-tuple-element.24.low_ref, f32[8,32,16,256]{3,2,1,0:T(8,128)} %get-tuple-element.29.high_ref, f32[2,32,256,256]{3,2,1,0:T(8,128)} %get-tuple-element.26.v_ref, f32[2,256,256]{2,1,0:T(8,128)} %multiply_select_fusion.1.from_left_ref, ...), custom_call_target="tpu_custom_call" | custom-call | flops 15032385536 | bytes 35651584 | tf_op jit(solution)/shard_map/nodes/pallas_call | solution.py:352
  376.9 66.2 %all_to_all.21.cubic_ref = f32[256,16,128]{2,1,0:T(8,128)} all-to-all(f32[256,16,128]{2,1,0:T(8,128)} %bitcast.14), channel_id=1, replica_groups=mesh['tm'=4,'gx'=8] {'gx'}, dimensions={0} | all-to-all | bytes 4194304 | tf_op jit(solution)/shard_map/all_to_all | solution.py:247
  443.1 4.8 all-to-all-start.2
  449.2 2.7 slice_select_fusion.start_ref
  451.9 7.2 %low.1 = (f32[256,32,256]{2,1,0:T(8,128)}, f32[128,16,128]{2,1,0:T(8,128)}) custom-call(f32[32]{0:T(128)} %dynamic_slice.6.fine_ref, f32[16]{0:T(128)} %dynamic_slice.7.coarse_ref, bf16[256,768]{1,0:T(8,128)(2,1)} %constant.88.clone.table_ref, f32[256,256]{1,0:T(8,128)} %constant.99.clone.eigen_ref, f32[128,128]{1,0:T(8,128)} %constant.100.clone.coarse_eigen_ref, ...), custom_call_target="tpu_custom_call" | custom-call | flops 1610612736 | bytes 10485760 | tf_op jit(solution)/shard_map/low/pallas_call | solution.py:385
  459.1 4.2 offset.1
  463.3 16.9 %collective-permute-start.5 = (f32[128,16,128]{2,1,0:T(8,128)}, f32[128,16,128]{2,1,0:T(8,128)S(1)}, u32[]{:S(2)}, u32[]{:S(2)}) collective-permute-start(f32[128,16,128]{2,1,0:T(8,128)} %offset.1), channel_id=1, source_target_pairs={{0,8},{8,16},{16,24},{1,9},{9,17},{17,25},{2,10},{10,18},{18,26},{... | collective-permute-start | bytes 3145736 | tf_op jit(solution)/shard_map/ppermute | solution.py:243
  480.1 12.0 %collective-permute-done.5 = f32[128,16,128]{2,1,0:T(8,128)S(1)} collective-permute-done((f32[128,16,128]{2,1,0:T(8,128)}, f32[128,16,128]{2,1,0:T(8,128)S(1)}, u32[]{:S(2)}, u32[]{:S(2)}) %collective-permute-start.5) | collective-permute-done | bytes 1048608 | tf_op jit(solution)/shard_map/ppermute | solution.py:243
  492.2 1.5 add_select_fusion.2
  493.7 4.3 collective-permute-start.6
  498.0 11.7 %collective-permute-done.6 = f32[128,16,128]{2,1,0:T(8,128)S(1)} collective-permute-done((f32[128,16,128]{2,1,0:T(8,128)S(1)}, f32[128,16,128]{2,1,0:T(8,128)S(1)}, u32[]{:S(2)}, u32[]{:S(2)}) %collective-permute-start.6) | collective-permute-done | bytes 1048608 | tf_op jit(solution)/shard_map/ppermute | solution.py:243
  509.7 1.5 add_select_fusion.1
  511.2 4.4 collective-permute-start.7
  516.2 11.1 %collective-permute-done.7 = f32[128,16,128]{2,1,0:T(8,128)S(1)} collective-permute-done((f32[128,16,128]{2,1,0:T(8,128)S(1)}, f32[128,16,128]{2,1,0:T(8,128)S(1)}, u32[]{:S(2)}, u32[]{:S(2)}) %collective-permute-start.7) | collective-permute-done | bytes 1048608 | tf_op jit(solution)/shard_map/ppermute | solution.py:243
  527.3 2.8 fusion
  530.1 8.8 %all-to-all-done.2.source_ref = f32[256,16,256]{2,1,0:T(8,128)} async-done(((f32[256,16,256]{2,1,0:T(8,128)}), f32[256,16,256]{2,1,0:T(8,128)}, u32[]{:S(2)}, u32[]{:S(2)}) %all-to-all-start.2) | async-done | bytes 4194336 | tf_op jit(solution)/shard_map/all_to_all | solution.py:247
  538.9 6.4 %high.1 = f32[256,32,256]{2,1,0:T(8,128)} custom-call(f32[16]{0:T(128)} %slice.37.fine_ref, bf16[256,768]{1,0:T(8,128)(2,1)} %constant.88.clone.table_ref, f32[256,256]{1,0:T(8,128)} %constant.99.clone.eigen_ref, f32[256,16,256]{2,1,0:T(8,128)} %all-to-all-done.2.source_ref, f32[256,32,256]{2,1,0:T(8,128)} %get-tuple-element.37._), custom_call_target="tpu_custom_call", output_to_operand_aliasing={{}: (4, {})} | custom-call | flops 1610612736 | bytes 10485760 | tf_op jit(solution)/shard_map/high/pallas_call | solution.py:419
  (24 shorter events, 2.7 us)
Async XLA Ops:
  0.6 95.2 %collective-permute-start = (f32[256,32,256]{2,1,0:T(8,128)}, f32[256,32,256]{2,1,0:T(8,128)}, u32[]{:S(2)}, u32[]{:S(2)}) collective-permute-start(f32[256,32,256]{2,1,0:T(8,128)} %bitcast.15), channel_id=1, source_target_pairs={{0,8},{8,16},{16,24},{1,9},{9,17},{17,25},{2,10},{10,18},{18,26},{... | collective-permute-start | bytes 25165832 | tf_op jit(solution)/shard_map/ppermute | solution.py:243
  251.1 4.7 copy-start.3
  251.1 6.1 %copy-start.2 = (f32[2,256,256]{2,1,0:T(8,128)S(1)}, f32[2,256,256]{2,1,0:T(8,128)}, u32[]{:S(2)}) copy-start(f32[2,256,256]{2,1,0:T(8,128)} %get-tuple-element.28) | copy-start | bytes 1572868
  251.1 41.0 %copy-start = (f32[2,256,256]{2,1,0:T(8,128)S(1)}, f32[2,256,256]{2,1,0:T(8,128)}, u32[]{:S(2)}) copy-start(f32[2,256,256]{2,1,0:T(8,128)} %constant.94.clone) | copy-start | bytes 1572868
  251.2 41.0 %copy-start.1 = (f32[2,256,256]{2,1,0:T(8,128)S(1)}, f32[2,256,256]{2,1,0:T(8,128)}, u32[]{:S(2)}) copy-start(f32[2,256,256]{2,1,0:T(8,128)} %constant.93.clone) | copy-start | bytes 1572868
  251.2 125.7 %all-to-all-start.1 = ((f32[256,16,256]{2,1,0:T(8,128)}), f32[256,16,256]{2,1,0:T(8,128)}, u32[]{:S(2)}, u32[]{:S(2)}) async-start(f32[256,16,256]{2,1,0:T(8,128)} %bitcast.13), calls=%async_computation.1 | async-start | bytes 8388608 | tf_op jit(solution)/shard_map/all_to_all | solution.py:247
  255.9 36.3 %collective-permute-start.1 = (f32[2,256,256]{2,1,0:T(8,128)S(1)}, f32[2,256,256]{2,1,0:T(8,128)}, u32[]{:S(2)}, u32[]{:S(2)}) collective-permute-start(f32[2,256,256]{2,1,0:T(8,128)S(1)} %copy-done.3), channel_id=1, source_target_pairs={{1,0},{2,1},{3,2},{4,3},{5,4},{6,5},{7,6},{9,8},{10,9},{11,10},{12... | collective-permute-start | bytes 1572872 | tf_op jit(solution)/shard_map/ppermute | solution.py:243
  257.2 37.5 %collective-permute-start.2 = (f32[2,256,256]{2,1,0:T(8,128)S(1)}, f32[2,256,256]{2,1,0:T(8,128)S(1)}, u32[]{:S(2)}, u32[]{:S(2)}) collective-permute-start(f32[2,256,256]{2,1,0:T(8,128)S(1)} %copy-done.2), channel_id=1, source_target_pairs={{0,1},{1,2},{2,3},{3,4},{4,5},{5,6},{6,7},{8,9},{9,10},{10,11},{11... | collective-permute-start | bytes 1572872 | tf_op jit(solution)/shard_map/ppermute | solution.py:243
  293.4 22.2 %collective-permute-start.4 = (f32[2,256,256]{2,1,0:T(8,128)S(1)}, f32[2,256,256]{2,1,0:T(8,128)}, u32[]{:S(2)}, u32[]{:S(2)}) collective-permute-start(f32[2,256,256]{2,1,0:T(8,128)S(1)} %multiply_add_fusion.1), channel_id=1, source_target_pairs={{1,0},{2,1},{3,2},{4,3},{5,4},{6,5},{7,6},{9,8},{10,9},{11,10},{12... | collective-permute-start | bytes 1572872 | tf_op jit(solution)/shard_map/ppermute | solution.py:243
  317.6 19.4 %collective-permute-start.3 = (f32[2,256,256]{2,1,0:T(8,128)S(1)}, f32[2,256,256]{2,1,0:T(8,128)S(1)}, u32[]{:S(2)}, u32[]{:S(2)}) collective-permute-start(f32[2,256,256]{2,1,0:T(8,128)S(1)} %get-tuple-element.35), channel_id=1, source_target_pairs={{0,1},{1,2},{2,3},{3,4},{4,5},{5,6},{6,7},{8,9},{9,10},{10,11},{11... | collective-permute-start | bytes 1572872 | tf_op jit(solution)/shard_map/ppermute | solution.py:243
  376.9 71.1 %copy-start.8 = (f32[128]{0:T(128)S(1)}, f32[128]{0:T(128)}, u32[]{:S(2)}) copy-start(f32[128]{0:T(128)} %constant.87.clone) | copy-start | bytes 1540
  376.9 71.7 %copy-start.7 = (f32[256]{0:T(256)S(1)}, f32[256]{0:T(256)}, u32[]{:S(2)}) copy-start(f32[256]{0:T(256)} %constant.86.clone) | copy-start | bytes 3076
  443.1 95.8 %all-to-all-start.2 = ((f32[256,16,256]{2,1,0:T(8,128)}), f32[256,16,256]{2,1,0:T(8,128)}, u32[]{:S(2)}, u32[]{:S(2)}) async-start(f32[256,16,256]{2,1,0:T(8,128)} %bitcast.12), calls=%async_computation.2 | async-start | bytes 8388608 | tf_op jit(solution)/shard_map/all_to_all | solution.py:247
  448.0 44.2 %copy-start.4 = (f32[128,128]{1,0:T(8,128)S(1)}, f32[128,128]{1,0:T(8,128)}, u32[]{:S(2)}) copy-start(f32[128,128]{1,0:T(8,128)} %constant.104) | copy-start | bytes 196612
  448.6 43.6 %copy-start.5 = (f32[16]{0:T(128)S(1)}, f32[16]{0:T(128)}, u32[]{:S(2)}) copy-start(f32[16]{0:T(128)} %dynamic_slice.7.coarse_ref) | copy-start | bytes 196
  451.9 63.7 %copy-start.6 = (f32[32]{0:T(128)S(1)}, f32[32]{0:T(128)}, u32[]{:S(2)}) copy-start(f32[32]{0:T(128)} %dynamic_slice.6.fine_ref) | copy-start | bytes 388
  463.3 28.9 %collective-permute-start.5 = (f32[128,16,128]{2,1,0:T(8,128)}, f32[128,16,128]{2,1,0:T(8,128)S(1)}, u32[]{:S(2)}, u32[]{:S(2)}) collective-permute-start(f32[128,16,128]{2,1,0:T(8,128)} %offset.1), channel_id=1, source_target_pairs={{0,8},{8,16},{16,24},{1,9},{9,17},{17,25},{2,10},{10,18},{18,26},{... | collective-permute-start | bytes 3145736 | tf_op jit(solution)/shard_map/ppermute | solution.py:243
  493.7 16.0 %collective-permute-start.6 = (f32[128,16,128]{2,1,0:T(8,128)S(1)}, f32[128,16,128]{2,1,0:T(8,128)S(1)}, u32[]{:S(2)}, u32[]{:S(2)}) collective-permute-start(f32[128,16,128]{2,1,0:T(8,128)S(1)} %add_select_fusion.2), channel_id=1, source_target_pairs={{0,8},{8,16},{16,24},{1,9},{9,17},{17,25},{2,10},{10,18},{18,26},{... | collective-permute-start | bytes 3145736 | tf_op jit(solution)/shard_map/ppermute | solution.py:243
  511.2 16.1 %collective-permute-start.7 = (f32[128,16,128]{2,1,0:T(8,128)S(1)}, f32[128,16,128]{2,1,0:T(8,128)S(1)}, u32[]{:S(2)}, u32[]{:S(2)}) collective-permute-start(f32[128,16,128]{2,1,0:T(8,128)S(1)} %add_select_fusion.1), channel_id=1, source_target_pairs={{0,8},{8,16},{16,24},{1,9},{9,17},{17,25},{2,10},{10,18},{18,26},{... | collective-permute-start | bytes 3145736 | tf_op jit(solution)/shard_map/ppermute | solution.py:243

commit v3 on v2

v3 whole, which is shorter than its diff:
```python
import functools
import math

import jax
import jax.numpy as jnp
import ml_dtypes
import numpy as np
from jax import lax
from jax.experimental import pallas as pl
from jax.experimental.pallas import tpu as pltpu
from jax.sharding import PartitionSpec as P

DIFFUSION = 0.25
BF16 = jnp.bfloat16
F32 = jnp.float32
ROWS = 8
VMEM_BYTES = 56 * 1024 * 1024


def sine_matrix(length):
    index = np.arange(1, length + 1)
    phase = np.outer(index, index) % (2 * (length + 1))
    return np.sin(phase * (math.pi / (length + 1))) * math.sqrt(2.0 / (length + 1))


def omega(count):
    return 2.0 - 2.0 * np.cos((np.arange(count) + 1.0) * (math.pi / (count + 1)))


def fine_order(grid, groups):
    block, coarse = grid // groups, grid // 2
    half = block // 2
    position = np.arange(grid)
    within, group = position % block, position // block
    return np.where(within < half, group * half + within, coarse + group * half + within - half)


def halves(table):
    high = table.astype(ml_dtypes.bfloat16)
    low = (table - high.astype(np.float64)).astype(ml_dtypes.bfloat16)
    return high, low


def left_table(table):
    high, low = halves(table)
    return np.concatenate([high, high, low], axis=1)


def right_table(table):
    high, low = halves(table)
    return np.concatenate([high, high, low], axis=0)


def split3(value, axis):
    high = value.astype(BF16)
    low = (value - high.astype(F32)).astype(BF16)
    return jnp.concatenate([high, low, high], axis=axis)


def left(table, value):
    return jnp.dot(table, split3(value, 0), preferred_element_type=F32)


def right(value, table):
    return jnp.dot(split3(value, 1), table, preferred_element_type=F32)


def cube(value):
    return value * value * value


def whole_block(shape):
    return pl.BlockSpec(shape, lambda *_: (0,) * len(shape))


SMEM = pl.BlockSpec(memory_space=pltpu.SMEM)


def call(kernel, name, grid, in_specs, out_specs, out_shape, scratch=(), flops=0, moved=0, aliases=None):
    return pl.pallas_call(
        kernel,
        grid=grid,
        in_specs=in_specs,
        out_specs=out_specs,
        out_shape=out_shape,
        scratch_shapes=list(scratch),
        input_output_aliases=aliases or {},
        compiler_params=pltpu.CompilerParams(vmem_limit_bytes=VMEM_BYTES),
        cost_estimate=pl.CostEstimate(flops=flops, bytes_accessed=moved, transcendentals=0),
        name=name,
    )


def depth_kernel(last_ref, table_ref, initial_ref, end_ref, *out_refs):
    value = jnp.swapaxes(jnp.where(last_ref[0] == 1, initial_ref[...], end_ref[0]), 0, 1)
    rows = jnp.stack([left(table_ref[...], value[row]) for row in range(ROWS)])
    groups, _, _, wide = out_refs[0].shape
    rows = jnp.swapaxes(rows, 0, 1).reshape(groups, -1, ROWS, wide)
    begin = 0
    for out_ref in out_refs:
        planes = out_ref.shape[1]
        out_ref[...] = rows[:, begin:begin + planes]
        begin += planes


def start_kernel(planes, modes_ref, sx_ref, sy_ref, syt_ref, rho_ref, power_ref, right_ref, left_ref, *refs):
    corner_ref, side_ref, high_ref, v_ref, power, to_right_ref, to_left_ref, cubic = refs[-8:]

    @pl.when(pl.program_id(0) == 0)
    def _():
        power[...] = power_ref[...]
        to_right_ref[...] = right_ref[...]
        to_left_ref[...] = left_ref[...]

    groups, _, block, wide = modes_ref.shape
    grid = groups * block
    half = block // 2
    modes = [modes_ref[:, j].reshape(grid, wide) for j in range(planes)]
    along_x = right(jnp.concatenate(modes, axis=0), sx_ref[...])
    terms = [cube(left(sy_ref[...], along_x[j * grid:(j + 1) * grid])) for j in range(planes)]
    along_x = right(jnp.concatenate(terms, axis=0), sx_ref[...])
    for j in range(planes):
        cubic[j] = left(syt_ref[...], along_x[j * grid:(j + 1) * grid])
    for strip in range(2 * groups):
        group, upper = strip // 2, strip % 2
        rows = slice(strip * half, (strip + 1) * half)
        within = slice(upper * half, (upper + 1) * half)
        rho = [rho_ref[node, rows] for node in range(2)]
        carried = [to_left_ref[node, rows] for node in range(2)]
        weight = [power[node, rows] for node in range(2)]
        total = [to_right_ref[node, rows] for node in range(2)]
        for j in reversed(range(planes)):
            mode = modes_ref[group, j, within]
            source = 2.0 * mode - cubic[j, rows]
            if upper:
                high_ref[group, j] = source
            else:
                corner_ref[group, j] = source[:, :wide // 2]
                side_ref[group, j] = source[:, wide // 2:]
            for node, value in enumerate((source, 0.5 * (mode + source))):
                carried[node] = value + rho[node] * carried[node]
                v_ref[node, j, rows] = carried[node]
                v_ref[2 + node, j, rows] = value
                total[node] += weight[node] * value
                weight[node] = weight[node] * rho[node]
        for node in range(2):
            to_left_ref[node, rows] = carried[node]
            power[node, rows] = weight[node]
            to_right_ref[node, rows] = total[node]


def node_kernel(planes, slab, v_ref, from_left_ref, from_right_ref, rho_ref, inverse_ref, kappa_ref,
                sx_ref, sy_ref, sxl_ref, syl_ref, out_ref, left_sum, right_sum, nodes):
    step = pl.program_id(0)
    plane = step * planes

    @pl.when(step == 0)
    def _():
        left_sum[...] = from_left_ref[...]

    @pl.when(plane % ROWS == 0)
    def _():
        rho = rho_ref[...]
        twice = rho * rho
        four = twice * twice
        eight = four * four
        right_sum[...] = lax.fori_loop(
            0, slab // ROWS - plane // ROWS, lambda _, total: total * eight, from_right_ref[...]
        )

    groups, _, half, low = out_ref.shape
    grid = v_ref.shape[2]
    wide = v_ref.shape[3]
    for strip in range(2 * groups):
        rows = slice(strip * half, (strip + 1) * half)
        rho = [rho_ref[node, rows] for node in range(2)]
        inverse = [inverse_ref[node, rows] for node in range(2)]
        kappa = [kappa_ref[node, rows] for node in range(2)]
        before = [left_sum[node, rows] for node in range(2)]
        after = [right_sum[node, rows] for node in range(2)]
        for j in range(planes):
            for node in range(2):
                behind = rho[node] * before[node]
                before[node] = v_ref[2 + node, j, rows] + behind
                nodes[node, j, rows] = kappa[node] * (behind + v_ref[node, j, rows] + after[node])
                after[node] = after[node] * inverse[node]
        for node in range(2):
            left_sum[node, rows] = before[node]
            right_sum[node, rows] = after[node]
    along_x = right(nodes[...].reshape(2 * planes * grid, wide), sx_ref[...])
    fields = [left(sy_ref[...], along_x[j * grid:(j + 1) * grid]) for j in range(2 * planes)]
    terms = [cube(fields[j]) + 4.0 * cube(fields[planes + j]) for j in range(planes)]
    along_x = right(jnp.concatenate(terms, axis=0), sxl_ref[...])
    for j in range(planes):
        term = left(syl_ref[...], along_x[j * grid:(j + 1) * grid])
        out_ref[:, j] = term.reshape(groups, half, low)


def joined(refs):
    parts = [ref[...] for ref in refs]
    parts = jnp.concatenate(parts, axis=1)
    return parts.reshape(parts.shape[0] * parts.shape[1], *parts.shape[2:])


def low_kernel(factor, fine_ref, coarse_ref, table_ref, eigen_ref, coarse_eigen_ref, corner_ref, start_ref,
               out_ref, gathered_ref):
    base = pl.program_id(0) * ROWS
    coarse = start_ref.shape[0]
    sources = jnp.swapaxes(corner_ref[...], 0, 1)
    starts = jnp.swapaxes(start_ref[...], 0, 1)
    ends, gathered = [], []
    for row in range(ROWS):
        source = left(table_ref[...], sources[row])
        eigen = eigen_ref[...] + fine_ref[base + row]
        node_end = source / (1.0 + eigen)
        ends.append(node_end)
        source, node_end, eigen = source[:coarse], node_end[:coarse], eigen[:coarse]
        start = starts[row]
        node_mid = 0.5 * (start + source) / (1.0 + 0.5 * eigen)
        rate = source - (1.0 + eigen) * start + (1.0 - eigen) * (4.0 * node_mid + node_end)
        coarse_eigen = coarse_eigen_ref[...] + coarse_ref[base + row]
        gathered.append(factor * (rate / 6.0 + coarse_eigen * node_end))
    out_ref[...] = jnp.swapaxes(jnp.stack(ends), 0, 1)
    gathered_ref[...] = jnp.swapaxes(jnp.stack(gathered), 0, 1)


def offset_kernel(factor, first_ref, coarse_ref, table_ref, coarse_eigen_ref, gathered_ref, start_ref, cubic_ref,
                  out_ref):
    base = pl.program_id(0) * ROWS
    first = first_ref[0] == 1
    cubics = jnp.swapaxes(cubic_ref[...], 0, 1)
    given = jnp.swapaxes(gathered_ref[...] + jnp.where(first, factor * start_ref[...], 0.0), 0, 1)
    rows = []
    for row in range(ROWS):
        total = given[row] - (factor / 6.0) * left(table_ref[...], cubics[row])
        rows.append(total / (1.0 + coarse_eigen_ref[...] + coarse_ref[base + row]))
    out_ref[...] = jnp.swapaxes(jnp.stack(rows), 0, 1)


def finish_kernel(fine_ref, table_ref, eigen_ref, *refs):
    base = pl.program_id(0) * ROWS
    out_ref = refs[-1]
    sources = jnp.swapaxes(joined(refs[:-2]), 0, 1)
    rows = []
    for row in range(ROWS):
        source = left(table_ref[...], sources[row])
        rows.append(source / (1.0 + eigen_ref[...] + fine_ref[base + row]))
    out_ref[...] = jnp.swapaxes(jnp.stack(rows), 0, 1)


def shifted(value, axis, by):
    length = lax.axis_size(axis)
    pairs = [(i, i + by) for i in range(length) if 0 <= i + by < length]
    return lax.ppermute(value, axis, pairs)


def turned(value, axis):
    length = lax.axis_size(axis)
    return lax.ppermute(value, axis, [(i, (i + 1) % length) for i in range(length)])


def exchange(value):
    return lax.all_to_all(value, "gx", split_axis=0, concat_axis=0, tiled=True)


def after(value, *earlier):
    return lax.optimization_barrier((value, *earlier))


def per_device(end_modes, initial_modes):
    grid = initial_modes.shape[0]
    coarse = grid // 2
    groups = lax.axis_size("gx")
    block = grid // groups
    half = block // 2
    planes = 4
    slice_index = lax.axis_index("tm")
    group_index = lax.axis_index("gx")
    is_first = slice_index == 0
    slices = lax.axis_size("tm")
    first = is_first.astype(jnp.int32)[None]
    last = (slice_index == slices - 1).astype(jnp.int32)[None]
    order = fine_order(grid, groups)
    sine = sine_matrix(grid)
    fine_w, coarse_w = omega(grid), omega(coarse)
    factor = ((coarse + 1) / (grid + 1)) ** 1.5
    unit = grid * block * grid

    flat = fine_w[order][:, None] + fine_w[None, :]
    scale = np.array([1.0, 0.5])[:, None, None] * DIFFUSION
    diagonal = 1.0 / scale + 2.0 + flat[None]
    rho = 2.0 / (diagonal + np.sqrt(diagonal * diagonal - 4.0))
    inverse = 1.0 / rho
    kappa = 1.0 / (scale * (inverse - rho))
    rho, inverse, kappa = (t.astype(np.float32) for t in (rho, inverse, kappa))
    rho_slab = (rho.astype(np.float64) ** block).astype(np.float32)
    rounds = 1
    while np.float32(float(rho.max()) ** (block * rounds)) > 0:
        rounds += 1

    depth_table = left_table(sine)
    x_table = right_table(sine)
    y_table = left_table(sine[:, order])
    back_table = left_table(sine[order, :])
    x_low_table = right_table(sine[:, :coarse])
    low_table = left_table(sine[:coarse, :])
    eigen = (DIFFUSION * (fine_w[:, None] + fine_w[None, :])).astype(np.float32)
    coarse_eigen = (0.25 * DIFFUSION * (coarse_w[:, None] + coarse_w[None, :])).astype(np.float32)
    fine_own = lax.dynamic_slice(jnp.asarray((DIFFUSION * fine_w[order]).astype(np.float32)), (group_index * block,), (block,))
    coarse_own = lax.dynamic_slice(
        jnp.asarray((0.25 * DIFFUSION * coarse_w).astype(np.float32)), (group_index * half,), (half,)
    )

    rows_spec = pl.BlockSpec((grid, ROWS, grid), lambda i: (0, i, 0))
    table_spec = whole_block(depth_table.shape)
    quarter = block // 4
    middle = 3 * quarter // planes // 2 * planes
    lengths = (quarter, middle, block - quarter - middle)
    begins = (0, quarter, quarter + middle)
    parts = len(lengths)
    outgoing = call(
        depth_kernel,
        "depth",
        (block // ROWS,),
        [SMEM, table_spec, rows_spec, pl.BlockSpec((1, grid, ROWS, grid), lambda i: (0, 0, i, 0))],
        [pl.BlockSpec((groups, length, ROWS, grid), lambda i: (0, 0, i, 0)) for length in lengths],
        [jax.ShapeDtypeStruct((groups, length, block, grid), F32) for length in lengths],
        flops=6 * unit * grid,
        moved=12 * unit,
    )(last, depth_table, initial_modes, end_modes)

    pair = (2, grid, grid)
    pair_spec = whole_block(pair)
    whole = (groups, block, half)
    shapes = [
        (*whole, coarse),
        (*whole, coarse),
        (groups, block - lengths[0], half, grid),
        (4, block, grid, grid),
    ]
    arrays = None
    state = (np.ones(pair, np.float32), np.zeros(pair, np.float32), np.zeros(pair, np.float32))
    backs, states = {}, {}
    for part in reversed(range(parts)):
        given = outgoing[part]
        if part + 1 in backs:
            given, *_ = after(given, backs[part + 1], *states.get(part + 2, ()))
        backs[part] = exchange(given)
        modes = turned(backs[part], "tm")
        steps = lengths[part] // planes
        bases = [begins[part] // planes] * 4
        if part == 0:
            shapes[2] = (groups, lengths[0], half, grid)
        else:
            bases[2] = (begins[part] - lengths[0]) // planes
        specs = [
            pl.BlockSpec(
                (4, planes, grid, grid) if n == 3 else (groups, planes, half, shapes[n][3]),
                lambda i, base=base, steps=steps: (0, base + steps - 1 - i, 0, 0),
            )
            for n, base in enumerate(bases)
        ]
        held = [n for n in range(4) if arrays is not None and not (part == 0 and n == 2)]
        outs = call(
            functools.partial(start_kernel, planes),
            "start",
            (steps,),
            [
                pl.BlockSpec((groups, planes, block, grid), lambda i, steps=steps: (0, steps - 1 - i, 0, 0)),
                whole_block(x_table.shape),
                table_spec,
                table_spec,
                pair_spec,
                pair_spec,
                pair_spec,
                pair_spec,
            ] + [pl.BlockSpec(memory_space=pl.ANY)] * len(held),
            specs + [pair_spec] * 3,
            [jax.ShapeDtypeStruct(shape, F32) for shape in shapes] + [jax.ShapeDtypeStruct(pair, F32)] * 3,
            scratch=[pltpu.VMEM((planes, grid, grid), F32)],
            flops=24 * unit * grid * lengths[part] // block,
            moved=24 * unit * lengths[part] // block,
            aliases={8 + place: n for place, n in enumerate(held)},
        )(modes, x_table, y_table, back_table, rho, *state, *(arrays[n] for n in held))
        if part == 0:
            high_first = outs[2]
        else:
            high_rest = outs[2]
        arrays, state = outs[:4], outs[4:]
        states[part] = state
    corner, side, _, v = arrays
    _, to_right, to_left = state
    high_rest, backs[0] = after(high_rest, backs[0])
    high_rest_back = exchange(high_rest.reshape(-1, half, grid))
    at_start, at_end = group_index == 0, group_index == groups - 1
    if rounds <= 2:
        rightward = jnp.where(at_start, to_right - rho_slab * (rho * to_left), to_right)
        leftward = jnp.where(at_end, to_left - rho_slab * (rho * to_right), to_left)
        from_left = shifted(rightward, "gx", 1) + rho_slab * shifted(rightward, "gx", 2)
        from_right = shifted(leftward, "gx", -1) + rho_slab * shifted(leftward, "gx", -2)
        from_left, from_right = (
            jnp.where(at_start, -rho * (to_left + rho_slab * from_right), from_left),
            jnp.where(at_end, -rho * (to_right + rho_slab * from_left), from_right),
        )
    else:
        from_left = jnp.zeros(pair, F32)
        from_right = jnp.zeros(pair, F32)
        for _ in range(rounds):
            rightward = to_right + rho_slab * from_left
            leftward = to_left + rho_slab * from_right
            from_left = jnp.where(at_start, -rho * leftward, shifted(rightward, "gx", 1))
            from_right = jnp.where(at_end, -rho * rightward, shifted(leftward, "gx", -1))

    corner, high_rest_back, from_left, from_right = after(corner, high_rest_back, from_left, from_right)
    corner_back = exchange(corner.reshape(grid, half, coarse))
    cubic = call(
        functools.partial(node_kernel, planes, block),
        "nodes",
        (block // planes,),
        [pl.BlockSpec((4, planes, grid, grid), lambda i: (0, i, 0, 0))]
        + [pair_spec] * 5
        + [
            whole_block(x_table.shape),
            table_spec,
            whole_block(x_low_table.shape),
            whole_block(low_table.shape),
        ],
        pl.BlockSpec((groups, planes, half, coarse), lambda i: (0, i, 0, 0)),
        jax.ShapeDtypeStruct((groups, block, half, coarse), F32),
        scratch=[pltpu.VMEM(pair, F32), pltpu.VMEM(pair, F32), pltpu.VMEM((2, planes, grid, grid), F32)],
        flops=28 * unit * grid,
        moved=17 * unit,
    )(v, from_left, from_right, rho, inverse, kappa, x_table, y_table, x_low_table, low_table)
    cubic, corner_back = after(cubic, corner_back)
    cubic_back = exchange(cubic.reshape(grid, half, coarse))
    high_first, cubic_back = after(high_first, cubic_back)
    high_first_back = exchange(high_first.reshape(-1, half, grid))
    side, high_first_back = after(side, high_first_back)
    side_back = exchange(side.reshape(grid, half, coarse))
    high_backs = [part.reshape(groups, -1, half, grid) for part in (high_first_back, high_rest_back)]
    start_low = jnp.where(
        is_first, initial_modes[:coarse, :half, :coarse], shifted(end_modes[0, :coarse, :half, :coarse], "tm", 1)
    )

    low_spec = pl.BlockSpec((coarse, ROWS, coarse), lambda i: (0, i, 0))
    coarse_eigen_spec = whole_block(coarse_eigen.shape)
    quarter_spec = pl.BlockSpec((grid, ROWS, coarse), lambda i: (0, i, 0))
    corner_shape = jax.ShapeDtypeStruct((coarse, half, coarse), F32)
    result_shape = jax.ShapeDtypeStruct((grid, block, grid), F32)
    result, gathered = call(
        functools.partial(low_kernel, factor),
        "low",
        (half // ROWS,),
        [SMEM, SMEM, table_spec, whole_block((grid, coarse)), coarse_eigen_spec, quarter_spec, low_spec],
        [quarter_spec, low_spec],
        [result_shape, corner_shape],
        flops=2 * unit * grid,
        moved=3 * unit,
    )(fine_own, coarse_own, depth_table, eigen[:, :coarse], coarse_eigen, corner_back, start_low)
    offset = call(
        functools.partial(offset_kernel, factor),
        "offset",
        (half // ROWS,),
        [SMEM, SMEM, whole_block(low_table.shape), coarse_eigen_spec, low_spec, low_spec, quarter_spec],
        low_spec,
        corner_shape,
        flops=unit * grid,
        moved=2 * unit,
    )(first, coarse_own, low_table, coarse_eigen, gathered, start_low, cubic_back)

    def finish(result, sources, weights, eigen, row, column):
        width = eigen.shape[1]
        return call(
            finish_kernel,
            "finish",
            (half // ROWS,),
            [SMEM, table_spec, whole_block(eigen.shape)]
            + [pl.BlockSpec((groups, part.shape[1], ROWS, width), lambda i: (0, 0, i, 0)) for part in sources]
            + [pl.BlockSpec(memory_space=pl.ANY)],
            pl.BlockSpec((grid, ROWS, width), lambda i: (0, row // ROWS + i, column)),
            result_shape,
            flops=3 * unit * width,
            moved=5 * unit * width // grid,
            aliases={3 + len(sources): 0},
        )(weights, depth_table, eigen, *sources, result)

    result = finish(result, high_backs, fine_own[half:], eigen, half, 0)
    decay = 1.0 / (1.0 + coarse_eigen[:, None, :] + coarse_own[None, :, None])
    coarse_end = offset
    for turn in range(1, slices):
        incoming = lax.ppermute(coarse_end, "tm", [(turn - 1, turn)])
        coarse_end = jnp.where(slice_index == turn, decay * incoming + offset, coarse_end)
    result = result.at[:coarse, :half, :coarse].set(coarse_end / factor)
    result = finish(
        result, [side_back.reshape(groups, block, half, coarse)], fine_own[:half], eigen[:, coarse:], 0, 1
    )
    return (result[None], coarse_end[None])


def solution(mesh):
    return jax.shard_map(
        per_device,
        mesh=mesh,
        in_specs=(P("tm", None, "gx", None), P(None, "gx", None)),
        out_specs=(P("tm", None, "gx", None), P("tm", None, "gx", None)),
        check_vma=False,
    )
```

time: 546 us -> 517 us (0.947)
  blocking collectives: 177 us -> 76.3 us
  waiting for transfers between devices: 192 us -> 229 us
  Pallas kernels: 101 us -> 116 us
  starting transfers between devices: 59.5 us -> 70.2 us
  local copies, waits for them, and re-layouts: 1.84 us -> 10.3 us
    ppermute x8 -> x5, waiting for transfers between devices: 183 us -> 30.9 us  [shifted(): return lax.ppermute(value, axis, pairs)]
    ppermute x0 -> x6, waiting for transfers between devices: none -> 103 us  [the longest x3 92 us: turned(): lax.ppermute(value, axis, [(i, (i + 1) % length) for i in range(length)])]
    all_to_all x2 -> x1, blocking collectives: 177 us -> 76.3 us  [exchange(): return lax.all_to_all(value, 'gx', split_axis=0, concat_axis=0, tiled=True)]
    all_to_all x2 -> x7, waiting for transfers between devices: 8.8 us -> 94.6 us  [exchange(): return lax.all_to_all(value, 'gx', split_axis=0, concat_axis=0, tiled=True)]
    ppermute x8 -> x5, starting transfers between devices: 50 us -> 13.8 us  [shifted(): return lax.ppermute(value, axis, pairs)]
    all_to_all x2 -> x7, starting transfers between devices: 9.5 us -> 42.5 us  [exchange(): return lax.all_to_all(value, 'gx', split_axis=0, concat_axis=0, tiled=True)]
    ppermute x0 -> x6, starting transfers between devices: none -> 13.9 us  [the longest x3 7.98 us: turned(): lax.ppermute(value, axis, [(i, (i + 1) % length) for i in range(length)])]
    pallas_call x1 -> x3, Pallas kernels: 32.2 us -> 44.8 us  [per_device(): call(functools.partial(start_kernel, planes), 'start', (steps,), [pl.Bloc...]
  transfers between devices with their start and end apart: 10 -> 18, of which waited for: 8 -> 11; matrix products, arithmetic and copies ran while one was open for 3% -> 4% of each run, Pallas kernels for 9% -> 19%
where the time goes in v3:
time: 517 us; the launch traced here: 515 us
  waiting for transfers between devices  229 us (44%)
  Pallas kernels  116 us (22%)
  blocking collectives  76.3 us (15%)
  starting transfers between devices  70.2 us (14%)
  other arithmetic  12.4 us (2%)
  local copies, waits for them, and re-layouts  10.3 us (2%)
    all_to_all x7, waiting for transfers between devices, exchange(): return lax.all_to_all(value, 'gx', split_axis=0, concat_axis=0, tiled=True)  94.6 us
    ppermute x3, waiting for transfers between devices, turned(): lax.ppermute(value, axis, [(i, (i + 1) % length) for i in range(length)])  92 us
    all_to_all x1, blocking collectives, exchange(): return lax.all_to_all(value, 'gx', split_axis=0, concat_axis=0, tiled=True)  76.3 us
    pallas_call x3, Pallas kernels, per_device(): call(functools.partial(start_kernel, planes), 'start', (steps,), [pl.Bloc...  44.8 us
    all_to_all x7, starting transfers between devices, exchange(): return lax.all_to_all(value, 'gx', split_axis=0, concat_axis=0, tiled=True)  42.5 us
    pallas_call x1, Pallas kernels, per_device(): call(functools.partial(node_kernel, planes, block), 'nodes', (block // pl...  38.6 us
    ppermute x5, waiting for transfers between devices, shifted(): return lax.ppermute(value, axis, pairs)  30.9 us
    ppermute x5, starting transfers between devices, shifted(): return lax.ppermute(value, axis, pairs)  13.8 us
  transfers between devices with their start and end apart: 18, of which 11 were waited for; matrix products, arithmetic and copies ran while one was open for 4% of the time, Pallas kernels for 19%

profile of v3, /device:TPU:1, one launch (start us, length us, event | category | flops | bytes accessed | tf_op | source)
XLA Modules:
  0.0 514.8 jit_solution(2483560603281466337)
XLA Ops:
  0.6 12.3 %depth.1 = (f32[8,8,32,256]{3,2,1,0:T(8,128)}, f32[8,12,32,256]{3,2,1,0:T(8,128)}, f32[8,12,32,256]{3,2,1,0:T(8,128)}) custom-call(s32[1]{0:T(128)} %bitcast.last_ref, bf16[256,768]{1,0:T(8,128)(2,1)} %constant.100.clone.table_ref, f32[256,32,256]{2,1,0:T(8,128)} %initial_ref.1, f32[1,256,32,256]{3,2,1,0:T(8,128)} %end_ref.1), custom_call_target="tpu_custom_call" | custom-call | flops 3221225472 | bytes 25165824 | tf_op jit(solution)/shard_map/depth/pallas_call | solution.py:321
  12.9 76.3 %all_to_all.40 = f32[8,12,32,256]{3,2,1,0:T(8,128)} all-to-all(f32[8,12,32,256]{3,2,1,0:T(8,128)} %get-tuple-element.54), channel_id=1, replica_groups=mesh['tm'=4,'gx'=8] {'gx'}, dimensions={0} | all-to-all | bytes 6291456 | tf_op jit(solution)/shard_map/all_to_all | solution.py:263
  89.2 4.1 all-to-all-start.1
  95.8 34.5 %collective-permute-done.modes_ref = f32[8,12,32,256]{3,2,1,0:T(8,128)S(1)} collective-permute-done((f32[8,12,32,256]{3,2,1,0:T(8,128)}, f32[8,12,32,256]{3,2,1,0:T(8,128)S(1)}, u32[]{:S(2)}, u32[]{:S(2)}) %collective-permute-start) | collective-permute-done | bytes 3145760 | tf_op jit(solution)/shard_map/ppermute | solution.py:259
  132.5 16.4 %start.3 = (f32[8,32,16,128]{3,2,1,0:T(8,128)}, f32[8,32,16,128]{3,2,1,0:T(8,128)}, f32[8,24,16,256]{3,2,1,0:T(8,128)}, f32[4,32,256,256]{3,2,1,0:T(8,128)}, f32...) custom-call(f32[8,12,32,256]{3,2,1,0:T(8,128)} %copy-done.12, ...), custom_call_target="tpu_custom_call" | custom-call | flops 4831838208 | bytes 18874368 | tf_op jit(solution)/shard_map/start/pallas_call | solution.py:364
  148.8 14.0 %all-to-all-done.1 = f32[8,12,32,256]{3,2,1,0:T(8,128)S(1)} async-done(((f32[8,12,32,256]{3,2,1,0:T(8,128)}), f32[8,12,32,256]{3,2,1,0:T(8,128)S(1)}, u32[]{:S(2)}, u32[]{:S(2)}) %all-to-all-start.1) | async-done | bytes 3145760 | tf_op jit(solution)/shard_map/all_to_all | solution.py:263
  162.8 5.0 all-to-all-start.2
  170.5 34.2 %collective-permute-done.2.modes_ref = f32[8,12,32,256]{3,2,1,0:T(8,128)S(1)} collective-permute-done((f32[8,12,32,256]{3,2,1,0:T(8,128)S(1)}, f32[8,12,32,256]{3,2,1,0:T(8,128)S(1)}, u32[]{:S(2)}, u32[]{:S(2)}) %collective-permute-start.2) | collective-permute-done | bytes 3145760 | tf_op jit(solution)/shard_map/ppermute | solution.py:259
  206.4 16.0 %start.4 = (f32[8,32,16,128]{3,2,1,0:T(8,128)}, f32[8,32,16,128]{3,2,1,0:T(8,128)}, f32[8,24,16,256]{3,2,1,0:T(8,128)}, f32[4,32,256,256]{3,2,1,0:T(8,128)}, f32...) custom-call(f32[8,12,32,256]{3,2,1,0:T(8,128)} %copy-done.5, ...), custom_call_target="tpu_custom_call", output_to_operand_aliasing={{0}: (8, {}), {1}: (9, {}), {2}: (10, {}), {3}: (11, {})} | custom-call | flops 4831838208 | bytes 18874368 | tf_op jit(solution)/shard_map/start/pallas_call | solution.py:364
  222.4 5.6 %all-to-all-start.3 = ((f32[192,16,256]{2,1,0:T(8,128)}), f32[192,16,256]{2,1,0:T(8,128)S(1)}, u32[]{:S(2)}, u32[]{:S(2)}) async-start(f32[192,16,256]{2,1,0:T(8,128)} %bitcast.16), calls=%async_computation.3 | async-start | bytes 6291456 | tf_op jit(solution)/shard_map/all_to_all | solution.py:263
  230.7 23.3 %collective-permute-done.1.modes_ref = f32[8,8,32,256]{3,2,1,0:T(8,128)} collective-permute-done((f32[8,8,32,256]{3,2,1,0:T(8,128)}, f32[8,8,32,256]{3,2,1,0:T(8,128)}, u32[]{:S(2)}, u32[]{:S(2)}) %collective-permute-start.1) | collective-permute-done | bytes 2097184 | tf_op jit(solution)/shard_map/ppermute | solution.py:259
  254.0 12.4 %start.5 = (f32[8,32,16,128]{3,2,1,0:T(8,128)}, f32[8,32,16,128]{3,2,1,0:T(8,128)}, f32[8,8,16,256]{3,2,1,0:T(8,128)}, f32[4,32,256,256]{3,2,1,0:T(8,128)}, f32[...) custom-call(f32[8,8,32,256]{3,2,1,0:T(8,128)} %collective-permute-do, ...), custom_call_target="tpu_custom_call", output_to_operand_aliasing={{0}: (8, {}), {1}: (9, {}), {3}: (10, {})} | custom-call | flops 3221225472 | bytes 12582912 | tf_op jit(solution)/shard_map/start/pallas_call | solution.py:364
  270.4 4.3 collective-permute-start.5
  274.8 4.2 collective-permute-start.6
  278.9 8.0 %collective-permute-done.3 = f32[2,256,256]{2,1,0:T(8,128)S(1)} collective-permute-done((f32[2,256,256]{2,1,0:T(8,128)S(1)}, f32[2,256,256]{2,1,0:T(8,128)S(1)}, u32[]{:S(2)}, u32[]{:S(2)}) %collective-permute-start.3) | collective-permute-done | bytes 524320 | tf_op jit(solution)/shard_map/ppermute | solution.py:254
  286.9 22.9 %collective-permute-done.4 = f32[2,256,256]{2,1,0:T(8,128)S(1)} collective-permute-done((f32[2,256,256]{2,1,0:T(8,128)S(1)}, f32[2,256,256]{2,1,0:T(8,128)S(1)}, u32[]{:S(2)}, u32[]{:S(2)}) %collective-permute-start.4) | collective-permute-done | bytes 524320 | tf_op jit(solution)/shard_map/ppermute | solution.py:254
  312.3 14.3 %all-to-all-start.4 = ((f32[256,16,128]{2,1,0:T(8,128)}), f32[256,16,128]{2,1,0:T(8,128)}, u32[]{:S(2)}, u32[]{:S(2)}) async-start(f32[256,16,128]{2,1,0:T(8,128)} %bitcast.2), calls=%async_computation.4 | async-start | bytes 4194304 | tf_op jit(solution)/shard_map/all_to_all | solution.py:263
  326.6 38.6 %nodes.1 = f32[8,32,16,128]{3,2,1,0:T(8,128)} custom-call(f32[4,32,256,256]{3,2,1,0:T(8,128)} %get-tuple-element.72.v_ref, f32[2,256,256]{2,1,0:T(8,128)} %get-tuple-element.78.from_left_ref, f32[2,256,256]{2,1,0:T(8,128)} %get-tuple-element.79.from_right_ref, f32[2,256,256]{2,1,0:T(8,128)} %constant.104.clone.rho_ref, ...), custom_call_target="tpu_custom_call" | custom-call | flops 15032385536 | bytes 35651584 | tf_op jit(solution)/shard_map/nodes/pallas_call | solution.py:416
  365.2 9.1 %all-to-all-done.4.corner_ref = f32[256,16,128]{2,1,0:T(8,128)} async-done(((f32[256,16,128]{2,1,0:T(8,128)}), f32[256,16,128]{2,1,0:T(8,128)}, u32[]{:S(2)}, u32[]{:S(2)}) %all-to-all-start.4) | async-done | bytes 2097184 | tf_op jit(solution)/shard_map/all_to_all | solution.py:263
  374.3 4.5 all-to-all-start.5
  381.1 2.8 collective-permute-start.7
  383.9 42.4 %all-to-all-done.5.cubic_ref = f32[256,16,128]{2,1,0:T(8,128)S(1)} async-done(((f32[256,16,128]{2,1,0:T(8,128)}), f32[256,16,128]{2,1,0:T(8,128)S(1)}, u32[]{:S(2)}, u32[]{:S(2)}) %all-to-all-start.5) | async-done | bytes 2097184 | tf_op jit(solution)/shard_map/all_to_all | solution.py:263
  426.4 4.5 all-to-all-start.6
  434.8 5.3 %low.1 = (f32[256,32,256]{2,1,0:T(8,128)}, f32[128,16,128]{2,1,0:T(8,128)}) custom-call(f32[32]{0:T(128)} %dynamic_slice.6.fine_ref, f32[16]{0:T(128)} %dynamic_slice.7.coarse_ref, bf16[256,768]{1,0:T(8,128)(2,1)} %constant.100.clone.table_ref, f32[256,128]{1,0:T(8,128)} %constant.113.clone.eigen_ref, f32[128,128]{1,0:T(8,128)} %constant.114.clone.coarse_eigen_ref, ...), custom_call_target="tpu_custom_call" | custom-call | flops 1073741824 | bytes 6291456 | tf_op jit(solution)/shard_map/low/pallas_call | solution.py:450
  440.1 4.2 offset.1
  445.7 10.2 %all-to-all-done.6 = f32[64,16,256]{2,1,0:T(8,128)S(1)} async-done(((f32[64,16,256]{2,1,0:T(8,128)}), f32[64,16,256]{2,1,0:T(8,128)S(1)}, u32[]{:S(2)}, u32[]{:S(2)}) %all-to-all-start.6) | async-done | bytes 1048608 | tf_op jit(solution)/shard_map/all_to_all | solution.py:263
  456.9 4.5 all-to-all-start.7
  463.9 3.8 collective-permute-start.9
  467.7 11.1 %collective-permute-done.9 = f32[128,16,128]{2,1,0:T(8,128)} collective-permute-done((f32[128,16,128]{2,1,0:T(8,128)}, f32[128,16,128]{2,1,0:T(8,128)}, u32[]{:S(2)}, u32[]{:S(2)}) %collective-permute-start.9) | collective-permute-done | bytes 1048608 | tf_op jit(solution)/shard_map/ppermute | solution.py:491
  481.9 6.5 %finish.2 = f32[256,32,256]{2,1,0:T(8,128)} custom-call(f32[16]{0:T(128)} %get-tuple-element.96.fine_ref, bf16[256,768]{1,0:T(8,128)(2,1)} %constant.100.clone.table_ref, f32[256,256]{1,0:T(8,128)} %constant.115.clone.eigen_ref, f32[8,8,16,256]{3,2,1,0:T(8,128)} %bitcast.18, f32[8,24,16,256]{3,2,1,0:T(8,128)} %bitcast.15, ...), custom_call_target="tpu_custom_call", output_to_operand_aliasing={{}: (5, {})} | custom-call | flops 1610612736 | bytes 10485760 | tf_op jit(solution)/shard_map/finish/pallas_call | solution.py:473
  490.0 18.9 %all-to-all-done.7 = f32[256,16,128]{2,1,0:T(8,128)S(1)} async-done(((f32[256,16,128]{2,1,0:T(8,128)}), f32[256,16,128]{2,1,0:T(8,128)S(1)}, u32[]{:S(2)}, u32[]{:S(2)}) %all-to-all-start.7) | async-done | bytes 2097184 | tf_op jit(solution)/shard_map/all_to_all | solution.py:263
  510.3 4.5 finish.3
  (56 shorter events, 35.4 us)
Async XLA Ops:
  89.2 73.6 %all-to-all-start.1 = ((f32[8,12,32,256]{3,2,1,0:T(8,128)}), f32[8,12,32,256]{3,2,1,0:T(8,128)S(1)}, u32[]{:S(2)}, u32[]{:S(2)}) async-start(f32[8,12,32,256]{3,2,1,0:T(8,128)} %get-tuple-element.55), calls=%async_computation.1 | async-start | bytes 6291456 | tf_op jit(solution)/shard_map/all_to_all | solution.py:263
  93.3 37.1 %collective-permute-start = (f32[8,12,32,256]{3,2,1,0:T(8,128)}, f32[8,12,32,256]{3,2,1,0:T(8,128)S(1)}, u32[]{:S(2)}, u32[]{:S(2)}) collective-permute-start(f32[8,12,32,256]{3,2,1,0:T(8,128)} %all_to_all.40), channel_id=1, source_target_pairs={{0,8},{8,16},{16,24},{24,0},{1,9},{9,17},{17,25},{25,1},{2,10},{10... | collective-permute-start | bytes 9437192 | tf_op jit(solution)/shard_map/ppermute | solution.py:259
  130.4 2.1 copy-start.12
  162.8 59.6 %all-to-all-start.2 = ((f32[8,8,32,256]{3,2,1,0:T(8,128)}), f32[8,8,32,256]{3,2,1,0:T(8,128)}, u32[]{:S(2)}, u32[]{:S(2)}) async-start(f32[8,8,32,256]{3,2,1,0:T(8,128)} %get-tuple-element.59), calls=%async_computation.2 | async-start | bytes 4194304 | tf_op jit(solution)/shard_map/all_to_all | solution.py:263
  167.8 36.9 %collective-permute-start.2 = (f32[8,12,32,256]{3,2,1,0:T(8,128)S(1)}, f32[8,12,32,256]{3,2,1,0:T(8,128)S(1)}, u32[]{:S(2)}, u32[]{:S(2)}) collective-permute-start(f32[8,12,32,256]{3,2,1,0:T(8,128)S(1)} %all-to-all-done.1), channel_id=1, source_target_pairs={{0,8},{8,16},{16,24},{24,0},{1,9},{9,17},{17,25},{25,1},{2,10},{10... | collective-permute-start | bytes 9437192 | tf_op jit(solution)/shard_map/ppermute | solution.py:259
  204.7 1.7 copy-start.5
  222.4 89.9 %all-to-all-start.3 = ((f32[192,16,256]{2,1,0:T(8,128)}), f32[192,16,256]{2,1,0:T(8,128)S(1)}, u32[]{:S(2)}, u32[]{:S(2)}) async-start(f32[192,16,256]{2,1,0:T(8,128)} %bitcast.16), calls=%async_computation.3 | async-start | bytes 6291456 | tf_op jit(solution)/shard_map/all_to_all | solution.py:263
  228.0 26.1 %collective-permute-start.1 = (f32[8,8,32,256]{3,2,1,0:T(8,128)}, f32[8,8,32,256]{3,2,1,0:T(8,128)}, u32[]{:S(2)}, u32[]{:S(2)}) collective-permute-start(f32[8,8,32,256]{3,2,1,0:T(8,128)} %all-to-all-done.2), channel_id=1, source_target_pairs={{0,8},{8,16},{16,24},{24,0},{1,9},{9,17},{17,25},{25,1},{2,10},{10... | collective-permute-start | bytes 6291464 | tf_op jit(solution)/shard_map/ppermute | solution.py:259
  254.0 12.5 %copy-start.7 = (f32[2,256,256]{2,1,0:T(8,128)S(1)}, f32[2,256,256]{2,1,0:T(8,128)}, u32[]{:S(2)}) copy-start(f32[2,256,256]{2,1,0:T(8,128)} %constant.119) | copy-start | bytes 1572868
  254.0 55.8 %copy-start.8 = (f32[2,256,256]{2,1,0:T(8,128)S(1)}, f32[2,256,256]{2,1,0:T(8,128)}, u32[]{:S(2)}) copy-start(f32[2,256,256]{2,1,0:T(8,128)} %constant.108.clone) | copy-start | bytes 1572868
  254.0 55.8 %copy-start.9 = (f32[2,256,256]{2,1,0:T(8,128)S(1)}, f32[2,256,256]{2,1,0:T(8,128)}, u32[]{:S(2)}) copy-start(f32[2,256,256]{2,1,0:T(8,128)} %constant.107.clone) | copy-start | bytes 1572868
  267.8 19.1 %collective-permute-start.3 = (f32[2,256,256]{2,1,0:T(8,128)S(1)}, f32[2,256,256]{2,1,0:T(8,128)S(1)}, u32[]{:S(2)}, u32[]{:S(2)}) collective-permute-start(f32[2,256,256]{2,1,0:T(8,128)S(1)} %get-tuple-element.95), channel_id=1, source_target_pairs={{1,0},{2,1},{3,2},{4,3},{5,4},{6,5},{7,6},{9,8},{10,9},{11,10},{12... | collective-permute-start | bytes 1572872 | tf_op jit(solution)/shard_map/ppermute | solution.py:254
  269.1 40.7 %collective-permute-start.4 = (f32[2,256,256]{2,1,0:T(8,128)S(1)}, f32[2,256,256]{2,1,0:T(8,128)S(1)}, u32[]{:S(2)}, u32[]{:S(2)}) collective-permute-start(f32[2,256,256]{2,1,0:T(8,128)S(1)} %get-tuple-element.95), channel_id=1, source_target_pairs={{2,0},{3,1},{4,2},{5,3},{6,4},{7,5},{10,8},{11,9},{12,10},{13,11},... | collective-permute-start | bytes 1572872 | tf_op jit(solution)/shard_map/ppermute | solution.py:254
  270.4 39.4 %collective-permute-start.5 = (f32[2,256,256]{2,1,0:T(8,128)S(1)}, f32[2,256,256]{2,1,0:T(8,128)S(1)}, u32[]{:S(2)}, u32[]{:S(2)}) collective-permute-start(f32[2,256,256]{2,1,0:T(8,128)S(1)} %get-tuple-element.94), channel_id=1, source_target_pairs={{0,1},{1,2},{2,3},{3,4},{4,5},{5,6},{6,7},{8,9},{9,10},{10,11},{11... | collective-permute-start | bytes 1572872 | tf_op jit(solution)/shard_map/ppermute | solution.py:254
  274.8 35.1 %collective-permute-start.6 = (f32[2,256,256]{2,1,0:T(8,128)S(1)}, f32[2,256,256]{2,1,0:T(8,128)S(1)}, u32[]{:S(2)}, u32[]{:S(2)}) collective-permute-start(f32[2,256,256]{2,1,0:T(8,128)S(1)} %get-tuple-element.94), channel_id=1, source_target_pairs={{0,2},{1,3},{2,4},{3,5},{4,6},{5,7},{8,10},{9,11},{10,12},{11,13},... | collective-permute-start | bytes 1572872 | tf_op jit(solution)/shard_map/ppermute | solution.py:254
  312.3 52.9 %copy-start.1 = (f32[192,16,256]{2,1,0:T(8,128)}, f32[192,16,256]{2,1,0:T(8,128)S(1)}, u32[]{:S(2)}) copy-start(f32[192,16,256]{2,1,0:T(8,128)S(1)} %all-to-all-done.3) | copy-start | bytes 9437188
  312.3 62.0 %all-to-all-start.4 = ((f32[256,16,128]{2,1,0:T(8,128)}), f32[256,16,128]{2,1,0:T(8,128)}, u32[]{:S(2)}, u32[]{:S(2)}) async-start(f32[256,16,128]{2,1,0:T(8,128)} %bitcast.2), calls=%async_computation.4 | async-start | bytes 4194304 | tf_op jit(solution)/shard_map/all_to_all | solution.py:263
  374.3 52.1 %all-to-all-start.5 = ((f32[256,16,128]{2,1,0:T(8,128)}), f32[256,16,128]{2,1,0:T(8,128)S(1)}, u32[]{:S(2)}, u32[]{:S(2)}) async-start(f32[256,16,128]{2,1,0:T(8,128)} %bitcast.19), calls=%async_computation.5 | async-start | bytes 4194304 | tf_op jit(solution)/shard_map/all_to_all | solution.py:263
  378.8 52.1 %copy-start.13 = (f32[256]{0:T(256)S(1)}, f32[256]{0:T(256)}, u32[]{:S(2)}) copy-start(f32[256]{0:T(256)} %constant.98.clone) | copy-start | bytes 3076
  378.8 52.6 %copy-start.14 = (f32[128]{0:T(128)S(1)}, f32[128]{0:T(128)}, u32[]{:S(2)}) copy-start(f32[128]{0:T(128)} %constant.99.clone) | copy-start | bytes 1540
  381.1 50.9 %collective-permute-start.7 = (f32[128,16,128]{2,1,0:T(8,128)}, f32[128,16,128]{2,1,0:T(8,128)}, u32[]{:S(2)}, u32[]{:S(2)}) collective-permute-start(f32[128,16,128]{2,1,0:T(8,128)} %slice_bitcast_fusion), channel_id=1, source_target_pairs={{0,8},{8,16},{16,24},{1,9},{9,17},{17,25},{2,10},{10,18},{18,26},{... | collective-permute-start | bytes 3145736 | tf_op jit(solution)/shard_map/ppermute | solution.py:254
  426.4 13.7 %copy-start.2 = (f32[256,16,128]{2,1,0:T(8,128)}, f32[256,16,128]{2,1,0:T(8,128)S(1)}, u32[]{:S(2)}) copy-start(f32[256,16,128]{2,1,0:T(8,128)S(1)} %all-to-all-done.5.cubic_ref) | copy-start | bytes 6291460
  426.4 29.6 %all-to-all-start.6 = ((f32[64,16,256]{2,1,0:T(8,128)}), f32[64,16,256]{2,1,0:T(8,128)S(1)}, u32[]{:S(2)}, u32[]{:S(2)}) async-start(f32[64,16,256]{2,1,0:T(8,128)} %bitcast.20), calls=%async_computation.6 | async-start | bytes 2097152 | tf_op jit(solution)/shard_map/all_to_all | solution.py:263
  444.3 17.1 %copy-start = (f32[128,16,128]{2,1,0:T(8,128)S(1)}, f32[128,16,128]{2,1,0:T(8,128)}, u32[]{:S(2)}) copy-start(f32[128,16,128]{2,1,0:T(8,128)} %offset.1) | copy-start | bytes 3145732
  444.3 17.1 %copy-start.6 = (f32[128,128]{1,0:T(8,128)S(1)}, f32[128,128]{1,0:T(8,128)}, u32[]{:S(2)}) copy-start(f32[128,128]{1,0:T(8,128)} %constant.120) | copy-start | bytes 196612
  444.3 17.2 %copy-start.10 = (f32[16]{0:T(128)S(1)}, f32[16]{0:T(128)}, u32[]{:S(2)}) copy-start(f32[16]{0:T(128)} %dynamic_slice.7.coarse_ref) | copy-start | bytes 196
  444.3 17.1 %collective-permute-start.8 = (f32[128,16,128]{2,1,0:T(8,128)}, f32[128,16,128]{2,1,0:T(8,128)}, u32[]{:S(2)}, u32[]{:S(2)}) collective-permute-start(f32[128,16,128]{2,1,0:T(8,128)} %offset.1), channel_id=1, source_target_pairs={{0,8},{1,9},{2,10},{3,11},{4,12},{5,13},{6,14},{7,15}} | collective-permute-start | bytes 3145736 | tf_op jit(solution)/shard_map/ppermute | solution.py:491
  456.9 52.1 %all-to-all-start.7 = ((f32[256,16,128]{2,1,0:T(8,128)}), f32[256,16,128]{2,1,0:T(8,128)S(1)}, u32[]{:S(2)}, u32[]{:S(2)}) async-start(f32[256,16,128]{2,1,0:T(8,128)} %bitcast.5), calls=%async_computation.7 | async-start | bytes 4194304 | tf_op jit(solution)/shard_map/all_to_all | solution.py:263
  461.4 19.9 %copy-start.11 = (f32[32]{0:T(128)S(1)}, f32[32]{0:T(128)}, u32[]{:S(2)}) copy-start(f32[32]{0:T(128)} %dynamic_slice.6.fine_ref) | copy-start | bytes 388
  463.9 14.8 %collective-permute-start.9 = (f32[128,16,128]{2,1,0:T(8,128)}, f32[128,16,128]{2,1,0:T(8,128)}, u32[]{:S(2)}, u32[]{:S(2)}) collective-permute-start(f32[128,16,128]{2,1,0:T(8,128)} %add_select_fusion), channel_id=1, source_target_pairs={{8,16},{9,17},{10,18},{11,19},{12,20},{13,21},{14,22},{15,23}} | collective-permute-start | bytes 3145736 | tf_op jit(solution)/shard_map/ppermute | solution.py:491
  480.6 7.8 %collective-permute-start.10 = (f32[128,16,128]{2,1,0:T(8,128)S(1)}, f32[128,16,128]{2,1,0:T(8,128)S(1)}, u32[]{:S(2)}, u32[]{:S(2)}) collective-permute-start(f32[128,16,128]{2,1,0:T(8,128)S(1)} %add_select_fusion.2), channel_id=1, source_target_pairs={{16,24},{17,25},{18,26},{19,27},{20,28},{21,29},{22,30},{23,31}} | collective-permute-start | bytes 3145736 | tf_op jit(solution)/shard_map/ppermute | solution.py:491
  509.0 1.3 copy-start.3
  (1 other events, 1.0 us)

commit v4 on v3

--- a/solution.py
+++ b/solution.py
@@ -318,16 +318,35 @@
     lengths = (quarter, middle, block - quarter - middle)
     begins = (0, quarter, quarter + middle)
     parts = len(lengths)
-    outgoing = call(
-        depth_kernel,
-        "depth",
-        (block // ROWS,),
-        [SMEM, table_spec, rows_spec, pl.BlockSpec((1, grid, ROWS, grid), lambda i: (0, 0, i, 0))],
-        [pl.BlockSpec((groups, length, ROWS, grid), lambda i: (0, 0, i, 0)) for length in lengths],
-        [jax.ShapeDtypeStruct((groups, length, block, grid), F32) for length in lengths],
-        flops=6 * unit * grid,
-        moved=12 * unit,
-    )(last, depth_table, initial_modes, end_modes)
+    end_begin = begins[1]
+
+    def depth(chosen):
+        span = slice(begins[chosen[0]], begins[chosen[-1]] + lengths[chosen[-1]])
+        table = depth_table.reshape(groups, block, -1)[:, span].reshape(-1, depth_table.shape[1])
+        return pl.pallas_call(
+            depth_kernel,
+            grid_spec=pltpu.PrefetchScalarGridSpec(
+                num_scalar_prefetch=1,
+                grid=(block // ROWS,),
+                in_specs=[
+                    whole_block(table.shape),
+                    pl.BlockSpec((grid, ROWS, grid), lambda i, last: (0, i * last[0], 0)),
+                    pl.BlockSpec((1, grid, ROWS, grid), lambda i, last: (0, 0, i * (1 - last[0]), 0)),
+                ],
+                out_specs=[
+                    pl.BlockSpec((groups, lengths[part], ROWS, grid), lambda i, last: (0, 0, i, 0))
+                    for part in chosen
+                ],
+            ),
+            out_shape=[jax.ShapeDtypeStruct((groups, lengths[part], block, grid), F32) for part in chosen],
+            compiler_params=pltpu.CompilerParams(vmem_limit_bytes=VMEM_BYTES),
+            cost_estimate=pl.CostEstimate(flops=6 * unit * grid, bytes_accessed=8 * unit, transcendentals=0),
+            name="depth",
+        )(last, table, initial_modes, end_modes)
+
+    outgoing = [*depth((0, 1)), *depth((2,))]
+    for part in (1, 0):
+        outgoing[part] = turned(outgoing[part], "tm")
 
     pair = (2, grid, grid)
     pair_spec = whole_block(pair)
@@ -335,7 +354,7 @@
     shapes = [
         (*whole, coarse),
         (*whole, coarse),
-        (groups, block - lengths[0], half, grid),
+        (groups, block - end_begin, half, grid),
         (4, block, grid, grid),
     ]
     arrays = None
@@ -346,13 +365,13 @@
         if part + 1 in backs:
             given, *_ = after(given, backs[part + 1], *states.get(part + 2, ()))
         backs[part] = exchange(given)
-        modes = turned(backs[part], "tm")
+        modes = turned(backs[part], "tm") if part == parts - 1 else backs[part]
         steps = lengths[part] // planes
         bases = [begins[part] // planes] * 4
-        if part == 0:
-            shapes[2] = (groups, lengths[0], half, grid)
+        if part >= 1:
+            bases[2] = (begins[part] - end_begin) // planes
         else:
-            bases[2] = (begins[part] - lengths[0]) // planes
+            shapes[2] = (groups, end_begin, half, grid)
         specs = [
             pl.BlockSpec(
                 (4, planes, grid, grid) if n == 3 else (groups, planes, half, shapes[n][3]),
@@ -382,10 +401,10 @@
             moved=24 * unit * lengths[part] // block,
             aliases={8 + place: n for place, n in enumerate(held)},
         )(modes, x_table, y_table, back_table, rho, *state, *(arrays[n] for n in held))
-        if part == 0:
+        if part >= 1:
+            high_rest = outs[2]
+        else:
             high_first = outs[2]
-        else:
-            high_rest = outs[2]
         arrays, state = outs[:4], outs[4:]
         states[part] = state
     corner, side, _, v = arrays

time: 517 us -> 507 us (0.981)
  blocking collectives: 76.3 us -> 0 us
  waiting for transfers between devices: 229 us -> 278 us
  starting transfers between devices: 70.2 us -> 81.1 us
  Pallas kernels: 116 us -> 122 us
    all_to_all x1 -> x0, blocking collectives: 76.3 us -> none  [exchange(): return lax.all_to_all(value, 'gx', split_axis=0, concat_axis=0, tiled=True)]
    all_to_all x7 -> x8, waiting for transfers between devices: 94.6 us -> 143 us  [exchange(): return lax.all_to_all(value, 'gx', split_axis=0, concat_axis=0, tiled=True)]
    ppermute x5, waiting for transfers between devices: 30.9 us -> 50.4 us  [shifted(): return lax.ppermute(value, axis, pairs)]
    ppermute x3, waiting for transfers between devices: 92 us -> 73.3 us  [turned(): lax.ppermute(value, axis, [(i, (i + 1) % length) for i in range(length)])]
    all_to_all x7 -> x8, starting transfers between devices: 42.5 us -> 55.5 us  [exchange(): return lax.all_to_all(value, 'gx', split_axis=0, concat_axis=0, tiled=True)]
    pallas_call x1 -> x2, Pallas kernels: 12.3 us -> 18.1 us  [depth(): pl.pallas_call(depth_kernel, grid_spec=pltpu.PrefetchScalarGridSpec(num_s...]
  transfers between devices with their start and end apart: 18 -> 19, of which waited for: 11 -> 13; matrix products, arithmetic and copies ran while one was open for 4% -> 4% of each run, Pallas kernels for 19% -> 22%
where the time goes in v4:
time: 507 us; the launch traced here: 504 us
  waiting for transfers between devices  278 us (55%)
  Pallas kernels  122 us (24%)
  starting transfers between devices  81.1 us (16%)
  other arithmetic  12.4 us (2%)
  local copies, waits for them, and re-layouts  10.2 us (2%)
    all_to_all x8, waiting for transfers between devices, exchange(): return lax.all_to_all(value, 'gx', split_axis=0, concat_axis=0, tiled=True)  143 us
    ppermute x3, waiting for transfers between devices, turned(): lax.ppermute(value, axis, [(i, (i + 1) % length) for i in range(length)])  73.3 us
    all_to_all x8, starting transfers between devices, exchange(): return lax.all_to_all(value, 'gx', split_axis=0, concat_axis=0, tiled=True)  55.5 us
    ppermute x5, waiting for transfers between devices, shifted(): return lax.ppermute(value, axis, pairs)  50.4 us
    pallas_call x3, Pallas kernels, per_device(): call(functools.partial(start_kernel, planes), 'start', (steps,), [pl.Bloc...  44.6 us
    pallas_call x1, Pallas kernels, per_device(): call(functools.partial(node_kernel, planes, block), 'nodes', (block // pl...  38.6 us
    pallas_call x2, Pallas kernels, depth(): pl.pallas_call(depth_kernel, grid_spec=pltpu.PrefetchScalarGridSpec(num_s...  18.1 us
    ppermute x5, starting transfers between devices, shifted(): return lax.ppermute(value, axis, pairs)  14.4 us
  transfers between devices with their start and end apart: 19, of which 13 were waited for; matrix products, arithmetic and copies ran while one was open for 4% of the time, Pallas kernels for 22%

profile of v4, /device:TPU:1, one launch (start us, length us, event | category | flops | bytes accessed | tf_op | source)
XLA Modules:
  0.0 503.9 jit_solution(10764045280135175748)
XLA Ops:
  0.6 8.7 %depth.3 = f32[8,12,32,256]{3,2,1,0:T(8,128)} custom-call(s32[1]{0:T(128)} %bitcast.last_ref, bf16[96,768]{1,0:T(8,128)(2,1)} %constant.105.clone.table_ref, f32[256,32,256]{2,1,0:T(8,128)} %initial_ref.3, f32[1,256,32,256]{3,2,1,0:T(8,128)} %end_ref.3), custom_call_target="tpu_custom_call" | custom-call | flops 3221225472 | bytes 16777216 | tf_op jit(solution)/shard_map/depth/pallas_call | solution.py:326
  9.3 6.4 %all-to-all-start = ((f32[8,12,32,256]{3,2,1,0:T(8,128)}), f32[8,12,32,256]{3,2,1,0:T(8,128)}, u32[]{:S(2)}, u32[]{:S(2)}) async-start(f32[8,12,32,256]{3,2,1,0:T(8,128)} %depth.3), calls=%async_computation | async-start | bytes 6291456 | tf_op jit(solution)/shard_map/all_to_all | solution.py:263
  15.7 9.4 %depth.2 = (f32[8,8,32,256]{3,2,1,0:T(8,128)}, f32[8,12,32,256]{3,2,1,0:T(8,128)}) custom-call(s32[1]{0:T(128)} %bitcast.last_ref, bf16[160,768]{1,0:T(8,128)(2,1)} %constant.104.clone.table_ref, f32[256,32,256]{2,1,0:T(8,128)} %initial_ref.3, f32[1,256,32,256]{3,2,1,0:T(8,128)} %end_ref.3), custom_call_target="tpu_custom_call" | custom-call | flops 3221225472 | bytes 16777216 | tf_op jit(solution)/shard_map/depth/pallas_call | solution.py:326
  27.2 34.5 %collective-permute-done.1 = f32[8,12,32,256]{3,2,1,0:T(8,128)S(1)} collective-permute-done((f32[8,12,32,256]{3,2,1,0:T(8,128)}, f32[8,12,32,256]{3,2,1,0:T(8,128)S(1)}, u32[]{:S(2)}, u32[]{:S(2)}) %collective-permute-start.1) | collective-permute-done | bytes 3145760 | tf_op jit(solution)/shard_map/ppermute | solution.py:259
  63.4 22.3 %all-to-all-done = f32[8,12,32,256]{3,2,1,0:T(8,128)} async-done(((f32[8,12,32,256]{3,2,1,0:T(8,128)}), f32[8,12,32,256]{3,2,1,0:T(8,128)}, u32[]{:S(2)}, u32[]{:S(2)}) %all-to-all-start) | async-done | bytes 3145760 | tf_op jit(solution)/shard_map/all_to_all | solution.py:263
  85.6 4.7 all-to-all-start.1
  92.4 34.5 %collective-permute-done.2.modes_ref = f32[8,12,32,256]{3,2,1,0:T(8,128)S(1)} collective-permute-done((f32[8,12,32,256]{3,2,1,0:T(8,128)}, f32[8,12,32,256]{3,2,1,0:T(8,128)S(1)}, u32[]{:S(2)}, u32[]{:S(2)}) %collective-permute-start.2) | collective-permute-done | bytes 3145760 | tf_op jit(solution)/shard_map/ppermute | solution.py:259
  128.8 16.2 %start.3 = (f32[8,32,16,128]{3,2,1,0:T(8,128)}, f32[8,32,16,128]{3,2,1,0:T(8,128)}, f32[8,24,16,256]{3,2,1,0:T(8,128)}, f32[4,32,256,256]{3,2,1,0:T(8,128)}, f32...) custom-call(f32[8,12,32,256]{3,2,1,0:T(8,128)} %copy-done.13, ...), custom_call_target="tpu_custom_call" | custom-call | flops 4831838208 | bytes 18874368 | tf_op jit(solution)/shard_map/start/pallas_call | solution.py:383
  145.0 4.3 collective-permute-done
  149.3 11.1 %all-to-all-done.1.modes_ref = f32[8,12,32,256]{3,2,1,0:T(8,128)S(1)} async-done(((f32[8,12,32,256]{3,2,1,0:T(8,128)}), f32[8,12,32,256]{3,2,1,0:T(8,128)S(1)}, u32[]{:S(2)}, u32[]{:S(2)}) %all-to-all-start.1) | async-done | bytes 3145760 | tf_op jit(solution)/shard_map/all_to_all | solution.py:263
  160.4 4.5 all-to-all-start.2
  164.9 15.9 %start.4 = (f32[8,32,16,128]{3,2,1,0:T(8,128)}, f32[8,32,16,128]{3,2,1,0:T(8,128)}, f32[8,24,16,256]{3,2,1,0:T(8,128)}, f32[4,32,256,256]{3,2,1,0:T(8,128)}, f32...) custom-call(f32[8,12,32,256]{3,2,1,0:T(8,128)} %copy-done.2, ...), custom_call_target="tpu_custom_call", output_to_operand_aliasing={{0}: (8, {}), {1}: (9, {}), {2}: (10, {}), {3}: (11, {})} | custom-call | flops 4831838208 | bytes 18874368 | tf_op jit(solution)/shard_map/start/pallas_call | solution.py:383
  180.8 31.1 %all-to-all-done.2.modes_ref = f32[8,8,32,256]{3,2,1,0:T(8,128)} async-done(((f32[8,8,32,256]{3,2,1,0:T(8,128)}), f32[8,8,32,256]{3,2,1,0:T(8,128)}, u32[]{:S(2)}, u32[]{:S(2)}) %all-to-all-start.2) | async-done | bytes 2097184 | tf_op jit(solution)/shard_map/all_to_all | solution.py:263
  211.9 5.1 %all-to-all-start.3 = ((f32[192,16,256]{2,1,0:T(8,128)}), f32[192,16,256]{2,1,0:T(8,128)S(1)}, u32[]{:S(2)}, u32[]{:S(2)}) async-start(f32[192,16,256]{2,1,0:T(8,128)} %bitcast.16), calls=%async_computation.3 | async-start | bytes 6291456 | tf_op jit(solution)/shard_map/all_to_all | solution.py:263
  217.1 12.4 %start.5 = (f32[8,32,16,128]{3,2,1,0:T(8,128)}, f32[8,32,16,128]{3,2,1,0:T(8,128)}, f32[8,8,16,256]{3,2,1,0:T(8,128)}, f32[4,32,256,256]{3,2,1,0:T(8,128)}, f32[...) custom-call(f32[8,8,32,256]{3,2,1,0:T(8,128)} %all-to-all-done.2.mod, ...), custom_call_target="tpu_custom_call", output_to_operand_aliasing={{0}: (8, {}), {1}: (9, {}), {3}: (10, {})} | custom-call | flops 3221225472 | bytes 12582912 | tf_op jit(solution)/shard_map/start/pallas_call | solution.py:383
  241.5 23.6 %collective-permute-done.3 = f32[2,256,256]{2,1,0:T(8,128)S(1)} collective-permute-done((f32[2,256,256]{2,1,0:T(8,128)S(1)}, f32[2,256,256]{2,1,0:T(8,128)S(1)}, u32[]{:S(2)}, u32[]{:S(2)}) %collective-permute-start.3) | collective-permute-done | bytes 524320 | tf_op jit(solution)/shard_map/ppermute | solution.py:254
  265.1 26.7 %collective-permute-done.4 = f32[2,256,256]{2,1,0:T(8,128)S(1)} collective-permute-done((f32[2,256,256]{2,1,0:T(8,128)S(1)}, f32[2,256,256]{2,1,0:T(8,128)S(1)}, u32[]{:S(2)}, u32[]{:S(2)}) %collective-permute-start.4) | collective-permute-done | bytes 524320 | tf_op jit(solution)/shard_map/ppermute | solution.py:254
  294.4 21.4 %all-to-all-start.4 = ((f32[256,16,128]{2,1,0:T(8,128)}), f32[256,16,128]{2,1,0:T(8,128)}, u32[]{:S(2)}, u32[]{:S(2)}) async-start(f32[256,16,128]{2,1,0:T(8,128)} %bitcast.2), calls=%async_computation.4 | async-start | bytes 4194304 | tf_op jit(solution)/shard_map/all_to_all | solution.py:263
  315.7 38.6 %nodes.1 = f32[8,32,16,128]{3,2,1,0:T(8,128)} custom-call(f32[4,32,256,256]{3,2,1,0:T(8,128)} %get-tuple-element.70.v_ref, f32[2,256,256]{2,1,0:T(8,128)} %get-tuple-element.76.from_left_ref, f32[2,256,256]{2,1,0:T(8,128)} %get-tuple-element.77.from_right_ref, f32[2,256,256]{2,1,0:T(8,128)} %constant.109.clone.rho_ref, ...), custom_call_target="tpu_custom_call" | custom-call | flops 15032385536 | bytes 35651584 | tf_op jit(solution)/shard_map/nodes/pallas_call | solution.py:435
  354.3 9.1 %all-to-all-done.4.corner_ref = f32[256,16,128]{2,1,0:T(8,128)} async-done(((f32[256,16,128]{2,1,0:T(8,128)}), f32[256,16,128]{2,1,0:T(8,128)}, u32[]{:S(2)}, u32[]{:S(2)}) %all-to-all-start.4) | async-done | bytes 2097184 | tf_op jit(solution)/shard_map/all_to_all | solution.py:263
  363.4 4.5 all-to-all-start.5
  374.0 41.4 %all-to-all-done.5.cubic_ref = f32[256,16,128]{2,1,0:T(8,128)S(1)} async-done(((f32[256,16,128]{2,1,0:T(8,128)}), f32[256,16,128]{2,1,0:T(8,128)S(1)}, u32[]{:S(2)}, u32[]{:S(2)}) %all-to-all-start.5) | async-done | bytes 2097184 | tf_op jit(solution)/shard_map/all_to_all | solution.py:263
  415.5 4.5 all-to-all-start.6
  423.9 5.3 %low.1 = (f32[256,32,256]{2,1,0:T(8,128)}, f32[128,16,128]{2,1,0:T(8,128)}) custom-call(f32[32]{0:T(128)} %dynamic_slice.6.fine_ref, f32[16]{0:T(128)} %dynamic_slice.7.coarse_ref, bf16[256,768]{1,0:T(8,128)(2,1)} %constant.118.clone.table_ref, f32[256,128]{1,0:T(8,128)} %constant.119.clone.eigen_ref, f32[128,128]{1,0:T(8,128)} %constant.120.clone.coarse_eigen_ref, ...), custom_call_target="tpu_custom_call" | custom-call | flops 1073741824 | bytes 6291456 | tf_op jit(solution)/shard_map/low/pallas_call | solution.py:469
  429.2 4.2 offset.1
  434.8 10.2 %all-to-all-done.6 = f32[64,16,256]{2,1,0:T(8,128)S(1)} async-done(((f32[64,16,256]{2,1,0:T(8,128)}), f32[64,16,256]{2,1,0:T(8,128)S(1)}, u32[]{:S(2)}, u32[]{:S(2)}) %all-to-all-start.6) | async-done | bytes 1048608 | tf_op jit(solution)/shard_map/all_to_all | solution.py:263
  446.0 4.5 all-to-all-start.7
  453.0 4.8 collective-permute-start.9
  457.8 11.1 %collective-permute-done.9 = f32[128,16,128]{2,1,0:T(8,128)} collective-permute-done((f32[128,16,128]{2,1,0:T(8,128)}, f32[128,16,128]{2,1,0:T(8,128)}, u32[]{:S(2)}, u32[]{:S(2)}) %collective-permute-start.9) | collective-permute-done | bytes 1048608 | tf_op jit(solution)/shard_map/ppermute | solution.py:510
  472.3 6.5 %finish.2 = f32[256,32,256]{2,1,0:T(8,128)} custom-call(f32[16]{0:T(128)} %get-tuple-element.94.fine_ref, bf16[256,768]{1,0:T(8,128)(2,1)} %constant.118.clone.table_ref, f32[256,256]{1,0:T(8,128)} %constant.121.clone.eigen_ref, f32[8,8,16,256]{3,2,1,0:T(8,128)} %bitcast.18, f32[8,24,16,256]{3,2,1,0:T(8,128)} %bitcast.15, ...), custom_call_target="tpu_custom_call", output_to_operand_aliasing={{}: (5, {})} | custom-call | flops 1610612736 | bytes 10485760 | tf_op jit(solution)/shard_map/finish/pallas_call | solution.py:492
  480.4 17.7 %all-to-all-done.7 = f32[256,16,128]{2,1,0:T(8,128)S(1)} async-done(((f32[256,16,128]{2,1,0:T(8,128)}), f32[256,16,128]{2,1,0:T(8,128)S(1)}, u32[]{:S(2)}, u32[]{:S(2)}) %all-to-all-start.7) | async-done | bytes 2097184 | tf_op jit(solution)/shard_map/all_to_all | solution.py:263
  499.4 4.5 finish.3
  (60 shorter events, 43.6 us)
Async XLA Ops:
  9.3 76.3 %all-to-all-start = ((f32[8,12,32,256]{3,2,1,0:T(8,128)}), f32[8,12,32,256]{3,2,1,0:T(8,128)}, u32[]{:S(2)}, u32[]{:S(2)}) async-start(f32[8,12,32,256]{3,2,1,0:T(8,128)} %depth.3), calls=%async_computation | async-start | bytes 6291456 | tf_op jit(solution)/shard_map/all_to_all | solution.py:263
  25.1 36.6 %collective-permute-start.1 = (f32[8,12,32,256]{3,2,1,0:T(8,128)}, f32[8,12,32,256]{3,2,1,0:T(8,128)S(1)}, u32[]{:S(2)}, u32[]{:S(2)}) collective-permute-start(f32[8,12,32,256]{3,2,1,0:T(8,128)} %get-tuple-element.52), channel_id=1, source_target_pairs={{0,8},{8,16},{16,24},{24,0},{1,9},{9,17},{17,25},{25,1},{2,10},{10... | collective-permute-start | bytes 9437192 | tf_op jit(solution)/shard_map/ppermute | solution.py:259
  85.6 74.7 %all-to-all-start.1 = ((f32[8,12,32,256]{3,2,1,0:T(8,128)}), f32[8,12,32,256]{3,2,1,0:T(8,128)S(1)}, u32[]{:S(2)}, u32[]{:S(2)}) async-start(f32[8,12,32,256]{3,2,1,0:T(8,128)} %copy-done.6), calls=%async_computation.1 | async-start | bytes 6291456 | tf_op jit(solution)/shard_map/all_to_all | solution.py:263
  90.3 36.5 %collective-permute-start.2 = (f32[8,12,32,256]{3,2,1,0:T(8,128)}, f32[8,12,32,256]{3,2,1,0:T(8,128)S(1)}, u32[]{:S(2)}, u32[]{:S(2)}) collective-permute-start(f32[8,12,32,256]{3,2,1,0:T(8,128)} %all-to-all-done), channel_id=1, source_target_pairs={{0,8},{8,16},{16,24},{24,0},{1,9},{9,17},{17,25},{25,1},{2,10},{10... | collective-permute-start | bytes 9437192 | tf_op jit(solution)/shard_map/ppermute | solution.py:259
  92.3 57.0 %collective-permute-start = (f32[8,8,32,256]{3,2,1,0:T(8,128)}, f32[8,8,32,256]{3,2,1,0:T(8,128)}, u32[]{:S(2)}, u32[]{:S(2)}) collective-permute-start(f32[8,8,32,256]{3,2,1,0:T(8,128)} %get-tuple-element.51), channel_id=1, source_target_pairs={{0,8},{8,16},{16,24},{24,0},{1,9},{9,17},{17,25},{25,1},{2,10},{10... | collective-permute-start | bytes 6291464 | tf_op jit(solution)/shard_map/ppermute | solution.py:259
  126.8 2.0 copy-start.13
  160.4 4.5 copy-start.2
  160.4 51.5 %all-to-all-start.2 = ((f32[8,8,32,256]{3,2,1,0:T(8,128)}), f32[8,8,32,256]{3,2,1,0:T(8,128)}, u32[]{:S(2)}, u32[]{:S(2)}) async-start(f32[8,8,32,256]{3,2,1,0:T(8,128)} %collective-permute-done), calls=%async_computation.2 | async-start | bytes 4194304 | tf_op jit(solution)/shard_map/all_to_all | solution.py:263
  211.9 82.4 %all-to-all-start.3 = ((f32[192,16,256]{2,1,0:T(8,128)}), f32[192,16,256]{2,1,0:T(8,128)S(1)}, u32[]{:S(2)}, u32[]{:S(2)}) async-start(f32[192,16,256]{2,1,0:T(8,128)} %bitcast.16), calls=%async_computation.3 | async-start | bytes 6291456 | tf_op jit(solution)/shard_map/all_to_all | solution.py:263
  217.0 12.5 %copy-start.8 = (f32[2,256,256]{2,1,0:T(8,128)S(1)}, f32[2,256,256]{2,1,0:T(8,128)}, u32[]{:S(2)}) copy-start(f32[2,256,256]{2,1,0:T(8,128)} %constant.125) | copy-start | bytes 1572868
  217.0 74.8 %copy-start.9 = (f32[2,256,256]{2,1,0:T(8,128)S(1)}, f32[2,256,256]{2,1,0:T(8,128)}, u32[]{:S(2)}) copy-start(f32[2,256,256]{2,1,0:T(8,128)} %constant.112.clone) | copy-start | bytes 1572868
  217.0 74.8 %copy-start.10 = (f32[2,256,256]{2,1,0:T(8,128)S(1)}, f32[2,256,256]{2,1,0:T(8,128)}, u32[]{:S(2)}) copy-start(f32[2,256,256]{2,1,0:T(8,128)} %constant.113.clone) | copy-start | bytes 1572868
  230.9 34.2 %collective-permute-start.3 = (f32[2,256,256]{2,1,0:T(8,128)S(1)}, f32[2,256,256]{2,1,0:T(8,128)S(1)}, u32[]{:S(2)}, u32[]{:S(2)}) collective-permute-start(f32[2,256,256]{2,1,0:T(8,128)S(1)} %get-tuple-element.93), channel_id=1, source_target_pairs={{1,0},{2,1},{3,2},{4,3},{5,4},{6,5},{7,6},{9,8},{10,9},{11,10},{12... | collective-permute-start | bytes 1572872 | tf_op jit(solution)/shard_map/ppermute | solution.py:254
  232.2 59.7 %collective-permute-start.4 = (f32[2,256,256]{2,1,0:T(8,128)S(1)}, f32[2,256,256]{2,1,0:T(8,128)S(1)}, u32[]{:S(2)}, u32[]{:S(2)}) collective-permute-start(f32[2,256,256]{2,1,0:T(8,128)S(1)} %get-tuple-element.93), channel_id=1, source_target_pairs={{2,0},{3,1},{4,2},{5,3},{6,4},{7,5},{10,8},{11,9},{12,10},{13,11},... | collective-permute-start | bytes 1572872 | tf_op jit(solution)/shard_map/ppermute | solution.py:254
  233.5 58.4 %collective-permute-start.5 = (f32[2,256,256]{2,1,0:T(8,128)S(1)}, f32[2,256,256]{2,1,0:T(8,128)S(1)}, u32[]{:S(2)}, u32[]{:S(2)}) collective-permute-start(f32[2,256,256]{2,1,0:T(8,128)S(1)} %get-tuple-element.92), channel_id=1, source_target_pairs={{0,1},{1,2},{2,3},{3,4},{4,5},{5,6},{6,7},{8,9},{9,10},{10,11},{11... | collective-permute-start | bytes 1572872 | tf_op jit(solution)/shard_map/ppermute | solution.py:254
  237.5 54.4 %collective-permute-start.6 = (f32[2,256,256]{2,1,0:T(8,128)S(1)}, f32[2,256,256]{2,1,0:T(8,128)S(1)}, u32[]{:S(2)}, u32[]{:S(2)}) collective-permute-start(f32[2,256,256]{2,1,0:T(8,128)S(1)} %get-tuple-element.92), channel_id=1, source_target_pairs={{0,2},{1,3},{2,4},{3,5},{4,6},{5,7},{8,10},{9,11},{10,12},{11,13},... | collective-permute-start | bytes 1572872 | tf_op jit(solution)/shard_map/ppermute | solution.py:254
  294.4 60.0 %copy-start.1 = (f32[192,16,256]{2,1,0:T(8,128)}, f32[192,16,256]{2,1,0:T(8,128)S(1)}, u32[]{:S(2)}) copy-start(f32[192,16,256]{2,1,0:T(8,128)S(1)} %all-to-all-done.3) | copy-start | bytes 9437188
  294.4 69.0 %all-to-all-start.4 = ((f32[256,16,128]{2,1,0:T(8,128)}), f32[256,16,128]{2,1,0:T(8,128)}, u32[]{:S(2)}, u32[]{:S(2)}) async-start(f32[256,16,128]{2,1,0:T(8,128)} %bitcast.2), calls=%async_computation.4 | async-start | bytes 4194304 | tf_op jit(solution)/shard_map/all_to_all | solution.py:263
  363.4 52.1 %all-to-all-start.5 = ((f32[256,16,128]{2,1,0:T(8,128)}), f32[256,16,128]{2,1,0:T(8,128)S(1)}, u32[]{:S(2)}, u32[]{:S(2)}) async-start(f32[256,16,128]{2,1,0:T(8,128)} %bitcast.19), calls=%async_computation.5 | async-start | bytes 4194304 | tf_op jit(solution)/shard_map/all_to_all | solution.py:263
  367.9 52.1 %copy-start.15 = (f32[128]{0:T(128)S(1)}, f32[128]{0:T(128)}, u32[]{:S(2)}) copy-start(f32[128]{0:T(128)} %constant.103.clone) | copy-start | bytes 1540
  367.9 52.7 %copy-start.14 = (f32[256]{0:T(256)S(1)}, f32[256]{0:T(256)}, u32[]{:S(2)}) copy-start(f32[256]{0:T(256)} %constant.102.clone) | copy-start | bytes 3076
  370.2 51.0 %collective-permute-start.7 = (f32[128,16,128]{2,1,0:T(8,128)}, f32[128,16,128]{2,1,0:T(8,128)}, u32[]{:S(2)}, u32[]{:S(2)}) collective-permute-start(f32[128,16,128]{2,1,0:T(8,128)} %slice_bitcast_fusion), channel_id=1, source_target_pairs={{0,8},{8,16},{16,24},{1,9},{9,17},{17,25},{2,10},{10,18},{18,26},{... | collective-permute-start | bytes 3145736 | tf_op jit(solution)/shard_map/ppermute | solution.py:254
  415.5 13.7 %copy-start.3 = (f32[256,16,128]{2,1,0:T(8,128)}, f32[256,16,128]{2,1,0:T(8,128)S(1)}, u32[]{:S(2)}) copy-start(f32[256,16,128]{2,1,0:T(8,128)S(1)} %all-to-all-done.5.cubic_ref) | copy-start | bytes 6291460
  415.5 29.6 %all-to-all-start.6 = ((f32[64,16,256]{2,1,0:T(8,128)}), f32[64,16,256]{2,1,0:T(8,128)S(1)}, u32[]{:S(2)}, u32[]{:S(2)}) async-start(f32[64,16,256]{2,1,0:T(8,128)} %bitcast.20), calls=%async_computation.6 | async-start | bytes 2097152 | tf_op jit(solution)/shard_map/all_to_all | solution.py:263
  433.4 17.1 %copy-start = (f32[128,16,128]{2,1,0:T(8,128)S(1)}, f32[128,16,128]{2,1,0:T(8,128)}, u32[]{:S(2)}) copy-start(f32[128,16,128]{2,1,0:T(8,128)} %offset.1) | copy-start | bytes 3145732
  433.4 17.1 %copy-start.7 = (f32[128,128]{1,0:T(8,128)S(1)}, f32[128,128]{1,0:T(8,128)}, u32[]{:S(2)}) copy-start(f32[128,128]{1,0:T(8,128)} %constant.126) | copy-start | bytes 196612
  433.4 17.1 %copy-start.11 = (f32[16]{0:T(128)S(1)}, f32[16]{0:T(128)}, u32[]{:S(2)}) copy-start(f32[16]{0:T(128)} %dynamic_slice.7.coarse_ref) | copy-start | bytes 196
  433.4 17.1 %collective-permute-start.8 = (f32[128,16,128]{2,1,0:T(8,128)}, f32[128,16,128]{2,1,0:T(8,128)}, u32[]{:S(2)}, u32[]{:S(2)}) collective-permute-start(f32[128,16,128]{2,1,0:T(8,128)} %offset.1), channel_id=1, source_target_pairs={{0,8},{1,9},{2,10},{3,11},{4,12},{5,13},{6,14},{7,15}} | collective-permute-start | bytes 3145736 | tf_op jit(solution)/shard_map/ppermute | solution.py:510
  446.0 52.1 %all-to-all-start.7 = ((f32[256,16,128]{2,1,0:T(8,128)}), f32[256,16,128]{2,1,0:T(8,128)S(1)}, u32[]{:S(2)}, u32[]{:S(2)}) async-start(f32[256,16,128]{2,1,0:T(8,128)} %bitcast.5), calls=%async_computation.7 | async-start | bytes 4194304 | tf_op jit(solution)/shard_map/all_to_all | solution.py:263
  450.5 21.1 %copy-start.12 = (f32[32]{0:T(128)S(1)}, f32[32]{0:T(128)}, u32[]{:S(2)}) copy-start(f32[32]{0:T(128)} %dynamic_slice.6.fine_ref) | copy-start | bytes 388
  453.0 15.8 %collective-permute-start.9 = (f32[128,16,128]{2,1,0:T(8,128)}, f32[128,16,128]{2,1,0:T(8,128)}, u32[]{:S(2)}, u32[]{:S(2)}) collective-permute-start(f32[128,16,128]{2,1,0:T(8,128)} %add_select_fusion), channel_id=1, source_target_pairs={{8,16},{9,17},{10,18},{11,19},{12,20},{13,21},{14,22},{15,23}} | collective-permute-start | bytes 3145736 | tf_op jit(solution)/shard_map/ppermute | solution.py:510
  470.7 8.1 %collective-permute-start.10 = (f32[128,16,128]{2,1,0:T(8,128)S(1)}, f32[128,16,128]{2,1,0:T(8,128)S(1)}, u32[]{:S(2)}, u32[]{:S(2)}) collective-permute-start(f32[128,16,128]{2,1,0:T(8,128)S(1)} %add_select_fusion.2), channel_id=1, source_target_pairs={{16,24},{17,25},{18,26},{19,27},{20,28},{21,29},{22,30},{23,31}} | collective-permute-start | bytes 3145736 | tf_op jit(solution)/shard_map/ppermute | solution.py:510
  (3 other events, 4.0 us)

commit v5 on v4

--- a/solution.py
+++ b/solution.py
@@ -104,7 +104,7 @@
 
 
 def start_kernel(planes, modes_ref, sx_ref, sy_ref, syt_ref, rho_ref, power_ref, right_ref, left_ref, *refs):
-    corner_ref, side_ref, high_ref, v_ref, power, to_right_ref, to_left_ref, cubic = refs[-8:]
+    corner_ref, rest_ref, v_ref, power, to_right_ref, to_left_ref, cubic = refs[-7:]
 
     @pl.when(pl.program_id(0) == 0)
     def _():
@@ -133,10 +133,10 @@
             mode = modes_ref[group, j, within]
             source = 2.0 * mode - cubic[j, rows]
             if upper:
-                high_ref[group, j] = source
+                rest_ref[group, j, :, :wide] = source
             else:
                 corner_ref[group, j] = source[:, :wide // 2]
-                side_ref[group, j] = source[:, wide // 2:]
+                rest_ref[group, j, :, wide:] = source[:, wide // 2:]
             for node, value in enumerate((source, 0.5 * (mode + source))):
                 carried[node] = value + rho[node] * carried[node]
                 v_ref[node, j, rows] = carried[node]
@@ -197,8 +197,7 @@
 
 
 def joined(refs):
-    parts = [ref[...] for ref in refs]
-    parts = jnp.concatenate(parts, axis=1)
+    parts = jnp.concatenate([ref[...] for ref in refs], axis=1)
     return parts.reshape(parts.shape[0] * parts.shape[1], *parts.shape[2:])
 
 
@@ -213,7 +212,7 @@
         source = left(table_ref[...], sources[row])
         eigen = eigen_ref[...] + fine_ref[base + row]
         node_end = source / (1.0 + eigen)
-        ends.append(node_end)
+        ends.append(node_end[coarse:])
         source, node_end, eigen = source[:coarse], node_end[:coarse], eigen[:coarse]
         start = starts[row]
         node_mid = 0.5 * (start + source) / (1.0 + 0.5 * eigen)
@@ -237,15 +236,28 @@
     out_ref[...] = jnp.swapaxes(jnp.stack(rows), 0, 1)
 
 
-def finish_kernel(fine_ref, table_ref, eigen_ref, *refs):
-    base = pl.program_id(0) * ROWS
+def finish_kernel(factor, fine_ref, table_ref, eigen_ref, corner_ref, end_ref, *refs):
     out_ref = refs[-1]
-    sources = jnp.swapaxes(joined(refs[:-2]), 0, 1)
-    rows = []
-    for row in range(ROWS):
-        source = left(table_ref[...], sources[row])
-        rows.append(source / (1.0 + eigen_ref[...] + fine_ref[base + row]))
-    out_ref[...] = jnp.swapaxes(jnp.stack(rows), 0, 1)
+    coarse = end_ref.shape[0]
+    steps = pl.num_programs(0) // 2
+    step = pl.program_id(0)
+    base = (step + steps) % (2 * steps) * ROWS
+    fields = [joined(refs[n:n + 2]) for n in range(0, 6, 2)]
+
+    def solved(source, eigen):
+        source = jnp.swapaxes(source, 0, 1)
+        rows = [left(table_ref[...], source[row]) / (1.0 + eigen + fine_ref[base + row]) for row in range(ROWS)]
+        return jnp.swapaxes(jnp.stack(rows), 0, 1)
+
+    @pl.when(step < steps)
+    def _():
+        out_ref[...] = solved(jnp.concatenate(fields[:2], axis=2), eigen_ref[...])
+
+    @pl.when(step >= steps)
+    def _():
+        out_ref[:coarse, :, :coarse] = end_ref[...] / factor
+        out_ref[coarse:, :, :coarse] = corner_ref[...]
+        out_ref[:, :, coarse:] = solved(fields[2], eigen_ref[:, coarse:])
 
 
 def shifted(value, axis, by):
@@ -313,10 +325,8 @@
 
     rows_spec = pl.BlockSpec((grid, ROWS, grid), lambda i: (0, i, 0))
     table_spec = whole_block(depth_table.shape)
-    quarter = block // 4
-    middle = 3 * quarter // planes // 2 * planes
-    lengths = (quarter, middle, block - quarter - middle)
-    begins = (0, quarter, quarter + middle)
+    lengths = (block // 2, block - block // 2)
+    begins = (0, block // 2)
     parts = len(lengths)
     end_begin = begins[1]
 
@@ -344,17 +354,15 @@
             name="depth",
         )(last, table, initial_modes, end_modes)
 
-    outgoing = [*depth((0, 1)), *depth((2,))]
-    for part in (1, 0):
-        outgoing[part] = turned(outgoing[part], "tm")
+    outgoing = [*depth((0,)), *depth((1,))]
+    outgoing[0] = turned(outgoing[0], "tm")
 
     pair = (2, grid, grid)
     pair_spec = whole_block(pair)
     whole = (groups, block, half)
     shapes = [
         (*whole, coarse),
-        (*whole, coarse),
-        (groups, block - end_begin, half, grid),
+        (groups, block - end_begin, half, grid + coarse),
         (4, block, grid, grid),
     ]
     arrays = None
@@ -367,19 +375,19 @@
         backs[part] = exchange(given)
         modes = turned(backs[part], "tm") if part == parts - 1 else backs[part]
         steps = lengths[part] // planes
-        bases = [begins[part] // planes] * 4
+        bases = [begins[part] // planes] * 3
         if part >= 1:
-            bases[2] = (begins[part] - end_begin) // planes
+            bases[1] = (begins[part] - end_begin) // planes
         else:
-            shapes[2] = (groups, end_begin, half, grid)
+            shapes[1] = (groups, end_begin, half, grid + coarse)
         specs = [
             pl.BlockSpec(
-                (4, planes, grid, grid) if n == 3 else (groups, planes, half, shapes[n][3]),
+                (4, planes, grid, grid) if n == 2 else (groups, planes, half, shapes[n][3]),
                 lambda i, base=base, steps=steps: (0, base + steps - 1 - i, 0, 0),
             )
             for n, base in enumerate(bases)
         ]
-        held = [n for n in range(4) if arrays is not None and not (part == 0 and n == 2)]
+        held = [n for n in range(3) if arrays is not None and not (part == 0 and n == 1)]
         outs = call(
             functools.partial(start_kernel, planes),
             "start",
@@ -402,15 +410,15 @@
             aliases={8 + place: n for place, n in enumerate(held)},
         )(modes, x_table, y_table, back_table, rho, *state, *(arrays[n] for n in held))
         if part >= 1:
-            high_rest = outs[2]
+            rest_last = outs[1]
         else:
-            high_first = outs[2]
-        arrays, state = outs[:4], outs[4:]
+            rest_first = outs[1]
+        arrays, state = outs[:3], outs[3:]
         states[part] = state
-    corner, side, _, v = arrays
+    corner, _, v = arrays
     _, to_right, to_left = state
-    high_rest, backs[0] = after(high_rest, backs[0])
-    high_rest_back = exchange(high_rest.reshape(-1, half, grid))
+    rest_last, backs[0] = after(rest_last, backs[0])
+    rest_last_back = exchange(rest_last)
     at_start, at_end = group_index == 0, group_index == groups - 1
     if rounds <= 2:
         rightward = jnp.where(at_start, to_right - rho_slab * (rho * to_left), to_right)
@@ -430,7 +438,7 @@
             from_left = jnp.where(at_start, -rho * leftward, shifted(rightward, "gx", 1))
             from_right = jnp.where(at_end, -rho * rightward, shifted(leftward, "gx", -1))
 
-    corner, high_rest_back, from_left, from_right = after(corner, high_rest_back, from_left, from_right)
+    corner, rest_last_back, from_left, from_right = after(corner, rest_last_back, from_left, from_right)
     corner_back = exchange(corner.reshape(grid, half, coarse))
     cubic = call(
         functools.partial(node_kernel, planes, block),
@@ -452,11 +460,8 @@
     )(v, from_left, from_right, rho, inverse, kappa, x_table, y_table, x_low_table, low_table)
     cubic, corner_back = after(cubic, corner_back)
     cubic_back = exchange(cubic.reshape(grid, half, coarse))
-    high_first, cubic_back = after(high_first, cubic_back)
-    high_first_back = exchange(high_first.reshape(-1, half, grid))
-    side, high_first_back = after(side, high_first_back)
-    side_back = exchange(side.reshape(grid, half, coarse))
-    high_backs = [part.reshape(groups, -1, half, grid) for part in (high_first_back, high_rest_back)]
+    rest_first, cubic_back = after(rest_first, cubic_back)
+    rest_backs = [exchange(rest_first), rest_last_back]
     start_low = jnp.where(
         is_first, initial_modes[:coarse, :half, :coarse], shifted(end_modes[0, :coarse, :half, :coarse], "tm", 1)
     )
@@ -466,13 +471,13 @@
     quarter_spec = pl.BlockSpec((grid, ROWS, coarse), lambda i: (0, i, 0))
     corner_shape = jax.ShapeDtypeStruct((coarse, half, coarse), F32)
     result_shape = jax.ShapeDtypeStruct((grid, block, grid), F32)
-    result, gathered = call(
+    corner_end, gathered = call(
         functools.partial(low_kernel, factor),
         "low",
         (half // ROWS,),
         [SMEM, SMEM, table_spec, whole_block((grid, coarse)), coarse_eigen_spec, quarter_spec, low_spec],
-        [quarter_spec, low_spec],
-        [result_shape, corner_shape],
+        [low_spec, low_spec],
+        [corner_shape, corner_shape],
         flops=2 * unit * grid,
         moved=3 * unit,
     )(fine_own, coarse_own, depth_table, eigen[:, :coarse], coarse_eigen, corner_back, start_low)
@@ -487,32 +492,32 @@
         moved=2 * unit,
     )(first, coarse_own, low_table, coarse_eigen, gathered, start_low, cubic_back)
 
-    def finish(result, sources, weights, eigen, row, column):
-        width = eigen.shape[1]
-        return call(
-            finish_kernel,
-            "finish",
-            (half // ROWS,),
-            [SMEM, table_spec, whole_block(eigen.shape)]
-            + [pl.BlockSpec((groups, part.shape[1], ROWS, width), lambda i: (0, 0, i, 0)) for part in sources]
-            + [pl.BlockSpec(memory_space=pl.ANY)],
-            pl.BlockSpec((grid, ROWS, width), lambda i: (0, row // ROWS + i, column)),
-            result_shape,
-            flops=3 * unit * width,
-            moved=5 * unit * width // grid,
-            aliases={3 + len(sources): 0},
-        )(weights, depth_table, eigen, *sources, result)
-
-    result = finish(result, high_backs, fine_own[half:], eigen, half, 0)
     decay = 1.0 / (1.0 + coarse_eigen[:, None, :] + coarse_own[None, :, None])
     coarse_end = offset
     for turn in range(1, slices):
         incoming = lax.ppermute(coarse_end, "tm", [(turn - 1, turn)])
         coarse_end = jnp.where(slice_index == turn, decay * incoming + offset, coarse_end)
-    result = result.at[:coarse, :half, :coarse].set(coarse_end / factor)
-    result = finish(
-        result, [side_back.reshape(groups, block, half, coarse)], fine_own[:half], eigen[:, coarse:], 0, 1
-    )
+    turns = half // ROWS
+    upper = [
+        pl.BlockSpec((groups, part.shape[1], ROWS, coarse), lambda i, n=n: (0, 0, jnp.minimum(i, turns - 1), n))
+        for n in range(2)
+        for part in rest_backs
+    ]
+    side = [
+        pl.BlockSpec((groups, part.shape[1], ROWS, coarse), lambda i: (0, 0, jnp.maximum(i - turns, 0), 2))
+        for part in rest_backs
+    ]
+    corner_spec = pl.BlockSpec((coarse, ROWS, coarse), lambda i: (0, jnp.maximum(i - turns, 0), 0))
+    result = call(
+        functools.partial(finish_kernel, factor),
+        "finish",
+        (2 * turns,),
+        [SMEM, table_spec, whole_block(eigen.shape), corner_spec, corner_spec] + upper + side,
+        pl.BlockSpec((grid, ROWS, grid), lambda i: (0, (i + turns) % (2 * turns), 0)),
+        result_shape,
+        flops=5 * unit * grid,
+        moved=9 * unit,
+    )(fine_own, depth_table, eigen, corner_end, coarse_end, *(rest_backs * 3))
     return (result[None], coarse_end[None])
 
 

time: 507 us -> 501 us (0.988)
  starting transfers between devices: 81.1 us -> 70.3 us
  waiting for transfers between devices: 278 us -> 288 us
    ppermute x3 -> x2, waiting for transfers between devices: 73.3 us -> 91.5 us  [turned(): lax.ppermute(value, axis, [(i, (i + 1) % length) for i in range(length)])]
    all_to_all x8 -> x6, starting transfers between devices: 55.5 us -> 46.7 us  [exchange(): return lax.all_to_all(value, 'gx', split_axis=0, concat_axis=0, tiled=True)]
    ppermute x5, waiting for transfers between devices: 50.4 us -> 43.1 us  [shifted(): return lax.ppermute(value, axis, pairs)]
    pallas_call x3 -> x2, Pallas kernels: 44.6 us -> 39.4 us  [per_device(): call(functools.partial(start_kernel, planes), 'start', (steps,), [pl.Bloc...]
    all_to_all x8 -> x6, waiting for transfers between devices: 143 us -> 139 us  [exchange(): return lax.all_to_all(value, 'gx', split_axis=0, concat_axis=0, tiled=True)]
    pallas_call x2 -> x1, Pallas kernels: 10.9 us -> 11.7 us  [per_device(): call(functools.partial(finish_kernel, factor), 'finish', (2 * turns,), [S...]
  transfers between devices with their start and end apart: 19 -> 16, of which waited for: 13 -> 11; matrix products, arithmetic and copies ran while one was open for 4% -> 4% of each run, Pallas kernels for 22% -> 19%
where the time goes in v5:
time: 501 us; the launch traced here: 498 us
  waiting for transfers between devices  288 us (57%)
  Pallas kernels  117 us (23%)
  starting transfers between devices  70.3 us (14%)
  other arithmetic  12.7 us (3%)
  local copies, waits for them, and re-layouts  8.91 us (2%)
    all_to_all x6, waiting for transfers between devices, exchange(): return lax.all_to_all(value, 'gx', split_axis=0, concat_axis=0, tiled=True)  139 us
    ppermute x2, waiting for transfers between devices, turned(): lax.ppermute(value, axis, [(i, (i + 1) % length) for i in range(length)])  91.5 us
    all_to_all x6, starting transfers between devices, exchange(): return lax.all_to_all(value, 'gx', split_axis=0, concat_axis=0, tiled=True)  46.7 us
    ppermute x5, waiting for transfers between devices, shifted(): return lax.ppermute(value, axis, pairs)  43.1 us
    pallas_call x2, Pallas kernels, per_device(): call(functools.partial(start_kernel, planes), 'start', (steps,), [pl.Bloc...  39.4 us
    pallas_call x1, Pallas kernels, per_device(): call(functools.partial(node_kernel, planes, block), 'nodes', (block // pl...  38.6 us
    pallas_call x2, Pallas kernels, depth(): pl.pallas_call(depth_kernel, grid_spec=pltpu.PrefetchScalarGridSpec(num_s...  18 us
    ppermute x3, waiting for transfers between devices, per_device(): incoming = lax.ppermute(coarse_end, 'tm', [(turn - 1, turn)])  14.7 us
  transfers between devices with their start and end apart: 16, of which 11 were waited for; matrix products, arithmetic and copies ran while one was open for 4% of the time, Pallas kernels for 19%

profile of v5, /device:TPU:1, one launch (start us, length us, event | category | flops | bytes accessed | tf_op | source)
XLA Modules:
  0.0 497.9 jit_solution(1753078747512965791)
XLA Ops:
  0.6 9.1 %depth.3 = f32[8,16,32,256]{3,2,1,0:T(8,128)} custom-call(s32[1]{0:T(128)} %bitcast.last_ref, bf16[128,768]{1,0:T(8,128)(2,1)} %constant.73.clone.table_ref, f32[256,32,256]{2,1,0:T(8,128)} %initial_ref.3, f32[1,256,32,256]{3,2,1,0:T(8,128)} %end_ref.3), custom_call_target="tpu_custom_call" | custom-call | flops 3221225472 | bytes 16777216 | tf_op jit(solution)/shard_map/depth/pallas_call | solution.py:336
  9.7 6.4 %all-to-all-start = ((f32[8,16,32,256]{3,2,1,0:T(8,128)}), f32[8,16,32,256]{3,2,1,0:T(8,128)}, u32[]{:S(2)}, u32[]{:S(2)}) async-start(f32[8,16,32,256]{3,2,1,0:T(8,128)} %depth.3), calls=%async_computation | async-start | bytes 8388608 | tf_op jit(solution)/shard_map/all_to_all | solution.py:275
  16.1 9.0 %depth.2 = f32[8,16,32,256]{3,2,1,0:T(8,128)} custom-call(s32[1]{0:T(128)} %bitcast.last_ref, bf16[128,768]{1,0:T(8,128)(2,1)} %constant.72.clone.table_ref, f32[256,32,256]{2,1,0:T(8,128)} %initial_ref.3, f32[1,256,32,256]{3,2,1,0:T(8,128)} %end_ref.3), custom_call_target="tpu_custom_call" | custom-call | flops 3221225472 | bytes 16777216 | tf_op jit(solution)/shard_map/depth/pallas_call | solution.py:336
  27.1 45.8 %collective-permute-done = f32[8,16,32,256]{3,2,1,0:T(8,128)} collective-permute-done((f32[8,16,32,256]{3,2,1,0:T(8,128)}, f32[8,16,32,256]{3,2,1,0:T(8,128)}, u32[]{:S(2)}, u32[]{:S(2)}) %collective-permute-start) | collective-permute-done | bytes 4194336 | tf_op jit(solution)/shard_map/ppermute | solution.py:271
  72.9 35.6 %all-to-all-done = f32[8,16,32,256]{3,2,1,0:T(8,128)} async-done(((f32[8,16,32,256]{3,2,1,0:T(8,128)}), f32[8,16,32,256]{3,2,1,0:T(8,128)}, u32[]{:S(2)}, u32[]{:S(2)}) %all-to-all-start) | async-done | bytes 4194336 | tf_op jit(solution)/shard_map/all_to_all | solution.py:275
  108.5 4.7 all-to-all-start.1
  113.2 2.9 collective-permute-start.1
  116.1 45.8 %collective-permute-done.1.modes_ref = f32[8,16,32,256]{3,2,1,0:T(8,128)S(1)} collective-permute-done((f32[8,16,32,256]{3,2,1,0:T(8,128)}, f32[8,16,32,256]{3,2,1,0:T(8,128)S(1)}, u32[]{:S(2)}, u32[]{:S(2)}) %collective-permute-start.1) | collective-permute-done | bytes 4194336 | tf_op jit(solution)/shard_map/ppermute | solution.py:271
  164.2 19.7 %start.2 = (f32[8,32,16,128]{3,2,1,0:T(8,128)}, f32[8,16,16,384]{3,2,1,0:T(8,128)}, f32[4,32,256,256]{3,2,1,0:T(8,128)}, f32[2,256,256]{2,1,0:T(8,128)}, f32[2,256,256]{2,1,0:T(8,128)}, /*index=5*/f32[2,256,256]{2,1,0:T(8,128)}) custom-call(f32[8,16,32,256]{3,2,1,0:T(8,128)} %copy-done.9, bf16[768,256]{1,0:T(8,128)(2,1)} %constant.74.clone.sx_ref, ...), custom_call_target="tpu_custom_call" | custom-call | flops 6442450944 | bytes 25165824 | tf_op jit(solution)/shard_map/start/pallas_call | solution.py:391
  183.9 21.0 %all-to-all-done.1.modes_ref = f32[8,16,32,256]{3,2,1,0:T(8,128)} async-done(((f32[8,16,32,256]{3,2,1,0:T(8,128)}), f32[8,16,32,256]{3,2,1,0:T(8,128)}, u32[]{:S(2)}, u32[]{:S(2)}) %all-to-all-start.1) | async-done | bytes 4194336 | tf_op jit(solution)/shard_map/all_to_all | solution.py:275
  204.9 5.3 %all-to-all-start.2 = ((f32[8,16,16,384]{3,2,1,0:T(8,128)}), f32[8,16,16,384]{3,2,1,0:T(8,128)S(1)}, u32[]{:S(2)}, u32[]{:S(2)}) async-start(f32[8,16,16,384]{3,2,1,0:T(8,128)} %get-tuple-element.34), calls=%async_computation.2 | async-start | bytes 6291456 | tf_op jit(solution)/shard_map/all_to_all | solution.py:275
  210.3 19.7 %start.3 = (f32[8,32,16,128]{3,2,1,0:T(8,128)}, f32[8,16,16,384]{3,2,1,0:T(8,128)}, f32[4,32,256,256]{3,2,1,0:T(8,128)}, f32[2,256,256]{2,1,0:T(8,128)}, f32[2,256,256]{2,1,0:T(8,128)}, /*index=5*/f32[2,256,256]{2,1,0:T(8,128)}) custom-call(f32[8,16,32,256]{3,2,1,0:T(8,128)} %all-to-all-done.1.modes_ref, ...), custom_call_target="tpu_custom_call", output_to_operand_aliasing={{0}: (8, {}), {2}: (9, {})} | custom-call | flops 6442450944 | bytes 25165824 | tf_op jit(solution)/shard_map/start/pallas_call | solution.py:391
  233.9 4.0 collective-permute-start.4
  238.0 4.0 collective-permute-start.5
  242.0 18.8 %collective-permute-done.2 = f32[2,256,256]{2,1,0:T(8,128)S(1)} collective-permute-done((f32[2,256,256]{2,1,0:T(8,128)S(1)}, f32[2,256,256]{2,1,0:T(8,128)S(1)}, u32[]{:S(2)}, u32[]{:S(2)}) %collective-permute-start.2) | collective-permute-done | bytes 524320 | tf_op jit(solution)/shard_map/ppermute | solution.py:266
  260.8 24.3 %collective-permute-done.3 = f32[2,256,256]{2,1,0:T(8,128)S(1)} collective-permute-done((f32[2,256,256]{2,1,0:T(8,128)S(1)}, f32[2,256,256]{2,1,0:T(8,128)S(1)}, u32[]{:S(2)}, u32[]{:S(2)}) %collective-permute-start.3) | collective-permute-done | bytes 524320 | tf_op jit(solution)/shard_map/ppermute | solution.py:266
  285.1 2.5 multiply_select_fusion
  287.6 21.4 %all-to-all-start.3 = ((f32[256,16,128]{2,1,0:T(8,128)}), f32[256,16,128]{2,1,0:T(8,128)}, u32[]{:S(2)}, u32[]{:S(2)}) async-start(f32[256,16,128]{2,1,0:T(8,128)} %bitcast.9), calls=%async_computation.3 | async-start | bytes 4194304 | tf_op jit(solution)/shard_map/all_to_all | solution.py:275
  308.9 38.6 %nodes.1 = f32[8,32,16,128]{3,2,1,0:T(8,128)} custom-call(f32[4,32,256,256]{3,2,1,0:T(8,128)} %get-tuple-element.31.v_ref, f32[2,256,256]{2,1,0:T(8,128)} %get-tuple-element.37.from_left_ref, f32[2,256,256]{2,1,0:T(8,128)} %get-tuple-element.38.from_right_ref, f32[2,256,256]{2,1,0:T(8,128)} %constant.77.clone.rho_ref, ...), custom_call_target="tpu_custom_call" | custom-call | flops 15032385536 | bytes 35651584 | tf_op jit(solution)/shard_map/nodes/pallas_call | solution.py:443
  347.6 9.1 %all-to-all-done.3.corner_ref = f32[256,16,128]{2,1,0:T(8,128)} async-done(((f32[256,16,128]{2,1,0:T(8,128)}), f32[256,16,128]{2,1,0:T(8,128)}, u32[]{:S(2)}, u32[]{:S(2)}) %all-to-all-start.3) | async-done | bytes 2097184 | tf_op jit(solution)/shard_map/all_to_all | solution.py:275
  356.6 4.5 all-to-all-start.4
  363.4 3.8 collective-permute-start.6
  367.2 41.5 %all-to-all-done.4.cubic_ref = f32[256,16,128]{2,1,0:T(8,128)S(1)} async-done(((f32[256,16,128]{2,1,0:T(8,128)}), f32[256,16,128]{2,1,0:T(8,128)S(1)}, u32[]{:S(2)}, u32[]{:S(2)}) %all-to-all-start.4) | async-done | bytes 2097184 | tf_op jit(solution)/shard_map/all_to_all | solution.py:275
  410.1 4.5 all-to-all-start.5
  415.8 2.7 slice_select_fusion.start_ref
  418.5 5.0 %low.1 = (f32[128,16,128]{2,1,0:T(8,128)}, f32[128,16,128]{2,1,0:T(8,128)}) custom-call(f32[32]{0:T(128)} %dynamic_slice.6.fine_ref, f32[16]{0:T(128)} %dynamic_slice.7.coarse_ref, bf16[256,768]{1,0:T(8,128)(2,1)} %constant.86.clone.table_ref, f32[256,128]{1,0:T(8,128)} %constant.87.clone.eigen_ref, f32[128,128]{1,0:T(8,128)} %constant.88.clone.coarse_eigen_ref, ...), custom_call_target="tpu_custom_call" | custom-call | flops 1073741824 | bytes 6291456 | tf_op jit(solution)/shard_map/low/pallas_call | solution.py:474
  423.5 4.2 offset.1
  429.0 3.6 collective-permute-done.7
  432.6 2.8 add_select_fusion
  437.6 11.1 %collective-permute-done.8 = f32[128,16,128]{2,1,0:T(8,128)} collective-permute-done((f32[128,16,128]{2,1,0:T(8,128)}, f32[128,16,128]{2,1,0:T(8,128)}, u32[]{:S(2)}, u32[]{:S(2)}) %collective-permute-start.8) | collective-permute-done | bytes 1048608 | tf_op jit(solution)/shard_map/ppermute | solution.py:498
  452.9 31.7 %all-to-all-done.5.refs_0_.refs_2_.refs_4_ = f32[8,16,16,384]{3,2,1,0:T(8,128)S(1)} async-done(((f32[8,16,16,384]{3,2,1,0:T(8,128)}), f32[8,16,16,384]{3,2,1,0:T(8,128)S(1)}, u32[]{:S(2)}, u32[]{:S(2)}) %all-to-all-start.5) | async-done | bytes 3145760 | tf_op jit(solution)/shard_map/all_to_all | solution.py:275
  486.2 11.7 %finish.1 = f32[256,32,256]{2,1,0:T(8,128)} custom-call(f32[32]{0:T(128)} %dynamic_slice.6.fine_ref, bf16[256,768]{1,0:T(8,128)(2,1)} %constant.86.clone.table_ref, f32[256,256]{1,0:T(8,128)} %constant.90.clone.eigen_ref, f32[128,16,128]{2,1,0:T(8,128)} %get-tuple-element.41.corner_ref, f32[128,16,128]{2,1,0:T(8,128)} %add_select_fusion.1.end_ref, ...), custom_call_target="tpu_custom_call" | custom-call | flops 2684354560 | bytes 18874368 | tf_op jit(solution)/shard_map/finish/pallas_call | solution.py:511
  (43 shorter events, 22.6 us)
Async XLA Ops:
  9.7 98.8 %all-to-all-start = ((f32[8,16,32,256]{3,2,1,0:T(8,128)}), f32[8,16,32,256]{3,2,1,0:T(8,128)}, u32[]{:S(2)}, u32[]{:S(2)}) async-start(f32[8,16,32,256]{3,2,1,0:T(8,128)} %depth.3), calls=%async_computation | async-start | bytes 8388608 | tf_op jit(solution)/shard_map/all_to_all | solution.py:275
  25.0 47.8 %collective-permute-start = (f32[8,16,32,256]{3,2,1,0:T(8,128)}, f32[8,16,32,256]{3,2,1,0:T(8,128)}, u32[]{:S(2)}, u32[]{:S(2)}) collective-permute-start(f32[8,16,32,256]{3,2,1,0:T(8,128)} %depth.2), channel_id=1, source_target_pairs={{0,8},{8,16},{16,24},{24,0},{1,9},{9,17},{17,25},{25,1},{2,10},{10... | collective-permute-start | bytes 12582920 | tf_op jit(solution)/shard_map/ppermute | solution.py:271
  108.5 96.4 %all-to-all-start.1 = ((f32[8,16,32,256]{3,2,1,0:T(8,128)}), f32[8,16,32,256]{3,2,1,0:T(8,128)}, u32[]{:S(2)}, u32[]{:S(2)}) async-start(f32[8,16,32,256]{3,2,1,0:T(8,128)} %collective-permute-done), calls=%async_computation.1 | async-start | bytes 8388608 | tf_op jit(solution)/shard_map/all_to_all | solution.py:275
  113.2 48.7 %collective-permute-start.1 = (f32[8,16,32,256]{3,2,1,0:T(8,128)}, f32[8,16,32,256]{3,2,1,0:T(8,128)S(1)}, u32[]{:S(2)}, u32[]{:S(2)}) collective-permute-start(f32[8,16,32,256]{3,2,1,0:T(8,128)} %all-to-all-done), channel_id=1, source_target_pairs={{0,8},{8,16},{16,24},{24,0},{1,9},{9,17},{17,25},{25,1},{2,10},{10... | collective-permute-start | bytes 12582920 | tf_op jit(solution)/shard_map/ppermute | solution.py:271
  161.8 2.3 copy-start.9
  204.9 82.6 %all-to-all-start.2 = ((f32[8,16,16,384]{3,2,1,0:T(8,128)}), f32[8,16,16,384]{3,2,1,0:T(8,128)S(1)}, u32[]{:S(2)}, u32[]{:S(2)}) async-start(f32[8,16,16,384]{3,2,1,0:T(8,128)} %get-tuple-element.34), calls=%async_computation.2 | async-start | bytes 6291456 | tf_op jit(solution)/shard_map/all_to_all | solution.py:275
  210.3 19.7 %copy-start.5 = (f32[2,256,256]{2,1,0:T(8,128)S(1)}, f32[2,256,256]{2,1,0:T(8,128)}, u32[]{:S(2)}) copy-start(f32[2,256,256]{2,1,0:T(8,128)} %constant.92) | copy-start | bytes 1572868
  210.3 74.8 %copy-start.6 = (f32[2,256,256]{2,1,0:T(8,128)S(1)}, f32[2,256,256]{2,1,0:T(8,128)}, u32[]{:S(2)}) copy-start(f32[2,256,256]{2,1,0:T(8,128)} %constant.80.clone) | copy-start | bytes 1572868
  210.3 74.8 %copy-start.7 = (f32[2,256,256]{2,1,0:T(8,128)S(1)}, f32[2,256,256]{2,1,0:T(8,128)}, u32[]{:S(2)}) copy-start(f32[2,256,256]{2,1,0:T(8,128)} %constant.81.clone) | copy-start | bytes 1572868
  231.3 29.4 %collective-permute-start.2 = (f32[2,256,256]{2,1,0:T(8,128)S(1)}, f32[2,256,256]{2,1,0:T(8,128)S(1)}, u32[]{:S(2)}, u32[]{:S(2)}) collective-permute-start(f32[2,256,256]{2,1,0:T(8,128)S(1)} %get-tuple-element.51), channel_id=1, source_target_pairs={{1,0},{2,1},{3,2},{4,3},{5,4},{6,5},{7,6},{9,8},{10,9},{11,10},{12... | collective-permute-start | bytes 1572872 | tf_op jit(solution)/shard_map/ppermute | solution.py:266
  232.6 52.5 %collective-permute-start.3 = (f32[2,256,256]{2,1,0:T(8,128)S(1)}, f32[2,256,256]{2,1,0:T(8,128)S(1)}, u32[]{:S(2)}, u32[]{:S(2)}) collective-permute-start(f32[2,256,256]{2,1,0:T(8,128)S(1)} %get-tuple-element.51), channel_id=1, source_target_pairs={{2,0},{3,1},{4,2},{5,3},{6,4},{7,5},{10,8},{11,9},{12,10},{13,11},... | collective-permute-start | bytes 1572872 | tf_op jit(solution)/shard_map/ppermute | solution.py:266
  233.9 51.2 %collective-permute-start.4 = (f32[2,256,256]{2,1,0:T(8,128)S(1)}, f32[2,256,256]{2,1,0:T(8,128)S(1)}, u32[]{:S(2)}, u32[]{:S(2)}) collective-permute-start(f32[2,256,256]{2,1,0:T(8,128)S(1)} %get-tuple-element.50), channel_id=1, source_target_pairs={{0,1},{1,2},{2,3},{3,4},{4,5},{5,6},{6,7},{8,9},{9,10},{10,11},{11... | collective-permute-start | bytes 1572872 | tf_op jit(solution)/shard_map/ppermute | solution.py:266
  238.0 47.1 %collective-permute-start.5 = (f32[2,256,256]{2,1,0:T(8,128)S(1)}, f32[2,256,256]{2,1,0:T(8,128)S(1)}, u32[]{:S(2)}, u32[]{:S(2)}) collective-permute-start(f32[2,256,256]{2,1,0:T(8,128)S(1)} %get-tuple-element.50), channel_id=1, source_target_pairs={{0,2},{1,3},{2,4},{3,5},{4,6},{5,7},{8,10},{9,11},{10,12},{11,13},... | collective-permute-start | bytes 1572872 | tf_op jit(solution)/shard_map/ppermute | solution.py:266
  287.6 60.0 %copy-start = (f32[8,16,16,384]{3,2,1,0:T(8,128)}, f32[8,16,16,384]{3,2,1,0:T(8,128)S(1)}, u32[]{:S(2)}) copy-start(f32[8,16,16,384]{3,2,1,0:T(8,128)S(1)} %all-to-all-done.2.refs_1_.refs_3_.refs_5_) | copy-start | bytes 9437188
  287.6 69.0 %all-to-all-start.3 = ((f32[256,16,128]{2,1,0:T(8,128)}), f32[256,16,128]{2,1,0:T(8,128)}, u32[]{:S(2)}, u32[]{:S(2)}) async-start(f32[256,16,128]{2,1,0:T(8,128)} %bitcast.9), calls=%async_computation.3 | async-start | bytes 4194304 | tf_op jit(solution)/shard_map/all_to_all | solution.py:275
  356.6 52.1 %all-to-all-start.4 = ((f32[256,16,128]{2,1,0:T(8,128)}), f32[256,16,128]{2,1,0:T(8,128)S(1)}, u32[]{:S(2)}, u32[]{:S(2)}) async-start(f32[256,16,128]{2,1,0:T(8,128)} %bitcast.11), calls=%async_computation.4 | async-start | bytes 4194304 | tf_op jit(solution)/shard_map/all_to_all | solution.py:275
  361.1 53.4 %copy-start.11 = (f32[128]{0:T(128)S(1)}, f32[128]{0:T(128)}, u32[]{:S(2)}) copy-start(f32[128]{0:T(128)} %constant.71.clone) | copy-start | bytes 1540
  361.1 54.1 %copy-start.10 = (f32[256]{0:T(256)S(1)}, f32[256]{0:T(256)}, u32[]{:S(2)}) copy-start(f32[256]{0:T(256)} %constant.70.clone) | copy-start | bytes 3076
  363.4 52.4 %collective-permute-start.6 = (f32[128,16,128]{2,1,0:T(8,128)}, f32[128,16,128]{2,1,0:T(8,128)}, u32[]{:S(2)}, u32[]{:S(2)}) collective-permute-start(f32[128,16,128]{2,1,0:T(8,128)} %slice_bitcast_fusion), channel_id=1, source_target_pairs={{0,8},{8,16},{16,24},{1,9},{9,17},{17,25},{2,10},{10,18},{18,26},{... | collective-permute-start | bytes 3145736 | tf_op jit(solution)/shard_map/ppermute | solution.py:266
  408.7 1.4 copy-start.3
  410.1 74.5 %all-to-all-start.5 = ((f32[8,16,16,384]{3,2,1,0:T(8,128)}), f32[8,16,16,384]{3,2,1,0:T(8,128)S(1)}, u32[]{:S(2)}, u32[]{:S(2)}) async-start(f32[8,16,16,384]{3,2,1,0:T(8,128)} %get-tuple-element.46), calls=%async_computation.5 | async-start | bytes 6291456 | tf_op jit(solution)/shard_map/all_to_all | solution.py:275
  418.5 14.1 %copy-start.4 = (f32[128,128]{1,0:T(8,128)S(1)}, f32[128,128]{1,0:T(8,128)}, u32[]{:S(2)}) copy-start(f32[128,128]{1,0:T(8,128)} %constant.93) | copy-start | bytes 196612
  418.5 14.1 %copy-start.8 = (f32[16]{0:T(128)S(1)}, f32[16]{0:T(128)}, u32[]{:S(2)}) copy-start(f32[16]{0:T(128)} %dynamic_slice.7.coarse_ref) | copy-start | bytes 196
  427.7 4.9 collective-permute-start.7
  435.3 13.3 %collective-permute-start.8 = (f32[128,16,128]{2,1,0:T(8,128)}, f32[128,16,128]{2,1,0:T(8,128)}, u32[]{:S(2)}, u32[]{:S(2)}) collective-permute-start(f32[128,16,128]{2,1,0:T(8,128)} %add_select_fusion), channel_id=1, source_target_pairs={{8,16},{9,17},{10,18},{11,19},{12,20},{13,21},{14,22},{15,23}} | collective-permute-start | bytes 3145736 | tf_op jit(solution)/shard_map/ppermute | solution.py:498
  437.6 14.0 %copy-start.2 = (f32[128,16,128]{2,1,0:T(8,128)S(1)}, f32[128,16,128]{2,1,0:T(8,128)}, u32[]{:S(2)}) copy-start(f32[128,16,128]{2,1,0:T(8,128)} %offset.1) | copy-start | bytes 3145732
  450.8 0.7 collective-permute-start.9
  484.6 1.6 copy-start.1

commit v6 on v5

--- a/solution.py
+++ b/solution.py
@@ -419,17 +419,21 @@
     _, to_right, to_left = state
     rest_last, backs[0] = after(rest_last, backs[0])
     rest_last_back = exchange(rest_last)
-    at_start, at_end = group_index == 0, group_index == groups - 1
-    if rounds <= 2:
-        rightward = jnp.where(at_start, to_right - rho_slab * (rho * to_left), to_right)
-        leftward = jnp.where(at_end, to_left - rho_slab * (rho * to_right), to_left)
-        from_left = shifted(rightward, "gx", 1) + rho_slab * shifted(rightward, "gx", 2)
-        from_right = shifted(leftward, "gx", -1) + rho_slab * shifted(leftward, "gx", -2)
-        from_left, from_right = (
-            jnp.where(at_start, -rho * (to_left + rho_slab * from_right), from_left),
-            jnp.where(at_end, -rho * (to_right + rho_slab * from_left), from_right),
-        )
+    if rounds <= 2 and groups % 2 == 0:
+        odd = group_index % 2 == 1
+        swap = [(i, i ^ 1) for i in range(groups)]
+        partner_right = lax.ppermute(to_right, "gx", swap)
+        partner_left = lax.ppermute(to_left, "gx", swap)
+        rightward = jnp.where(odd, to_right + rho_slab * partner_right, partner_right + rho_slab * to_right)
+        leftward = jnp.where(odd, partner_left + rho_slab * to_left, to_left + rho_slab * partner_left)
+        rightward, leftward = after(rightward, leftward)
+        before, behind = after(shifted(rightward, "gx", 2), shifted(leftward, "gx", -2))
+        before = jnp.where(group_index < 2, -rho * leftward, before)
+        behind = jnp.where(group_index >= groups - 2, -rho * rightward, behind)
+        from_left = jnp.where(odd, partner_right + rho_slab * before, before)
+        from_right = jnp.where(odd, behind, partner_left + rho_slab * behind)
     else:
+        at_start, at_end = group_index == 0, group_index == groups - 1
         from_left = jnp.zeros(pair, F32)
         from_right = jnp.zeros(pair, F32)
         for _ in range(rounds):

time: 501 us -> 496 us (0.990)
  starting transfers between devices: 70.3 us -> 56.1 us
  waiting for transfers between devices: 288 us -> 296 us
    ppermute x0 -> x2, waiting for transfers between devices: none -> 38.8 us  [the longest x1 27.1 us: per_device(): partner_right = lax.ppermute(to_right, 'gx', swap)]
    ppermute x5 -> x3, waiting for transfers between devices: 43.1 us -> 14 us  [shifted(): return lax.ppermute(value, axis, pairs)]
    all_to_all x6, starting transfers between devices: 46.7 us -> 37 us  [exchange(): return lax.all_to_all(value, 'gx', split_axis=0, concat_axis=0, tiled=True)]
    ppermute x5 -> x3, starting transfers between devices: 14.4 us -> 8.27 us  [shifted(): return lax.ppermute(value, axis, pairs)]
  transfers between devices with their start and end apart: 16 -> 16, of which waited for: 11 -> 13; matrix products, arithmetic and copies ran while one was open for 4% -> 4% of each run, Pallas kernels for 19% -> 19%
where the time goes in v6:
time: 496 us; the launch traced here: 494 us
  waiting for transfers between devices  296 us (60%)
  Pallas kernels  117 us (24%)
  starting transfers between devices  56.1 us (11%)
  other arithmetic  15 us (3%)
  local copies, waits for them, and re-layouts  8.94 us (2%)
    all_to_all x6, waiting for transfers between devices, exchange(): return lax.all_to_all(value, 'gx', split_axis=0, concat_axis=0, tiled=True)  137 us
    ppermute x2, waiting for transfers between devices, turned(): lax.ppermute(value, axis, [(i, (i + 1) % length) for i in range(length)])  91.5 us
    pallas_call x2, Pallas kernels, per_device(): call(functools.partial(start_kernel, planes), 'start', (steps,), [pl.Bloc...  39.3 us
    pallas_call x1, Pallas kernels, per_device(): call(functools.partial(node_kernel, planes, block), 'nodes', (block // pl...  38.6 us
    all_to_all x6, starting transfers between devices, exchange(): return lax.all_to_all(value, 'gx', split_axis=0, concat_axis=0, tiled=True)  37 us
    ppermute x1, waiting for transfers between devices, per_device(): partner_right = lax.ppermute(to_right, 'gx', swap)  27.1 us
    pallas_call x2, Pallas kernels, depth(): pl.pallas_call(depth_kernel, grid_spec=pltpu.PrefetchScalarGridSpec(num_s...  18 us
    ppermute x3, waiting for transfers between devices, per_device(): incoming = lax.ppermute(coarse_end, 'tm', [(turn - 1, turn)])  14.7 us
  transfers between devices with their start and end apart: 16, of which 13 were waited for; matrix products, arithmetic and copies ran while one was open for 4% of the time, Pallas kernels for 19%

profile of v6, /device:TPU:1, one launch (start us, length us, event | category | flops | bytes accessed | tf_op | source)
XLA Modules:
  0.0 493.8 jit_solution(18190926873128990206)
XLA Ops:
  0.6 9.0 %depth.3 = f32[8,16,32,256]{3,2,1,0:T(8,128)} custom-call(s32[1]{0:T(128)} %bitcast.last_ref, bf16[128,768]{1,0:T(8,128)(2,1)} %constant.82.clone.table_ref, f32[256,32,256]{2,1,0:T(8,128)} %initial_ref.3, f32[1,256,32,256]{3,2,1,0:T(8,128)} %end_ref.3), custom_call_target="tpu_custom_call" | custom-call | flops 3221225472 | bytes 16777216 | tf_op jit(solution)/shard_map/depth/pallas_call | solution.py:336
  9.7 6.4 %all-to-all-start = ((f32[8,16,32,256]{3,2,1,0:T(8,128)}), f32[8,16,32,256]{3,2,1,0:T(8,128)}, u32[]{:S(2)}, u32[]{:S(2)}) async-start(f32[8,16,32,256]{3,2,1,0:T(8,128)} %depth.3), calls=%async_computation | async-start | bytes 8388608 | tf_op jit(solution)/shard_map/all_to_all | solution.py:275
  16.0 9.0 %depth.2 = f32[8,16,32,256]{3,2,1,0:T(8,128)} custom-call(s32[1]{0:T(128)} %bitcast.last_ref, bf16[128,768]{1,0:T(8,128)(2,1)} %constant.81.clone.table_ref, f32[256,32,256]{2,1,0:T(8,128)} %initial_ref.3, f32[1,256,32,256]{3,2,1,0:T(8,128)} %end_ref.3), custom_call_target="tpu_custom_call" | custom-call | flops 3221225472 | bytes 16777216 | tf_op jit(solution)/shard_map/depth/pallas_call | solution.py:336
  27.1 45.8 %collective-permute-done = f32[8,16,32,256]{3,2,1,0:T(8,128)} collective-permute-done((f32[8,16,32,256]{3,2,1,0:T(8,128)}, f32[8,16,32,256]{3,2,1,0:T(8,128)}, u32[]{:S(2)}, u32[]{:S(2)}) %collective-permute-start) | collective-permute-done | bytes 4194336 | tf_op jit(solution)/shard_map/ppermute | solution.py:271
  72.8 35.6 %all-to-all-done = f32[8,16,32,256]{3,2,1,0:T(8,128)} async-done(((f32[8,16,32,256]{3,2,1,0:T(8,128)}), f32[8,16,32,256]{3,2,1,0:T(8,128)}, u32[]{:S(2)}, u32[]{:S(2)}) %all-to-all-start) | async-done | bytes 4194336 | tf_op jit(solution)/shard_map/all_to_all | solution.py:275
  108.5 4.7 all-to-all-start.1
  113.1 2.9 collective-permute-start.1
  116.0 45.8 %collective-permute-done.1.modes_ref = f32[8,16,32,256]{3,2,1,0:T(8,128)S(1)} collective-permute-done((f32[8,16,32,256]{3,2,1,0:T(8,128)}, f32[8,16,32,256]{3,2,1,0:T(8,128)S(1)}, u32[]{:S(2)}, u32[]{:S(2)}) %collective-permute-start.1) | collective-permute-done | bytes 4194336 | tf_op jit(solution)/shard_map/ppermute | solution.py:271
  164.2 19.7 %start.2 = (f32[8,32,16,128]{3,2,1,0:T(8,128)}, f32[8,16,16,384]{3,2,1,0:T(8,128)}, f32[4,32,256,256]{3,2,1,0:T(8,128)}, f32[2,256,256]{2,1,0:T(8,128)}, f32[2,256,256]{2,1,0:T(8,128)}, /*index=5*/f32[2,256,256]{2,1,0:T(8,128)}) custom-call(f32[8,16,32,256]{3,2,1,0:T(8,128)} %copy-done.6, bf16[768,256]{1,0:T(8,128)(2,1)} %constant.83.clone.sx_ref, ...), custom_call_target="tpu_custom_call" | custom-call | flops 6442450944 | bytes 25165824 | tf_op jit(solution)/shard_map/start/pallas_call | solution.py:391
  183.9 21.0 %all-to-all-done.1.modes_ref = f32[8,16,32,256]{3,2,1,0:T(8,128)} async-done(((f32[8,16,32,256]{3,2,1,0:T(8,128)}), f32[8,16,32,256]{3,2,1,0:T(8,128)}, u32[]{:S(2)}, u32[]{:S(2)}) %all-to-all-start.1) | async-done | bytes 4194336 | tf_op jit(solution)/shard_map/all_to_all | solution.py:275
  204.9 5.3 %all-to-all-start.2 = ((f32[8,16,16,384]{3,2,1,0:T(8,128)}), f32[8,16,16,384]{3,2,1,0:T(8,128)S(1)}, u32[]{:S(2)}, u32[]{:S(2)}) async-start(f32[8,16,16,384]{3,2,1,0:T(8,128)} %get-tuple-element.38), calls=%async_computation.2 | async-start | bytes 6291456 | tf_op jit(solution)/shard_map/all_to_all | solution.py:275
  210.3 19.5 %start.3 = (f32[8,32,16,128]{3,2,1,0:T(8,128)}, f32[8,16,16,384]{3,2,1,0:T(8,128)}, f32[4,32,256,256]{3,2,1,0:T(8,128)}, f32[2,256,256]{2,1,0:T(8,128)}, f32[2,256,256]{2,1,0:T(8,128)}, /*index=5*/f32[2,256,256]{2,1,0:T(8,128)}) custom-call(f32[8,16,32,256]{3,2,1,0:T(8,128)} %all-to-all-done.1.modes_ref, ...), custom_call_target="tpu_custom_call", output_to_operand_aliasing={{0}: (8, {}), {2}: (9, {})} | custom-call | flops 6442450944 | bytes 25165824 | tf_op jit(solution)/shard_map/start/pallas_call | solution.py:391
  231.4 27.1 %collective-permute-done.2 = f32[2,256,256]{2,1,0:T(8,128)} collective-permute-done((f32[2,256,256]{2,1,0:T(8,128)}, f32[2,256,256]{2,1,0:T(8,128)}, u32[]{:S(2)}, u32[]{:S(2)}) %collective-permute-start.2) | collective-permute-done | bytes 524320 | tf_op jit(solution)/shard_map/ppermute | solution.py:425
  258.5 11.8 %collective-permute-done.3 = f32[2,256,256]{2,1,0:T(8,128)} collective-permute-done((f32[2,256,256]{2,1,0:T(8,128)}, f32[2,256,256]{2,1,0:T(8,128)}, u32[]{:S(2)}, u32[]{:S(2)}) %collective-permute-start.3) | collective-permute-done | bytes 524320 | tf_op jit(solution)/shard_map/ppermute | solution.py:426
  270.3 2.9 add_select_fusion.5
  276.5 8.6 %collective-permute-done.4 = f32[2,256,256]{2,1,0:T(8,128)} collective-permute-done((f32[2,256,256]{2,1,0:T(8,128)}, f32[2,256,256]{2,1,0:T(8,128)}, u32[]{:S(2)}, u32[]{:S(2)}) %collective-permute-start.4) | collective-permute-done | bytes 524320 | tf_op jit(solution)/shard_map/ppermute | solution.py:266
  285.1 5.4 %collective-permute-done.5 = f32[2,256,256]{2,1,0:T(8,128)} collective-permute-done((f32[2,256,256]{2,1,0:T(8,128)}, f32[2,256,256]{2,1,0:T(8,128)}, u32[]{:S(2)}, u32[]{:S(2)}) %collective-permute-start.5) | collective-permute-done | bytes 524320 | tf_op jit(solution)/shard_map/ppermute | solution.py:266
  290.5 3.2 add_select_fusion.3
  293.7 11.1 %all-to-all-start.3 = ((f32[256,16,128]{2,1,0:T(8,128)}), f32[256,16,128]{2,1,0:T(8,128)}, u32[]{:S(2)}, u32[]{:S(2)}) async-start(f32[256,16,128]{2,1,0:T(8,128)} %bitcast.9), calls=%async_computation.3 | async-start | bytes 4194304 | tf_op jit(solution)/shard_map/all_to_all | solution.py:275
  304.8 38.6 %nodes.1 = f32[8,32,16,128]{3,2,1,0:T(8,128)} custom-call(f32[4,32,256,256]{3,2,1,0:T(8,128)} %get-tuple-element.35.v_ref, f32[2,256,256]{2,1,0:T(8,128)} %get-tuple-element.45.from_left_ref, f32[2,256,256]{2,1,0:T(8,128)} %get-tuple-element.46.from_right_ref, f32[2,256,256]{2,1,0:T(8,128)} %constant.86.clone.rho_ref, ...), custom_call_target="tpu_custom_call" | custom-call | flops 15032385536 | bytes 35651584 | tf_op jit(solution)/shard_map/nodes/pallas_call | solution.py:447
  343.4 9.6 %all-to-all-done.3.corner_ref = f32[256,16,128]{2,1,0:T(8,128)} async-done(((f32[256,16,128]{2,1,0:T(8,128)}), f32[256,16,128]{2,1,0:T(8,128)}, u32[]{:S(2)}, u32[]{:S(2)}) %all-to-all-start.3) | async-done | bytes 2097184 | tf_op jit(solution)/shard_map/all_to_all | solution.py:275
  353.0 4.0 all-to-all-start.4
  359.3 4.9 collective-permute-start.6
  364.3 39.3 %all-to-all-done.4.cubic_ref = f32[256,16,128]{2,1,0:T(8,128)S(1)} async-done(((f32[256,16,128]{2,1,0:T(8,128)}), f32[256,16,128]{2,1,0:T(8,128)S(1)}, u32[]{:S(2)}, u32[]{:S(2)}) %all-to-all-start.4) | async-done | bytes 2097184 | tf_op jit(solution)/shard_map/all_to_all | solution.py:275
  404.9 5.5 %all-to-all-start.5 = ((f32[8,16,16,384]{3,2,1,0:T(8,128)}), f32[8,16,16,384]{3,2,1,0:T(8,128)S(1)}, u32[]{:S(2)}, u32[]{:S(2)}) async-start(f32[8,16,16,384]{3,2,1,0:T(8,128)} %get-tuple-element.54), calls=%async_computation.5 | async-start | bytes 6291456 | tf_op jit(solution)/shard_map/all_to_all | solution.py:275
  414.4 5.1 %low.1 = (f32[128,16,128]{2,1,0:T(8,128)}, f32[128,16,128]{2,1,0:T(8,128)}) custom-call(f32[32]{0:T(128)} %dynamic_slice.6.fine_ref, f32[16]{0:T(128)} %dynamic_slice.7.coarse_ref, bf16[256,768]{1,0:T(8,128)(2,1)} %constant.95.clone.table_ref, f32[256,128]{1,0:T(8,128)} %constant.96.clone.eigen_ref, f32[128,128]{1,0:T(8,128)} %constant.97.clone.coarse_eigen_ref, ...), custom_call_target="tpu_custom_call" | custom-call | flops 1073741824 | bytes 6291456 | tf_op jit(solution)/shard_map/low/pallas_call | solution.py:478
  419.4 4.2 offset.1
  424.9 3.6 collective-permute-done.7
  428.5 2.8 add_select_fusion
  433.5 11.1 %collective-permute-done.8 = f32[128,16,128]{2,1,0:T(8,128)} collective-permute-done((f32[128,16,128]{2,1,0:T(8,128)}, f32[128,16,128]{2,1,0:T(8,128)}, u32[]{:S(2)}, u32[]{:S(2)}) %collective-permute-start.8) | collective-permute-done | bytes 1048608 | tf_op jit(solution)/shard_map/ppermute | solution.py:502
  448.8 31.7 %all-to-all-done.5.refs_0_.refs_2_.refs_4_ = f32[8,16,16,384]{3,2,1,0:T(8,128)S(1)} async-done(((f32[8,16,16,384]{3,2,1,0:T(8,128)}), f32[8,16,16,384]{3,2,1,0:T(8,128)S(1)}, u32[]{:S(2)}, u32[]{:S(2)}) %all-to-all-start.5) | async-done | bytes 3145760 | tf_op jit(solution)/shard_map/all_to_all | solution.py:275
  482.1 11.7 %finish.1 = f32[256,32,256]{2,1,0:T(8,128)} custom-call(f32[32]{0:T(128)} %dynamic_slice.6.fine_ref, bf16[256,768]{1,0:T(8,128)(2,1)} %constant.95.clone.table_ref, f32[256,256]{1,0:T(8,128)} %constant.99.clone.eigen_ref, f32[128,16,128]{2,1,0:T(8,128)} %get-tuple-element.49.corner_ref, f32[128,16,128]{2,1,0:T(8,128)} %add_select_fusion.1.end_ref, ...), custom_call_target="tpu_custom_call" | custom-call | flops 2684354560 | bytes 18874368 | tf_op jit(solution)/shard_map/finish/pallas_call | solution.py:515
  (37 shorter events, 26.4 us)
Async XLA Ops:
  9.7 98.8 %all-to-all-start = ((f32[8,16,32,256]{3,2,1,0:T(8,128)}), f32[8,16,32,256]{3,2,1,0:T(8,128)}, u32[]{:S(2)}, u32[]{:S(2)}) async-start(f32[8,16,32,256]{3,2,1,0:T(8,128)} %depth.3), calls=%async_computation | async-start | bytes 8388608 | tf_op jit(solution)/shard_map/all_to_all | solution.py:275
  25.0 47.8 %collective-permute-start = (f32[8,16,32,256]{3,2,1,0:T(8,128)}, f32[8,16,32,256]{3,2,1,0:T(8,128)}, u32[]{:S(2)}, u32[]{:S(2)}) collective-permute-start(f32[8,16,32,256]{3,2,1,0:T(8,128)} %depth.2), channel_id=1, source_target_pairs={{0,8},{8,16},{16,24},{24,0},{1,9},{9,17},{17,25},{25,1},{2,10},{10... | collective-permute-start | bytes 12582920 | tf_op jit(solution)/shard_map/ppermute | solution.py:271
  108.5 96.5 %all-to-all-start.1 = ((f32[8,16,32,256]{3,2,1,0:T(8,128)}), f32[8,16,32,256]{3,2,1,0:T(8,128)}, u32[]{:S(2)}, u32[]{:S(2)}) async-start(f32[8,16,32,256]{3,2,1,0:T(8,128)} %collective-permute-done), calls=%async_computation.1 | async-start | bytes 8388608 | tf_op jit(solution)/shard_map/all_to_all | solution.py:275
  113.1 48.6 %collective-permute-start.1 = (f32[8,16,32,256]{3,2,1,0:T(8,128)}, f32[8,16,32,256]{3,2,1,0:T(8,128)S(1)}, u32[]{:S(2)}, u32[]{:S(2)}) collective-permute-start(f32[8,16,32,256]{3,2,1,0:T(8,128)} %all-to-all-done), channel_id=1, source_target_pairs={{0,8},{8,16},{16,24},{24,0},{1,9},{9,17},{17,25},{25,1},{2,10},{10... | collective-permute-start | bytes 12582920 | tf_op jit(solution)/shard_map/ppermute | solution.py:271
  161.8 2.4 copy-start.6
  204.9 88.8 %all-to-all-start.2 = ((f32[8,16,16,384]{3,2,1,0:T(8,128)}), f32[8,16,16,384]{3,2,1,0:T(8,128)S(1)}, u32[]{:S(2)}, u32[]{:S(2)}) async-start(f32[8,16,16,384]{3,2,1,0:T(8,128)} %get-tuple-element.38), calls=%async_computation.2 | async-start | bytes 6291456 | tf_op jit(solution)/shard_map/all_to_all | solution.py:275
  229.8 28.7 %collective-permute-start.2 = (f32[2,256,256]{2,1,0:T(8,128)}, f32[2,256,256]{2,1,0:T(8,128)}, u32[]{:S(2)}, u32[]{:S(2)}) collective-permute-start(f32[2,256,256]{2,1,0:T(8,128)} %get-tuple-element.39), channel_id=1, source_target_pairs={{0,1},{1,0},{2,3},{3,2},{4,5},{5,4},{6,7},{7,6},{8,9},{9,8},{10,11... | collective-permute-start | bytes 1572872 | tf_op jit(solution)/shard_map/ppermute | solution.py:425
  231.3 38.9 %collective-permute-start.3 = (f32[2,256,256]{2,1,0:T(8,128)}, f32[2,256,256]{2,1,0:T(8,128)}, u32[]{:S(2)}, u32[]{:S(2)}) collective-permute-start(f32[2,256,256]{2,1,0:T(8,128)} %get-tuple-element.40), channel_id=1, source_target_pairs={{0,1},{1,0},{2,3},{3,2},{4,5},{5,4},{6,7},{7,6},{8,9},{9,8},{10,11... | collective-permute-start | bytes 1572872 | tf_op jit(solution)/shard_map/ppermute | solution.py:426
  273.1 12.0 %collective-permute-start.4 = (f32[2,256,256]{2,1,0:T(8,128)}, f32[2,256,256]{2,1,0:T(8,128)}, u32[]{:S(2)}, u32[]{:S(2)}) collective-permute-start(f32[2,256,256]{2,1,0:T(8,128)} %get-tuple-element.42), channel_id=1, source_target_pairs={{0,2},{1,3},{2,4},{3,5},{4,6},{5,7},{8,10},{9,11},{10,12},{11,13},... | collective-permute-start | bytes 1572872 | tf_op jit(solution)/shard_map/ppermute | solution.py:266
  275.2 15.3 %collective-permute-start.5 = (f32[2,256,256]{2,1,0:T(8,128)}, f32[2,256,256]{2,1,0:T(8,128)}, u32[]{:S(2)}, u32[]{:S(2)}) collective-permute-start(f32[2,256,256]{2,1,0:T(8,128)} %get-tuple-element.41), channel_id=1, source_target_pairs={{2,0},{3,1},{4,2},{5,3},{6,4},{7,5},{10,8},{11,9},{12,10},{13,11},... | collective-permute-start | bytes 1572872 | tf_op jit(solution)/shard_map/ppermute | solution.py:266
  293.7 49.7 %copy-start = (f32[8,16,16,384]{3,2,1,0:T(8,128)}, f32[8,16,16,384]{3,2,1,0:T(8,128)S(1)}, u32[]{:S(2)}) copy-start(f32[8,16,16,384]{3,2,1,0:T(8,128)S(1)} %all-to-all-done.2.refs_1_.refs_3_.refs_5_) | copy-start | bytes 9437188
  293.7 59.3 %all-to-all-start.3 = ((f32[256,16,128]{2,1,0:T(8,128)}), f32[256,16,128]{2,1,0:T(8,128)}, u32[]{:S(2)}, u32[]{:S(2)}) async-start(f32[256,16,128]{2,1,0:T(8,128)} %bitcast.9), calls=%async_computation.3 | async-start | bytes 4194304 | tf_op jit(solution)/shard_map/all_to_all | solution.py:275
  353.0 50.5 %all-to-all-start.4 = ((f32[256,16,128]{2,1,0:T(8,128)}), f32[256,16,128]{2,1,0:T(8,128)S(1)}, u32[]{:S(2)}, u32[]{:S(2)}) async-start(f32[256,16,128]{2,1,0:T(8,128)} %bitcast.11), calls=%async_computation.4 | async-start | bytes 4194304 | tf_op jit(solution)/shard_map/all_to_all | solution.py:275
  357.0 53.4 %copy-start.8 = (f32[128]{0:T(128)S(1)}, f32[128]{0:T(128)}, u32[]{:S(2)}) copy-start(f32[128]{0:T(128)} %constant.80.clone) | copy-start | bytes 1540
  357.0 54.0 %copy-start.7 = (f32[256]{0:T(256)S(1)}, f32[256]{0:T(256)}, u32[]{:S(2)}) copy-start(f32[256]{0:T(256)} %constant.79.clone) | copy-start | bytes 3076
  359.3 52.3 %collective-permute-start.6 = (f32[128,16,128]{2,1,0:T(8,128)}, f32[128,16,128]{2,1,0:T(8,128)}, u32[]{:S(2)}, u32[]{:S(2)}) collective-permute-start(f32[128,16,128]{2,1,0:T(8,128)} %slice_bitcast_fusion), channel_id=1, source_target_pairs={{0,8},{8,16},{16,24},{1,9},{9,17},{17,25},{2,10},{10,18},{18,26},{... | collective-permute-start | bytes 3145736 | tf_op jit(solution)/shard_map/ppermute | solution.py:266
  403.5 1.3 copy-start.3
  404.9 75.6 %all-to-all-start.5 = ((f32[8,16,16,384]{3,2,1,0:T(8,128)}), f32[8,16,16,384]{3,2,1,0:T(8,128)S(1)}, u32[]{:S(2)}, u32[]{:S(2)}) async-start(f32[8,16,16,384]{3,2,1,0:T(8,128)} %get-tuple-element.54), calls=%async_computation.5 | async-start | bytes 6291456 | tf_op jit(solution)/shard_map/all_to_all | solution.py:275
  414.4 14.1 %copy-start.4 = (f32[128,128]{1,0:T(8,128)S(1)}, f32[128,128]{1,0:T(8,128)}, u32[]{:S(2)}) copy-start(f32[128,128]{1,0:T(8,128)} %constant.101) | copy-start | bytes 196612
  414.4 14.1 %copy-start.5 = (f32[16]{0:T(128)S(1)}, f32[16]{0:T(128)}, u32[]{:S(2)}) copy-start(f32[16]{0:T(128)} %dynamic_slice.7.coarse_ref) | copy-start | bytes 196
  423.6 4.9 collective-permute-start.7
  431.2 13.3 %collective-permute-start.8 = (f32[128,16,128]{2,1,0:T(8,128)}, f32[128,16,128]{2,1,0:T(8,128)}, u32[]{:S(2)}, u32[]{:S(2)}) collective-permute-start(f32[128,16,128]{2,1,0:T(8,128)} %add_select_fusion), channel_id=1, source_target_pairs={{8,16},{9,17},{10,18},{11,19},{12,20},{13,21},{14,22},{15,23}} | collective-permute-start | bytes 3145736 | tf_op jit(solution)/shard_map/ppermute | solution.py:502
  433.5 14.0 %copy-start.2 = (f32[128,16,128]{2,1,0:T(8,128)S(1)}, f32[128,16,128]{2,1,0:T(8,128)}, u32[]{:S(2)}) copy-start(f32[128,16,128]{2,1,0:T(8,128)} %offset.1) | copy-start | bytes 3145732
  446.7 0.7 collective-permute-start.9
  480.5 1.6 copy-start.1

commit v7 on v6

--- a/solution.py
+++ b/solution.py
@@ -285,7 +285,7 @@
     groups = lax.axis_size("gx")
     block = grid // groups
     half = block // 2
-    planes = 4
+    planes = 2
     slice_index = lax.axis_index("tm")
     group_index = lax.axis_index("gx")
     is_first = slice_index == 0
@@ -325,8 +325,9 @@
 
     rows_spec = pl.BlockSpec((grid, ROWS, grid), lambda i: (0, i, 0))
     table_spec = whole_block(depth_table.shape)
-    lengths = (block // 2, block - block // 2)
-    begins = (0, block // 2)
+    shorter = 7 * block // 16 // planes * planes
+    lengths = (shorter, block - shorter)
+    begins = (0, shorter)
     parts = len(lengths)
     end_begin = begins[1]
 

time: 496 us -> 492 us (level)
  Pallas kernels: 117 us -> 125 us
  starting transfers between devices: 56.1 us -> 48.1 us
    all_to_all x6, waiting for transfers between devices: 137 us -> 122 us  [exchange(): return lax.all_to_all(value, 'gx', split_axis=0, concat_axis=0, tiled=True)]
    ppermute x1, waiting for transfers between devices: 11.8 us -> 19.7 us  [per_device(): partner_left = lax.ppermute(to_left, 'gx', swap)]
    ppermute x3, waiting for transfers between devices: 14 us -> 21.2 us  [shifted(): return lax.ppermute(value, axis, pairs)]
    all_to_all x6, starting transfers between devices: 37 us -> 30.2 us  [exchange(): return lax.all_to_all(value, 'gx', split_axis=0, concat_axis=0, tiled=True)]
  transfers between devices with their start and end apart: 16 -> 16, of which waited for: 13 -> 13; matrix products, arithmetic and copies ran while one was open for 4% -> 4% of each run, Pallas kernels for 19% -> 21%
where the time goes in v7:
time: 492 us; the launch traced here: 489 us
  waiting for transfers between devices  292 us (59%)
  Pallas kernels  125 us (25%)
  starting transfers between devices  48.1 us (10%)
  other arithmetic  15 us (3%)
  local copies, waits for them, and re-layouts  8.99 us (2%)
    all_to_all x6, waiting for transfers between devices, exchange(): return lax.all_to_all(value, 'gx', split_axis=0, concat_axis=0, tiled=True)  122 us
    ppermute x2, waiting for transfers between devices, turned(): lax.ppermute(value, axis, [(i, (i + 1) % length) for i in range(length)])  91.5 us
    pallas_call x1, Pallas kernels, per_device(): call(functools.partial(node_kernel, planes, block), 'nodes', (block // pl...  43 us
    pallas_call x2, Pallas kernels, per_device(): call(functools.partial(start_kernel, planes), 'start', (steps,), [pl.Bloc...  42.6 us
    all_to_all x6, starting transfers between devices, exchange(): return lax.all_to_all(value, 'gx', split_axis=0, concat_axis=0, tiled=True)  30.2 us
    ppermute x1, waiting for transfers between devices, per_device(): partner_right = lax.ppermute(to_right, 'gx', swap)  23.1 us
    ppermute x3, waiting for transfers between devices, shifted(): return lax.ppermute(value, axis, pairs)  21.2 us
    ppermute x1, waiting for transfers between devices, per_device(): partner_left = lax.ppermute(to_left, 'gx', swap)  19.7 us
  transfers between devices with their start and end apart: 16, of which 13 were waited for; matrix products, arithmetic and copies ran while one was open for 4% of the time, Pallas kernels for 21%

profile of v7, /device:TPU:1, one launch (start us, length us, event | category | flops | bytes accessed | tf_op | source)
XLA Modules:
  0.0 489.3 jit_solution(5817005059648102595)
XLA Ops:
  0.6 9.1 %depth.3 = f32[8,18,32,256]{3,2,1,0:T(8,128)} custom-call(s32[1]{0:T(128)} %bitcast.last_ref, bf16[144,768]{1,0:T(8,128)(2,1)} %constant.82.clone.table_ref, f32[256,32,256]{2,1,0:T(8,128)} %initial_ref.3, f32[1,256,32,256]{3,2,1,0:T(8,128)} %end_ref.3), custom_call_target="tpu_custom_call" | custom-call | flops 3221225472 | bytes 16777216 | tf_op jit(solution)/shard_map/depth/pallas_call | solution.py:337
  9.7 6.4 %all-to-all-start = ((f32[8,18,32,256]{3,2,1,0:T(8,128)}), f32[8,18,32,256]{3,2,1,0:T(8,128)}, u32[]{:S(2)}, u32[]{:S(2)}) async-start(f32[8,18,32,256]{3,2,1,0:T(8,128)} %depth.3), calls=%async_computation | async-start | bytes 9437184 | tf_op jit(solution)/shard_map/all_to_all | solution.py:275
  16.1 8.9 %depth.2 = f32[8,14,32,256]{3,2,1,0:T(8,128)} custom-call(s32[1]{0:T(128)} %bitcast.last_ref, bf16[112,768]{1,0:T(8,128)(2,1)} %constant.81.clone.table_ref, f32[256,32,256]{2,1,0:T(8,128)} %initial_ref.3, f32[1,256,32,256]{3,2,1,0:T(8,128)} %end_ref.3), custom_call_target="tpu_custom_call" | custom-call | flops 3221225472 | bytes 16777216 | tf_op jit(solution)/shard_map/depth/pallas_call | solution.py:337
  27.1 40.1 %collective-permute-done = f32[8,14,32,256]{3,2,1,0:T(8,128)} collective-permute-done((f32[8,14,32,256]{3,2,1,0:T(8,128)}, f32[8,14,32,256]{3,2,1,0:T(8,128)}, u32[]{:S(2)}, u32[]{:S(2)}) %collective-permute-start) | collective-permute-done | bytes 3670048 | tf_op jit(solution)/shard_map/ppermute | solution.py:271
  67.2 52.5 %all-to-all-done = f32[8,18,32,256]{3,2,1,0:T(8,128)} async-done(((f32[8,18,32,256]{3,2,1,0:T(8,128)}), f32[8,18,32,256]{3,2,1,0:T(8,128)}, u32[]{:S(2)}, u32[]{:S(2)}) %all-to-all-start) | async-done | bytes 4718624 | tf_op jit(solution)/shard_map/all_to_all | solution.py:275
  119.8 4.7 all-to-all-start.1
  124.4 2.8 collective-permute-start.1
  127.3 51.4 %collective-permute-done.1.modes_ref = f32[8,18,32,256]{3,2,1,0:T(8,128)S(1)} collective-permute-done((f32[8,18,32,256]{3,2,1,0:T(8,128)}, f32[8,18,32,256]{3,2,1,0:T(8,128)S(1)}, u32[]{:S(2)}, u32[]{:S(2)}) %collective-permute-start.1) | collective-permute-done | bytes 4718624 | tf_op jit(solution)/shard_map/ppermute | solution.py:271
  181.2 23.5 %start.2 = (f32[8,32,16,128]{3,2,1,0:T(8,128)}, f32[8,18,16,384]{3,2,1,0:T(8,128)}, f32[4,32,256,256]{3,2,1,0:T(8,128)}, f32[2,256,256]{2,1,0:T(8,128)}, f32[2,256,256]{2,1,0:T(8,128)}, /*index=5*/f32[2,256,256]{2,1,0:T(8,128)}) custom-call(f32[8,18,32,256]{3,2,1,0:T(8,128)} %copy-done.6, bf16[768,256]{1,0:T(8,128)(2,1)} %constant.83.clone.sx_ref, ...), custom_call_target="tpu_custom_call" | custom-call | flops 7247757312 | bytes 28311552 | tf_op jit(solution)/shard_map/start/pallas_call | solution.py:392
  205.0 5.3 %all-to-all-start.2 = ((f32[8,18,16,384]{3,2,1,0:T(8,128)}), f32[8,18,16,384]{3,2,1,0:T(8,128)S(1)}, u32[]{:S(2)}, u32[]{:S(2)}) async-start(f32[8,18,16,384]{3,2,1,0:T(8,128)} %get-tuple-element.38), calls=%async_computation.2 | async-start | bytes 7077888 | tf_op jit(solution)/shard_map/all_to_all | solution.py:275
  210.3 19.1 %start.3 = (f32[8,32,16,128]{3,2,1,0:T(8,128)}, f32[8,14,16,384]{3,2,1,0:T(8,128)}, f32[4,32,256,256]{3,2,1,0:T(8,128)}, f32[2,256,256]{2,1,0:T(8,128)}, f32[2,256,256]{2,1,0:T(8,128)}, /*index=5*/f32[2,256,256]{2,1,0:T(8,128)}) custom-call(f32[8,14,32,256]{3,2,1,0:T(8,128)} %all-to-all-done.1.modes_ref, ...), custom_call_target="tpu_custom_call", output_to_operand_aliasing={{0}: (8, {}), {2}: (9, {})} | custom-call | flops 5637144576 | bytes 22020096 | tf_op jit(solution)/shard_map/start/pallas_call | solution.py:392
  231.0 23.1 %collective-permute-done.2 = f32[2,256,256]{2,1,0:T(8,128)} collective-permute-done((f32[2,256,256]{2,1,0:T(8,128)}, f32[2,256,256]{2,1,0:T(8,128)}, u32[]{:S(2)}, u32[]{:S(2)}) %collective-permute-start.2) | collective-permute-done | bytes 524320 | tf_op jit(solution)/shard_map/ppermute | solution.py:426
  254.1 19.7 %collective-permute-done.3 = f32[2,256,256]{2,1,0:T(8,128)} collective-permute-done((f32[2,256,256]{2,1,0:T(8,128)}, f32[2,256,256]{2,1,0:T(8,128)}, u32[]{:S(2)}, u32[]{:S(2)}) %collective-permute-start.3) | collective-permute-done | bytes 524320 | tf_op jit(solution)/shard_map/ppermute | solution.py:427
  273.8 2.9 add_select_fusion.5
  280.0 8.6 %collective-permute-done.4 = f32[2,256,256]{2,1,0:T(8,128)} collective-permute-done((f32[2,256,256]{2,1,0:T(8,128)}, f32[2,256,256]{2,1,0:T(8,128)}, u32[]{:S(2)}, u32[]{:S(2)}) %collective-permute-start.4) | collective-permute-done | bytes 524320 | tf_op jit(solution)/shard_map/ppermute | solution.py:266
  288.6 12.6 %collective-permute-done.5 = f32[2,256,256]{2,1,0:T(8,128)} collective-permute-done((f32[2,256,256]{2,1,0:T(8,128)}, f32[2,256,256]{2,1,0:T(8,128)}, u32[]{:S(2)}, u32[]{:S(2)}) %collective-permute-start.5) | collective-permute-done | bytes 524320 | tf_op jit(solution)/shard_map/ppermute | solution.py:266
  301.3 3.2 add_select_fusion.3
  304.5 4.4 all-to-all-start.3
  308.9 43.0 %nodes.1 = f32[8,32,16,128]{3,2,1,0:T(8,128)} custom-call(f32[4,32,256,256]{3,2,1,0:T(8,128)} %get-tuple-element.35.v_ref, f32[2,256,256]{2,1,0:T(8,128)} %get-tuple-element.45.from_left_ref, f32[2,256,256]{2,1,0:T(8,128)} %get-tuple-element.46.from_right_ref, f32[2,256,256]{2,1,0:T(8,128)} %constant.86.clone.rho_ref, ...), custom_call_target="tpu_custom_call" | custom-call | flops 15032385536 | bytes 35651584 | tf_op jit(solution)/shard_map/nodes/pallas_call | solution.py:448
  351.9 4.0 all-to-all-done.3.corner_ref
  355.9 5.0 %all-to-all-start.4 = ((f32[256,16,128]{2,1,0:T(8,128)}), f32[256,16,128]{2,1,0:T(8,128)S(1)}, u32[]{:S(2)}, u32[]{:S(2)}) async-start(f32[256,16,128]{2,1,0:T(8,128)} %bitcast.11), calls=%async_computation.4 | async-start | bytes 4194304 | tf_op jit(solution)/shard_map/all_to_all | solution.py:275
  363.2 3.8 collective-permute-start.6
  367.0 41.5 %all-to-all-done.4.cubic_ref = f32[256,16,128]{2,1,0:T(8,128)S(1)} async-done(((f32[256,16,128]{2,1,0:T(8,128)}), f32[256,16,128]{2,1,0:T(8,128)S(1)}, u32[]{:S(2)}, u32[]{:S(2)}) %all-to-all-start.4) | async-done | bytes 2097184 | tf_op jit(solution)/shard_map/all_to_all | solution.py:275
  409.8 4.5 all-to-all-start.5
  415.6 2.7 slice_select_fusion.start_ref
  418.3 5.0 %low.1 = (f32[128,16,128]{2,1,0:T(8,128)}, f32[128,16,128]{2,1,0:T(8,128)}) custom-call(f32[32]{0:T(128)} %dynamic_slice.6.fine_ref, f32[16]{0:T(128)} %dynamic_slice.7.coarse_ref, bf16[256,768]{1,0:T(8,128)(2,1)} %constant.95.clone.table_ref, f32[256,128]{1,0:T(8,128)} %constant.96.clone.eigen_ref, f32[128,128]{1,0:T(8,128)} %constant.97.clone.coarse_eigen_ref, ...), custom_call_target="tpu_custom_call" | custom-call | flops 1073741824 | bytes 6291456 | tf_op jit(solution)/shard_map/low/pallas_call | solution.py:479
  423.3 4.2 offset.1
  428.8 3.6 collective-permute-done.7
  432.4 2.8 add_select_fusion
  437.4 11.1 %collective-permute-done.8 = f32[128,16,128]{2,1,0:T(8,128)} collective-permute-done((f32[128,16,128]{2,1,0:T(8,128)}, f32[128,16,128]{2,1,0:T(8,128)}, u32[]{:S(2)}, u32[]{:S(2)}) %collective-permute-start.8) | collective-permute-done | bytes 1048608 | tf_op jit(solution)/shard_map/ppermute | solution.py:503
  452.7 23.3 %all-to-all-done.5.refs_0_.refs_2_.refs_4_ = f32[8,14,16,384]{3,2,1,0:T(8,128)S(1)} async-done(((f32[8,14,16,384]{3,2,1,0:T(8,128)}), f32[8,14,16,384]{3,2,1,0:T(8,128)S(1)}, u32[]{:S(2)}, u32[]{:S(2)}) %all-to-all-start.5) | async-done | bytes 2752544 | tf_op jit(solution)/shard_map/all_to_all | solution.py:275
  477.5 11.8 %finish.1 = f32[256,32,256]{2,1,0:T(8,128)} custom-call(f32[32]{0:T(128)} %dynamic_slice.6.fine_ref, bf16[256,768]{1,0:T(8,128)(2,1)} %constant.95.clone.table_ref, f32[256,256]{1,0:T(8,128)} %constant.99.clone.eigen_ref, f32[128,16,128]{2,1,0:T(8,128)} %get-tuple-element.49.corner_ref, f32[128,16,128]{2,1,0:T(8,128)} %add_select_fusion.1.end_ref, ...), custom_call_target="tpu_custom_call" | custom-call | flops 2684354560 | bytes 18874368 | tf_op jit(solution)/shard_map/finish/pallas_call | solution.py:516
  (37 shorter events, 24.2 us)
Async XLA Ops:
  9.7 110.0 %all-to-all-start = ((f32[8,18,32,256]{3,2,1,0:T(8,128)}), f32[8,18,32,256]{3,2,1,0:T(8,128)}, u32[]{:S(2)}, u32[]{:S(2)}) async-start(f32[8,18,32,256]{3,2,1,0:T(8,128)} %depth.3), calls=%async_computation | async-start | bytes 9437184 | tf_op jit(solution)/shard_map/all_to_all | solution.py:275
  25.0 42.2 %collective-permute-start = (f32[8,14,32,256]{3,2,1,0:T(8,128)}, f32[8,14,32,256]{3,2,1,0:T(8,128)}, u32[]{:S(2)}, u32[]{:S(2)}) collective-permute-start(f32[8,14,32,256]{3,2,1,0:T(8,128)} %depth.2), channel_id=1, source_target_pairs={{0,8},{8,16},{16,24},{24,0},{1,9},{9,17},{17,25},{25,1},{2,10},{10... | collective-permute-start | bytes 11010056 | tf_op jit(solution)/shard_map/ppermute | solution.py:271
  119.8 85.3 %all-to-all-start.1 = ((f32[8,14,32,256]{3,2,1,0:T(8,128)}), f32[8,14,32,256]{3,2,1,0:T(8,128)}, u32[]{:S(2)}, u32[]{:S(2)}) async-start(f32[8,14,32,256]{3,2,1,0:T(8,128)} %collective-permute-done), calls=%async_computation.1 | async-start | bytes 7340032 | tf_op jit(solution)/shard_map/all_to_all | solution.py:275
  124.4 54.2 %collective-permute-start.1 = (f32[8,18,32,256]{3,2,1,0:T(8,128)}, f32[8,18,32,256]{3,2,1,0:T(8,128)S(1)}, u32[]{:S(2)}, u32[]{:S(2)}) collective-permute-start(f32[8,18,32,256]{3,2,1,0:T(8,128)} %all-to-all-done), channel_id=1, source_target_pairs={{0,8},{8,16},{16,24},{24,0},{1,9},{9,17},{17,25},{25,1},{2,10},{10... | collective-permute-start | bytes 14155784 | tf_op jit(solution)/shard_map/ppermute | solution.py:271
  178.7 2.5 copy-start.6
  205.0 99.5 %all-to-all-start.2 = ((f32[8,18,16,384]{3,2,1,0:T(8,128)}), f32[8,18,16,384]{3,2,1,0:T(8,128)S(1)}, u32[]{:S(2)}, u32[]{:S(2)}) async-start(f32[8,18,16,384]{3,2,1,0:T(8,128)} %get-tuple-element.38), calls=%async_computation.2 | async-start | bytes 7077888 | tf_op jit(solution)/shard_map/all_to_all | solution.py:275
  229.4 24.7 %collective-permute-start.2 = (f32[2,256,256]{2,1,0:T(8,128)}, f32[2,256,256]{2,1,0:T(8,128)}, u32[]{:S(2)}, u32[]{:S(2)}) collective-permute-start(f32[2,256,256]{2,1,0:T(8,128)} %get-tuple-element.39), channel_id=1, source_target_pairs={{0,1},{1,0},{2,3},{3,2},{4,5},{5,4},{6,7},{7,6},{8,9},{9,8},{10,11... | collective-permute-start | bytes 1572872 | tf_op jit(solution)/shard_map/ppermute | solution.py:426
  230.9 42.9 %collective-permute-start.3 = (f32[2,256,256]{2,1,0:T(8,128)}, f32[2,256,256]{2,1,0:T(8,128)}, u32[]{:S(2)}, u32[]{:S(2)}) collective-permute-start(f32[2,256,256]{2,1,0:T(8,128)} %get-tuple-element.40), channel_id=1, source_target_pairs={{0,1},{1,0},{2,3},{3,2},{4,5},{5,4},{6,7},{7,6},{8,9},{9,8},{10,11... | collective-permute-start | bytes 1572872 | tf_op jit(solution)/shard_map/ppermute | solution.py:427
  276.7 11.9 %collective-permute-start.4 = (f32[2,256,256]{2,1,0:T(8,128)}, f32[2,256,256]{2,1,0:T(8,128)}, u32[]{:S(2)}, u32[]{:S(2)}) collective-permute-start(f32[2,256,256]{2,1,0:T(8,128)} %get-tuple-element.42), channel_id=1, source_target_pairs={{0,2},{1,3},{2,4},{3,5},{4,6},{5,7},{8,10},{9,11},{10,12},{11,13},... | collective-permute-start | bytes 1572872 | tf_op jit(solution)/shard_map/ppermute | solution.py:266
  278.8 22.5 %collective-permute-start.5 = (f32[2,256,256]{2,1,0:T(8,128)}, f32[2,256,256]{2,1,0:T(8,128)}, u32[]{:S(2)}, u32[]{:S(2)}) collective-permute-start(f32[2,256,256]{2,1,0:T(8,128)} %get-tuple-element.41), channel_id=1, source_target_pairs={{2,0},{3,1},{4,2},{5,3},{6,4},{7,5},{10,8},{11,9},{12,10},{13,11},... | collective-permute-start | bytes 1572872 | tf_op jit(solution)/shard_map/ppermute | solution.py:266
  304.5 47.4 %copy-start = (f32[8,18,16,384]{3,2,1,0:T(8,128)}, f32[8,18,16,384]{3,2,1,0:T(8,128)S(1)}, u32[]{:S(2)}) copy-start(f32[8,18,16,384]{3,2,1,0:T(8,128)S(1)} %all-to-all-done.2.refs_1_.refs_3_.refs_5_) | copy-start | bytes 10616836
  304.5 51.4 %all-to-all-start.3 = ((f32[256,16,128]{2,1,0:T(8,128)}), f32[256,16,128]{2,1,0:T(8,128)}, u32[]{:S(2)}, u32[]{:S(2)}) async-start(f32[256,16,128]{2,1,0:T(8,128)} %bitcast.9), calls=%async_computation.3 | async-start | bytes 4194304 | tf_op jit(solution)/shard_map/all_to_all | solution.py:275
  355.9 52.6 %all-to-all-start.4 = ((f32[256,16,128]{2,1,0:T(8,128)}), f32[256,16,128]{2,1,0:T(8,128)S(1)}, u32[]{:S(2)}, u32[]{:S(2)}) async-start(f32[256,16,128]{2,1,0:T(8,128)} %bitcast.11), calls=%async_computation.4 | async-start | bytes 4194304 | tf_op jit(solution)/shard_map/all_to_all | solution.py:275
  360.9 53.4 %copy-start.8 = (f32[128]{0:T(128)S(1)}, f32[128]{0:T(128)}, u32[]{:S(2)}) copy-start(f32[128]{0:T(128)} %constant.80.clone) | copy-start | bytes 1540
  360.9 54.1 %copy-start.7 = (f32[256]{0:T(256)S(1)}, f32[256]{0:T(256)}, u32[]{:S(2)}) copy-start(f32[256]{0:T(256)} %constant.79.clone) | copy-start | bytes 3076
  363.2 52.4 %collective-permute-start.6 = (f32[128,16,128]{2,1,0:T(8,128)}, f32[128,16,128]{2,1,0:T(8,128)}, u32[]{:S(2)}, u32[]{:S(2)}) collective-permute-start(f32[128,16,128]{2,1,0:T(8,128)} %slice_bitcast_fusion), channel_id=1, source_target_pairs={{0,8},{8,16},{16,24},{1,9},{9,17},{17,25},{2,10},{10,18},{18,26},{... | collective-permute-start | bytes 3145736 | tf_op jit(solution)/shard_map/ppermute | solution.py:266
  408.5 1.3 copy-start.3
  409.8 66.2 %all-to-all-start.5 = ((f32[8,14,16,384]{3,2,1,0:T(8,128)}), f32[8,14,16,384]{3,2,1,0:T(8,128)S(1)}, u32[]{:S(2)}, u32[]{:S(2)}) async-start(f32[8,14,16,384]{3,2,1,0:T(8,128)} %get-tuple-element.54), calls=%async_computation.5 | async-start | bytes 5505024 | tf_op jit(solution)/shard_map/all_to_all | solution.py:275
  423.3 9.1 %copy-start.4 = (f32[128,128]{1,0:T(8,128)S(1)}, f32[128,128]{1,0:T(8,128)}, u32[]{:S(2)}) copy-start(f32[128,128]{1,0:T(8,128)} %constant.101) | copy-start | bytes 196612
  423.3 9.1 %copy-start.5 = (f32[16]{0:T(128)S(1)}, f32[16]{0:T(128)}, u32[]{:S(2)}) copy-start(f32[16]{0:T(128)} %dynamic_slice.7.coarse_ref) | copy-start | bytes 196
  427.5 4.9 collective-permute-start.7
  435.2 13.3 %collective-permute-start.8 = (f32[128,16,128]{2,1,0:T(8,128)}, f32[128,16,128]{2,1,0:T(8,128)}, u32[]{:S(2)}, u32[]{:S(2)}) collective-permute-start(f32[128,16,128]{2,1,0:T(8,128)} %add_select_fusion), channel_id=1, source_target_pairs={{8,16},{9,17},{10,18},{11,19},{12,20},{13,21},{14,22},{15,23}} | collective-permute-start | bytes 3145736 | tf_op jit(solution)/shard_map/ppermute | solution.py:503
  437.4 14.0 %copy-start.2 = (f32[128,16,128]{2,1,0:T(8,128)S(1)}, f32[128,16,128]{2,1,0:T(8,128)}, u32[]{:S(2)}) copy-start(f32[128,16,128]{2,1,0:T(8,128)} %offset.1) | copy-start | bytes 3145732
  450.6 0.7 collective-permute-start.9
  476.0 1.5 copy-start.1

commit v8 on v7

--- a/solution.py
+++ b/solution.py
@@ -445,11 +445,12 @@
 
     corner, rest_last_back, from_left, from_right = after(corner, rest_last_back, from_left, from_right)
     corner_back = exchange(corner.reshape(grid, half, coarse))
+    node_planes = 2 * planes
     cubic = call(
-        functools.partial(node_kernel, planes, block),
+        functools.partial(node_kernel, node_planes, block),
         "nodes",
-        (block // planes,),
-        [pl.BlockSpec((4, planes, grid, grid), lambda i: (0, i, 0, 0))]
+        (block // node_planes,),
+        [pl.BlockSpec((4, node_planes, grid, grid), lambda i: (0, i, 0, 0))]
         + [pair_spec] * 5
         + [
             whole_block(x_table.shape),
@@ -457,9 +458,9 @@
             whole_block(x_low_table.shape),
             whole_block(low_table.shape),
         ],
-        pl.BlockSpec((groups, planes, half, coarse), lambda i: (0, i, 0, 0)),
+        pl.BlockSpec((groups, node_planes, half, coarse), lambda i: (0, i, 0, 0)),
         jax.ShapeDtypeStruct((groups, block, half, coarse), F32),
-        scratch=[pltpu.VMEM(pair, F32), pltpu.VMEM(pair, F32), pltpu.VMEM((2, planes, grid, grid), F32)],
+        scratch=[pltpu.VMEM(pair, F32), pltpu.VMEM(pair, F32), pltpu.VMEM((2, node_planes, grid, grid), F32)],
         flops=28 * unit * grid,
         moved=17 * unit,
     )(v, from_left, from_right, rho, inverse, kappa, x_table, y_table, x_low_table, low_table)

time: 492 us -> 492 us (level)
  Pallas kernels: 125 us -> 120 us
  transfers between devices with their start and end apart: 16 -> 16, of which waited for: 13 -> 13; matrix products, arithmetic and copies ran while one was open for 4% -> 4% of each run, Pallas kernels for 21% -> 20%
where the time goes in v8:
time: 492 us; the launch traced here: 489 us
  waiting for transfers between devices  296 us (60%)
  Pallas kernels  120 us (24%)
  starting transfers between devices  48.3 us (10%)
  other arithmetic  15 us (3%)
  local copies, waits for them, and re-layouts  8.99 us (2%)
    all_to_all x6, waiting for transfers between devices, exchange(): return lax.all_to_all(value, 'gx', split_axis=0, concat_axis=0, tiled=True)  126 us
    ppermute x2, waiting for transfers between devices, turned(): lax.ppermute(value, axis, [(i, (i + 1) % length) for i in range(length)])  91.5 us
    pallas_call x2, Pallas kernels, per_device(): call(functools.partial(start_kernel, planes), 'start', (steps,), [pl.Bloc...  42.6 us
    pallas_call x1, Pallas kernels, per_device(): call(functools.partial(node_kernel, node_planes, block), 'nodes', (block...  38.6 us
    all_to_all x6, starting transfers between devices, exchange(): return lax.all_to_all(value, 'gx', split_axis=0, concat_axis=0, tiled=True)  30.4 us
    ppermute x1, waiting for transfers between devices, per_device(): partner_right = lax.ppermute(to_right, 'gx', swap)  23.1 us
    ppermute x3, waiting for transfers between devices, shifted(): return lax.ppermute(value, axis, pairs)  21.2 us
    ppermute x1, waiting for transfers between devices, per_device(): partner_left = lax.ppermute(to_left, 'gx', swap)  19.7 us
  transfers between devices with their start and end apart: 16, of which 13 were waited for; matrix products, arithmetic and copies ran while one was open for 4% of the time, Pallas kernels for 20%

profile of v8, /device:TPU:1, one launch (start us, length us, event | category | flops | bytes accessed | tf_op | source)
XLA Modules:
  0.0 489.4 jit_solution(1881006798847661073)
XLA Ops:
  0.6 9.1 %depth.3 = f32[8,18,32,256]{3,2,1,0:T(8,128)} custom-call(s32[1]{0:T(128)} %bitcast.last_ref, bf16[144,768]{1,0:T(8,128)(2,1)} %constant.82.clone.table_ref, f32[256,32,256]{2,1,0:T(8,128)} %initial_ref.3, f32[1,256,32,256]{3,2,1,0:T(8,128)} %end_ref.3), custom_call_target="tpu_custom_call" | custom-call | flops 3221225472 | bytes 16777216 | tf_op jit(solution)/shard_map/depth/pallas_call | solution.py:337
  9.7 6.4 %all-to-all-start = ((f32[8,18,32,256]{3,2,1,0:T(8,128)}), f32[8,18,32,256]{3,2,1,0:T(8,128)}, u32[]{:S(2)}, u32[]{:S(2)}) async-start(f32[8,18,32,256]{3,2,1,0:T(8,128)} %depth.3), calls=%async_computation | async-start | bytes 9437184 | tf_op jit(solution)/shard_map/all_to_all | solution.py:275
  16.1 8.9 %depth.2 = f32[8,14,32,256]{3,2,1,0:T(8,128)} custom-call(s32[1]{0:T(128)} %bitcast.last_ref, bf16[112,768]{1,0:T(8,128)(2,1)} %constant.81.clone.table_ref, f32[256,32,256]{2,1,0:T(8,128)} %initial_ref.3, f32[1,256,32,256]{3,2,1,0:T(8,128)} %end_ref.3), custom_call_target="tpu_custom_call" | custom-call | flops 3221225472 | bytes 16777216 | tf_op jit(solution)/shard_map/depth/pallas_call | solution.py:337
  27.1 40.1 %collective-permute-done = f32[8,14,32,256]{3,2,1,0:T(8,128)} collective-permute-done((f32[8,14,32,256]{3,2,1,0:T(8,128)}, f32[8,14,32,256]{3,2,1,0:T(8,128)}, u32[]{:S(2)}, u32[]{:S(2)}) %collective-permute-start) | collective-permute-done | bytes 3670048 | tf_op jit(solution)/shard_map/ppermute | solution.py:271
  67.2 52.5 %all-to-all-done = f32[8,18,32,256]{3,2,1,0:T(8,128)} async-done(((f32[8,18,32,256]{3,2,1,0:T(8,128)}), f32[8,18,32,256]{3,2,1,0:T(8,128)}, u32[]{:S(2)}, u32[]{:S(2)}) %all-to-all-start) | async-done | bytes 4718624 | tf_op jit(solution)/shard_map/all_to_all | solution.py:275
  119.8 4.7 all-to-all-start.1
  124.4 2.8 collective-permute-start.1
  127.3 51.4 %collective-permute-done.1.modes_ref = f32[8,18,32,256]{3,2,1,0:T(8,128)S(1)} collective-permute-done((f32[8,18,32,256]{3,2,1,0:T(8,128)}, f32[8,18,32,256]{3,2,1,0:T(8,128)S(1)}, u32[]{:S(2)}, u32[]{:S(2)}) %collective-permute-start.1) | collective-permute-done | bytes 4718624 | tf_op jit(solution)/shard_map/ppermute | solution.py:271
  181.2 23.5 %start.2 = (f32[8,32,16,128]{3,2,1,0:T(8,128)}, f32[8,18,16,384]{3,2,1,0:T(8,128)}, f32[4,32,256,256]{3,2,1,0:T(8,128)}, f32[2,256,256]{2,1,0:T(8,128)}, f32[2,256,256]{2,1,0:T(8,128)}, /*index=5*/f32[2,256,256]{2,1,0:T(8,128)}) custom-call(f32[8,18,32,256]{3,2,1,0:T(8,128)} %copy-done.6, bf16[768,256]{1,0:T(8,128)(2,1)} %constant.83.clone.sx_ref, ...), custom_call_target="tpu_custom_call" | custom-call | flops 7247757312 | bytes 28311552 | tf_op jit(solution)/shard_map/start/pallas_call | solution.py:392
  205.0 5.3 %all-to-all-start.2 = ((f32[8,18,16,384]{3,2,1,0:T(8,128)}), f32[8,18,16,384]{3,2,1,0:T(8,128)S(1)}, u32[]{:S(2)}, u32[]{:S(2)}) async-start(f32[8,18,16,384]{3,2,1,0:T(8,128)} %get-tuple-element.38), calls=%async_computation.2 | async-start | bytes 7077888 | tf_op jit(solution)/shard_map/all_to_all | solution.py:275
  210.3 19.1 %start.3 = (f32[8,32,16,128]{3,2,1,0:T(8,128)}, f32[8,14,16,384]{3,2,1,0:T(8,128)}, f32[4,32,256,256]{3,2,1,0:T(8,128)}, f32[2,256,256]{2,1,0:T(8,128)}, f32[2,256,256]{2,1,0:T(8,128)}, /*index=5*/f32[2,256,256]{2,1,0:T(8,128)}) custom-call(f32[8,14,32,256]{3,2,1,0:T(8,128)} %all-to-all-done.1.modes_ref, ...), custom_call_target="tpu_custom_call", output_to_operand_aliasing={{0}: (8, {}), {2}: (9, {})} | custom-call | flops 5637144576 | bytes 22020096 | tf_op jit(solution)/shard_map/start/pallas_call | solution.py:392
  231.0 23.1 %collective-permute-done.2 = f32[2,256,256]{2,1,0:T(8,128)} collective-permute-done((f32[2,256,256]{2,1,0:T(8,128)}, f32[2,256,256]{2,1,0:T(8,128)}, u32[]{:S(2)}, u32[]{:S(2)}) %collective-permute-start.2) | collective-permute-done | bytes 524320 | tf_op jit(solution)/shard_map/ppermute | solution.py:426
  254.1 19.7 %collective-permute-done.3 = f32[2,256,256]{2,1,0:T(8,128)} collective-permute-done((f32[2,256,256]{2,1,0:T(8,128)}, f32[2,256,256]{2,1,0:T(8,128)}, u32[]{:S(2)}, u32[]{:S(2)}) %collective-permute-start.3) | collective-permute-done | bytes 524320 | tf_op jit(solution)/shard_map/ppermute | solution.py:427
  273.8 2.9 add_select_fusion.5
  280.0 8.6 %collective-permute-done.4 = f32[2,256,256]{2,1,0:T(8,128)} collective-permute-done((f32[2,256,256]{2,1,0:T(8,128)}, f32[2,256,256]{2,1,0:T(8,128)}, u32[]{:S(2)}, u32[]{:S(2)}) %collective-permute-start.4) | collective-permute-done | bytes 524320 | tf_op jit(solution)/shard_map/ppermute | solution.py:266
  288.6 12.6 %collective-permute-done.5 = f32[2,256,256]{2,1,0:T(8,128)} collective-permute-done((f32[2,256,256]{2,1,0:T(8,128)}, f32[2,256,256]{2,1,0:T(8,128)}, u32[]{:S(2)}, u32[]{:S(2)}) %collective-permute-start.5) | collective-permute-done | bytes 524320 | tf_op jit(solution)/shard_map/ppermute | solution.py:266
  301.3 3.2 add_select_fusion.3
  304.5 4.4 all-to-all-start.3
  308.9 38.6 %nodes.1 = f32[8,32,16,128]{3,2,1,0:T(8,128)} custom-call(f32[4,32,256,256]{3,2,1,0:T(8,128)} %get-tuple-element.35.v_ref, f32[2,256,256]{2,1,0:T(8,128)} %get-tuple-element.45.from_left_ref, f32[2,256,256]{2,1,0:T(8,128)} %get-tuple-element.46.from_right_ref, f32[2,256,256]{2,1,0:T(8,128)} %constant.86.clone.rho_ref, ...), custom_call_target="tpu_custom_call" | custom-call | flops 15032385536 | bytes 35651584 | tf_op jit(solution)/shard_map/nodes/pallas_call | solution.py:449
  347.5 8.4 %all-to-all-done.3.corner_ref = f32[256,16,128]{2,1,0:T(8,128)} async-done(((f32[256,16,128]{2,1,0:T(8,128)}), f32[256,16,128]{2,1,0:T(8,128)}, u32[]{:S(2)}, u32[]{:S(2)}) %all-to-all-start.3) | async-done | bytes 2097184 | tf_op jit(solution)/shard_map/all_to_all | solution.py:275
  355.9 5.0 %all-to-all-start.4 = ((f32[256,16,128]{2,1,0:T(8,128)}), f32[256,16,128]{2,1,0:T(8,128)S(1)}, u32[]{:S(2)}, u32[]{:S(2)}) async-start(f32[256,16,128]{2,1,0:T(8,128)} %bitcast.11), calls=%async_computation.4 | async-start | bytes 4194304 | tf_op jit(solution)/shard_map/all_to_all | solution.py:275
  363.2 3.8 collective-permute-start.6
  367.0 41.5 %all-to-all-done.4.cubic_ref = f32[256,16,128]{2,1,0:T(8,128)S(1)} async-done(((f32[256,16,128]{2,1,0:T(8,128)}), f32[256,16,128]{2,1,0:T(8,128)S(1)}, u32[]{:S(2)}, u32[]{:S(2)}) %all-to-all-start.4) | async-done | bytes 2097184 | tf_op jit(solution)/shard_map/all_to_all | solution.py:275
  409.8 4.7 all-to-all-start.5
  415.8 2.7 slice_select_fusion.start_ref
  418.5 5.0 %low.1 = (f32[128,16,128]{2,1,0:T(8,128)}, f32[128,16,128]{2,1,0:T(8,128)}) custom-call(f32[32]{0:T(128)} %dynamic_slice.6.fine_ref, f32[16]{0:T(128)} %dynamic_slice.7.coarse_ref, bf16[256,768]{1,0:T(8,128)(2,1)} %constant.95.clone.table_ref, f32[256,128]{1,0:T(8,128)} %constant.96.clone.eigen_ref, f32[128,128]{1,0:T(8,128)} %constant.97.clone.coarse_eigen_ref, ...), custom_call_target="tpu_custom_call" | custom-call | flops 1073741824 | bytes 6291456 | tf_op jit(solution)/shard_map/low/pallas_call | solution.py:480
  423.5 4.2 offset.1
  429.0 3.6 collective-permute-done.7
  432.6 2.8 add_select_fusion
  437.6 11.1 %collective-permute-done.8 = f32[128,16,128]{2,1,0:T(8,128)} collective-permute-done((f32[128,16,128]{2,1,0:T(8,128)}, f32[128,16,128]{2,1,0:T(8,128)}, u32[]{:S(2)}, u32[]{:S(2)}) %collective-permute-start.8) | collective-permute-done | bytes 1048608 | tf_op jit(solution)/shard_map/ppermute | solution.py:504
  452.9 23.2 %all-to-all-done.5.refs_0_.refs_2_.refs_4_ = f32[8,14,16,384]{3,2,1,0:T(8,128)S(1)} async-done(((f32[8,14,16,384]{3,2,1,0:T(8,128)}), f32[8,14,16,384]{3,2,1,0:T(8,128)S(1)}, u32[]{:S(2)}, u32[]{:S(2)}) %all-to-all-start.5) | async-done | bytes 2752544 | tf_op jit(solution)/shard_map/all_to_all | solution.py:275
  477.6 11.8 %finish.1 = f32[256,32,256]{2,1,0:T(8,128)} custom-call(f32[32]{0:T(128)} %dynamic_slice.6.fine_ref, bf16[256,768]{1,0:T(8,128)(2,1)} %constant.95.clone.table_ref, f32[256,256]{1,0:T(8,128)} %constant.99.clone.eigen_ref, f32[128,16,128]{2,1,0:T(8,128)} %get-tuple-element.49.corner_ref, f32[128,16,128]{2,1,0:T(8,128)} %add_select_fusion.1.end_ref, ...), custom_call_target="tpu_custom_call" | custom-call | flops 2684354560 | bytes 18874368 | tf_op jit(solution)/shard_map/finish/pallas_call | solution.py:517
  (37 shorter events, 24.2 us)
Async XLA Ops:
  9.7 110.0 %all-to-all-start = ((f32[8,18,32,256]{3,2,1,0:T(8,128)}), f32[8,18,32,256]{3,2,1,0:T(8,128)}, u32[]{:S(2)}, u32[]{:S(2)}) async-start(f32[8,18,32,256]{3,2,1,0:T(8,128)} %depth.3), calls=%async_computation | async-start | bytes 9437184 | tf_op jit(solution)/shard_map/all_to_all | solution.py:275
  25.0 42.2 %collective-permute-start = (f32[8,14,32,256]{3,2,1,0:T(8,128)}, f32[8,14,32,256]{3,2,1,0:T(8,128)}, u32[]{:S(2)}, u32[]{:S(2)}) collective-permute-start(f32[8,14,32,256]{3,2,1,0:T(8,128)} %depth.2), channel_id=1, source_target_pairs={{0,8},{8,16},{16,24},{24,0},{1,9},{9,17},{17,25},{25,1},{2,10},{10... | collective-permute-start | bytes 11010056 | tf_op jit(solution)/shard_map/ppermute | solution.py:271
  119.8 85.3 %all-to-all-start.1 = ((f32[8,14,32,256]{3,2,1,0:T(8,128)}), f32[8,14,32,256]{3,2,1,0:T(8,128)}, u32[]{:S(2)}, u32[]{:S(2)}) async-start(f32[8,14,32,256]{3,2,1,0:T(8,128)} %collective-permute-done), calls=%async_computation.1 | async-start | bytes 7340032 | tf_op jit(solution)/shard_map/all_to_all | solution.py:275
  124.4 54.2 %collective-permute-start.1 = (f32[8,18,32,256]{3,2,1,0:T(8,128)}, f32[8,18,32,256]{3,2,1,0:T(8,128)S(1)}, u32[]{:S(2)}, u32[]{:S(2)}) collective-permute-start(f32[8,18,32,256]{3,2,1,0:T(8,128)} %all-to-all-done), channel_id=1, source_target_pairs={{0,8},{8,16},{16,24},{24,0},{1,9},{9,17},{17,25},{25,1},{2,10},{10... | collective-permute-start | bytes 14155784 | tf_op jit(solution)/shard_map/ppermute | solution.py:271
  178.7 2.5 copy-start.6
  205.0 99.5 %all-to-all-start.2 = ((f32[8,18,16,384]{3,2,1,0:T(8,128)}), f32[8,18,16,384]{3,2,1,0:T(8,128)S(1)}, u32[]{:S(2)}, u32[]{:S(2)}) async-start(f32[8,18,16,384]{3,2,1,0:T(8,128)} %get-tuple-element.38), calls=%async_computation.2 | async-start | bytes 7077888 | tf_op jit(solution)/shard_map/all_to_all | solution.py:275
  229.4 24.7 %collective-permute-start.2 = (f32[2,256,256]{2,1,0:T(8,128)}, f32[2,256,256]{2,1,0:T(8,128)}, u32[]{:S(2)}, u32[]{:S(2)}) collective-permute-start(f32[2,256,256]{2,1,0:T(8,128)} %get-tuple-element.39), channel_id=1, source_target_pairs={{0,1},{1,0},{2,3},{3,2},{4,5},{5,4},{6,7},{7,6},{8,9},{9,8},{10,11... | collective-permute-start | bytes 1572872 | tf_op jit(solution)/shard_map/ppermute | solution.py:426
  230.9 42.9 %collective-permute-start.3 = (f32[2,256,256]{2,1,0:T(8,128)}, f32[2,256,256]{2,1,0:T(8,128)}, u32[]{:S(2)}, u32[]{:S(2)}) collective-permute-start(f32[2,256,256]{2,1,0:T(8,128)} %get-tuple-element.40), channel_id=1, source_target_pairs={{0,1},{1,0},{2,3},{3,2},{4,5},{5,4},{6,7},{7,6},{8,9},{9,8},{10,11... | collective-permute-start | bytes 1572872 | tf_op jit(solution)/shard_map/ppermute | solution.py:427
  276.7 11.9 %collective-permute-start.4 = (f32[2,256,256]{2,1,0:T(8,128)}, f32[2,256,256]{2,1,0:T(8,128)}, u32[]{:S(2)}, u32[]{:S(2)}) collective-permute-start(f32[2,256,256]{2,1,0:T(8,128)} %get-tuple-element.42), channel_id=1, source_target_pairs={{0,2},{1,3},{2,4},{3,5},{4,6},{5,7},{8,10},{9,11},{10,12},{11,13},... | collective-permute-start | bytes 1572872 | tf_op jit(solution)/shard_map/ppermute | solution.py:266
  278.8 22.5 %collective-permute-start.5 = (f32[2,256,256]{2,1,0:T(8,128)}, f32[2,256,256]{2,1,0:T(8,128)}, u32[]{:S(2)}, u32[]{:S(2)}) collective-permute-start(f32[2,256,256]{2,1,0:T(8,128)} %get-tuple-element.41), channel_id=1, source_target_pairs={{2,0},{3,1},{4,2},{5,3},{6,4},{7,5},{10,8},{11,9},{12,10},{13,11},... | collective-permute-start | bytes 1572872 | tf_op jit(solution)/shard_map/ppermute | solution.py:266
  304.5 43.0 %copy-start = (f32[8,18,16,384]{3,2,1,0:T(8,128)}, f32[8,18,16,384]{3,2,1,0:T(8,128)S(1)}, u32[]{:S(2)}) copy-start(f32[8,18,16,384]{3,2,1,0:T(8,128)S(1)} %all-to-all-done.2.refs_1_.refs_3_.refs_5_) | copy-start | bytes 10616836
  304.5 51.4 %all-to-all-start.3 = ((f32[256,16,128]{2,1,0:T(8,128)}), f32[256,16,128]{2,1,0:T(8,128)}, u32[]{:S(2)}, u32[]{:S(2)}) async-start(f32[256,16,128]{2,1,0:T(8,128)} %bitcast.9), calls=%async_computation.3 | async-start | bytes 4194304 | tf_op jit(solution)/shard_map/all_to_all | solution.py:275
  355.9 52.6 %all-to-all-start.4 = ((f32[256,16,128]{2,1,0:T(8,128)}), f32[256,16,128]{2,1,0:T(8,128)S(1)}, u32[]{:S(2)}, u32[]{:S(2)}) async-start(f32[256,16,128]{2,1,0:T(8,128)} %bitcast.11), calls=%async_computation.4 | async-start | bytes 4194304 | tf_op jit(solution)/shard_map/all_to_all | solution.py:275
  360.9 53.6 %copy-start.8 = (f32[128]{0:T(128)S(1)}, f32[128]{0:T(128)}, u32[]{:S(2)}) copy-start(f32[128]{0:T(128)} %constant.80.clone) | copy-start | bytes 1540
  360.9 54.2 %copy-start.7 = (f32[256]{0:T(256)S(1)}, f32[256]{0:T(256)}, u32[]{:S(2)}) copy-start(f32[256]{0:T(256)} %constant.79.clone) | copy-start | bytes 3076
  363.2 52.6 %collective-permute-start.6 = (f32[128,16,128]{2,1,0:T(8,128)}, f32[128,16,128]{2,1,0:T(8,128)}, u32[]{:S(2)}, u32[]{:S(2)}) collective-permute-start(f32[128,16,128]{2,1,0:T(8,128)} %slice_bitcast_fusion), channel_id=1, source_target_pairs={{0,8},{8,16},{16,24},{1,9},{9,17},{17,25},{2,10},{10,18},{18,26},{... | collective-permute-start | bytes 3145736 | tf_op jit(solution)/shard_map/ppermute | solution.py:266
  408.5 1.3 copy-start.3
  409.8 66.3 %all-to-all-start.5 = ((f32[8,14,16,384]{3,2,1,0:T(8,128)}), f32[8,14,16,384]{3,2,1,0:T(8,128)S(1)}, u32[]{:S(2)}, u32[]{:S(2)}) async-start(f32[8,14,16,384]{3,2,1,0:T(8,128)} %get-tuple-element.54), calls=%async_computation.5 | async-start | bytes 5505024 | tf_op jit(solution)/shard_map/all_to_all | solution.py:275
  423.5 9.1 %copy-start.4 = (f32[128,128]{1,0:T(8,128)S(1)}, f32[128,128]{1,0:T(8,128)}, u32[]{:S(2)}) copy-start(f32[128,128]{1,0:T(8,128)} %constant.101) | copy-start | bytes 196612
  423.5 9.1 %copy-start.5 = (f32[16]{0:T(128)S(1)}, f32[16]{0:T(128)}, u32[]{:S(2)}) copy-start(f32[16]{0:T(128)} %dynamic_slice.7.coarse_ref) | copy-start | bytes 196
  427.7 4.9 collective-permute-start.7
  435.3 13.3 %collective-permute-start.8 = (f32[128,16,128]{2,1,0:T(8,128)}, f32[128,16,128]{2,1,0:T(8,128)}, u32[]{:S(2)}, u32[]{:S(2)}) collective-permute-start(f32[128,16,128]{2,1,0:T(8,128)} %add_select_fusion), channel_id=1, source_target_pairs={{8,16},{9,17},{10,18},{11,19},{12,20},{13,21},{14,22},{15,23}} | collective-permute-start | bytes 3145736 | tf_op jit(solution)/shard_map/ppermute | solution.py:504
  437.6 14.0 %copy-start.2 = (f32[128,16,128]{2,1,0:T(8,128)S(1)}, f32[128,16,128]{2,1,0:T(8,128)}, u32[]{:S(2)}) copy-start(f32[128,16,128]{2,1,0:T(8,128)} %offset.1) | copy-start | bytes 3145732
  450.8 0.7 collective-permute-start.9
  476.1 1.5 copy-start.1
